TPU v7x, 256 devices: a whole 4x4x8 slice. The times are simulated.
256 devices in a mesh: feat: 16 (over x, y), group: 8 (over z), rep: 2 (over core).
Axes of the slice: x: 4, y: 4, z: 8, core: 2. Of those that a mesh axis runs over, the one named last changes fastest.
Arguments:
- seed_feats: bfloat16 [65536, 768], P(('rep', 'group'), 'feat'), parts along dimension 0, may hold values from -6 to 6
- src_feats: bfloat16 [131072, 768], P(('rep', 'group'), 'feat'), parts along dimension 0, may hold values from -6 to 6
- counts: int32 [1536, 128, 128], P(('rep', 'group')), parts along dimension 0, may hold values from 0 to 3, as said below
- dst_block: int32 [1536], P(('rep', 'group')), parts along dimension 0, may hold values from 0 to 255
- src_block: int32 [1536], P(('rep', 'group')), parts along dimension 0, may hold values from 0 to 63
- w_self: bfloat16 [768, 1024], replicated, may hold values from -0.21875 to 0.21875
- w_neigh: bfloat16 [768, 1024], replicated, may hold values from -0.21875 to 0.21875
- cotangent: bfloat16 [65536, 1024], P(('rep', 'group'), 'feat'), parts along dimension 0, may hold values from -6 to 6
Outputs:
- hidden: bfloat16 [65536, 1024], P(('rep', 'group'), 'feat'), parts along dimension 0
- grad_self: float32 [1536, 1024], P(('rep', 'feat'), 'group'), parts along dimension 0
- grad_neigh: float32 [1536, 1024], P(('rep', 'feat'), 'group'), parts along dimension 0
There are 2 independent parts, one for each index of `rep`. A program takes and returns all parts, laid end to end along the dimension named above; an argument that names none is the same for every part. Nothing has to cross between parts.
Inputs may be any that keep to these rules, and one draw needn't show every extreme that they name: Small edge counts; tiles are sparse.
All inputs are finite; a program needn't handle non-finite values.
Results may differ from a plain program's by a relative error of at most 0.013.
The roundings to bfloat16 on the way count: a program that leaves them out, or rounds other values in their place, can miss the bound.
Values may be sent and summed in bfloat16 or wider, within the bound.
No kernel may reach another device: no remote copies, remote signals or barrier semaphores. Data moves between devices by JAX's collectives and lax.ppermute only.
A program may use at most 128 MiB of HBM per device.

v0:
```python
import jax
import jax.numpy as jnp
from jax import lax
from jax.sharding import PartitionSpec as P


def shards(seed_feats, src_feats, counts, dst_block, src_block, w_self, w_neigh, cotangent):
    tile = counts.shape[1]
    cols = seed_feats.shape[1]
    seeds_here = seed_feats.shape[0]
    groups = lax.axis_size("group")
    nblk = groups * seeds_here // tile
    blocks = src_feats.reshape(-1, tile, cols)[src_block]
    tile_out = jnp.einsum(
        "tij,tjf->tif", counts.astype(jnp.bfloat16), blocks, preferred_element_type=jnp.float32
    )
    partial_sum = jax.ops.segment_sum(tile_out, dst_block, nblk).reshape(-1, cols)
    partial_deg = jax.ops.segment_sum(
        jnp.sum(counts, axis=2).astype(jnp.float32), dst_block, nblk
    ).reshape(-1)
    neigh_sum, degree = (
        lax.psum_scatter(partial_sum, "group", scatter_dimension=0, tiled=True),
        lax.psum_scatter(partial_deg, "group", scatter_dimension=0, tiled=True),
    )
    neigh_mean = (neigh_sum / (degree[:, None] + 1.0)).astype(jnp.bfloat16)
    start_col = lax.axis_index("feat") * cols
    self_rows = lax.dynamic_slice_in_dim(w_self, start_col, cols, 0)
    neigh_rows = lax.dynamic_slice_in_dim(w_neigh, start_col, cols, 0)
    dims = (((0,), (1,)), ((), ()))
    first = lax.dot_general(self_rows, seed_feats, dims, preferred_element_type=jnp.float32)
    second = lax.dot_general(neigh_rows, neigh_mean, dims, preferred_element_type=jnp.float32)
    pre_cols = lax.psum_scatter(first + second, "feat", scatter_dimension=0, tiled=True)
    hidden = jnp.maximum(pre_cols.T, 0.0).astype(jnp.bfloat16)
    dpre = jnp.where(hidden > 0, cotangent, jnp.zeros_like(cotangent))
    stacked = jnp.concatenate([seed_feats, neigh_mean], axis=1)
    partial_grad = lax.dot_general(
        stacked,
        lax.all_gather(dpre, "feat", axis=1, tiled=True),
        (((0,), (0,)), ((), ())),
        preferred_element_type=jnp.float32,
    )
    summed = lax.psum_scatter(partial_grad, "group", scatter_dimension=1, tiled=True)
    return (hidden, summed[:cols], summed[cols:])


def solution(mesh):
    in_specs = (
        P(("rep", "group"), "feat"),
        P(("rep", "group"), "feat"),
        P(("rep", "group"), None, None),
        P(("rep", "group")),
        P(("rep", "group")),
        P(),
        P(),
        P(("rep", "group"), "feat"),
    )
    out_specs = (
        P(("rep", "group"), "feat"),
        P(("rep", "feat"), "group"),
        P(("rep", "feat"), "group"),
    )
    return jax.shard_map(shards, mesh=mesh, in_specs=in_specs, out_specs=out_specs, check_vma=False)
```

profile of v0, /device:TPU:32, one launch (start us, length us, event | category | flops | bytes accessed | tf_op | source)
XLA Modules:
  0.0 423.0 jit_solution(7636661628309229000)
XLA Ops:
  7.2 0.0 copy-start
  7.2 0.0 copy-start.5
  7.2 0.0 copy-start.6
  7.2 0.0 copy-start.3
  7.2 0.0 all-reduce.3.cloned.1.call-start
  7.3 4.6 %reduce_sum.9 = s32[96,128]{1,0:T(8,128)S(1)} reduce(s32[96,128,128]{2,1,0:T(8,128)} %param.10, s32[]{:T(128)} %constant.3.clone.1), dimensions={2}, to_apply=%region_2.0 | reduce | flops 1560576 | bytes 6340612 | tf_op jit(solution)/shard_map/reduce_sum | solution.py:19
  11.9 0.0 copy-done.5
  11.9 1.5 scatter_custom_fusion.1
  13.4 0.0 all-reduce.3.cloned.1.call-update
  13.4 0.0 reduce-scatter.4.cloned.1.call-start
  13.5 0.0 copy-done.6
  13.5 0.0 copy-done.3
  13.5 0.1 copy_bitcast_fusion.1
  13.7 0.8 gather_fusion
  14.5 6.5 %fusion.2 = f32[96,128,48]{1,2,0:T(8,128)} fusion(bf16[96,128,48]{1,2,0:T(8,128)(2,1)S(1)} %gather_fusion, s32[96,128,128]{2,1,0:T(8,128)} %param.10), kind=kOutput, calls=%fused_computation.7 | convolution fusion | flops 152567808 | bytes 9830400 | tf_op jit(solution)/shard_map/tij,tjf->tif/dot_general | solution.py:14
  21.0 3.1 broadcast_in_dim.14
  24.0 14.1 %scatter_fusion = f32[256,128,48]{1,2,0:T(8,128)} fusion(f32[256,128,48]{1,2,0:T(8,128)} %broadcast_in_dim.14, s32[96]{0:T(128)S(1)} %copy-done.5, f32[96,128,48]{1,2,0:T(8,128)} %fusion.2), kind=kCustom, calls=%fused_computation.1 | custom fusion | flops 589824 | bytes 7078272 | tf_op jit(solution)/shard_map/scatter-add | solution.py:17
  38.1 5.9 %copy_bitcast_fusion = f32[32768,48]{0,1:T(8,128)} fusion(f32[256,128,48]{1,2,0:T(8,128)} %scatter_fusion), kind=kLoop, calls=%fused_computation.4 | loop fusion | bytes 12582912 | tf_op jit(solution)/shard_map/reshape | solution.py:17
  44.0 0.0 copy-start.7
  44.0 0.0 copy-start.2
  44.0 0.0 reduce-scatter.4.cloned.1.call-update
  44.0 0.0 reduce-scatter.6.cloned.1.call-start
  44.1 0.6 copy-done.7
  44.6 0.6 dynamic-slice
  45.9 0.0 copy-done
  45.9 0.0 copy-done.2
  45.9 8.1 %fusion.11 = f32[1024,4096]{1,0:T(8,128)} fusion(bf16[4096,48]{0,1:T(8,128)(2,1)S(1)} %copy-done.2, bf16[768,1024]{1,0:T(8,128)(2,1)S(1)} %copy-done, s32[]{:T(128)S(6)} %select_n.11), kind=kOutput, calls=%fused_computation.18 | convolution fusion | flops 402653184 | bytes 17268740 | tf_op jit(solution)/shard_map/dot_general | solution.py:30
  54.0 33.9 %all-reduce.3.cloned.1.call-done = f32[32768]{0:T(1024)} async-done(((f32[32768]{0:T(1024)}), f32[32768]{0:T(1024)}) %all-reduce.3.cloned.1.call-update) | async-done | bytes 131088
  87.9 0.7 dynamic-slice_add_fusion
  88.7 74.0 %reduce-scatter.4.cloned.1.call-done = f32[4096,48]{0,1:T(8,128)} async-done(((f32[32768,48]{0,1:T(8,128)}), f32[4096,48]{0,1:T(8,128)}) %reduce-scatter.4.cloned.1.call-update) | async-done | bytes 786448 | tf_op jit(solution)/shard_map/reduce_scatter | solution.py:22
  162.7 1.2 divide_convert_fusion
  163.9 13.9 %convolution_add_fusion = f32[1024,4096]{1,0:T(8,128)} fusion(f32[1024,4096]{1,0:T(8,128)} %fusion.11, bf16[4096,48]{0,1:T(8,128)(2,1)S(1)} %divide_convert_fusion, bf16[768,1024]{1,0:T(8,128)(2,1)} %param.14, s32[]{:T(128)S(6)} %select_n.11), kind=kOutput, calls=%fused_computation.3 | convolution fusion | flops 406847488 | bytes 34045956 | tf_op jit(solution)/shard_map/dot_general | solution.py:31
  177.8 0.0 copy-start.4
  177.8 0.0 reduce-scatter.6.cloned.1.call-update
  177.8 0.0 copy-start.1
  177.8 0.0 all-gather.2.cloned.1.call-start
  177.9 116.1 %reduce-scatter.6.cloned.1.call-done = f32[64,4096]{1,0:T(8,128)} async-done(((f32[1024,4096]{1,0:T(8,128)}), f32[64,4096]{1,0:T(8,128)}) %reduce-scatter.6.cloned.1.call-update) | async-done | bytes 1048592 | tf_op jit(solution)/shard_map/reduce_scatter | solution.py:32
  294.0 0.0 copy-done.4
  294.0 2.3 compare_select_fusion
  296.3 0.0 all-gather.2.cloned.1.call-update
  296.4 0.0 reduce-scatter.8.cloned.1.call-start
  296.4 75.6 %all-gather.2.cloned.1.call-done = bf16[4096,1024]{0,1:T(8,128)(2,1)} async-done(((bf16[4096,64]{0,1:T(8,128)(2,1)}), bf16[4096,1024]{0,1:T(8,128)(2,1)}) %all-gather.2.cloned.1.call-update) | async-done | bytes 8388624 | tf_op jit(solution)/shard_map/all_gather | solution.py:38
  372.0 6.9 %fusion.5 = f32[96,1024]{1,0:T(8,128)} fusion(bf16[4096,1024]{0,1:T(8,128)(2,1)} %all-gather.2.cloned.1.call-done, bf16[4096,48]{0,1:T(8,128)(2,1)S(1)} %divide_convert_fusion, bf16[4096,48]{0,1:T(8,128)(2,1)S(1)} %copy-done.2), kind=kOutput, calls=%fused_computation.11 | convolution fusion | flops 806879232 | bytes 9568256 | tf_op jit(solution)/shard_map/dot_general | solution.py:36
  378.9 0.0 reduce-scatter.8.cloned.1.call-update
  378.9 36.2 %reduce-scatter.8.cloned.1.call-done = f32[96,128]{1,0:T(8,128)} async-done(((f32[96,1024]{1,0:T(8,128)}), f32[96,128]{1,0:T(8,128)}) %reduce-scatter.8.cloned.1.call-update) | async-done | bytes 49168 | tf_op jit(solution)/shard_map/reduce_scatter | solution.py:42
  415.1 1.4 fusion.20
  416.5 0.0 copy-done.1
  (2 shorter events, 0.0 us)
Async XLA Ops:
  7.2 38.7 %copy-start = (bf16[768,1024]{1,0:T(8,128)(2,1)S(1)}, bf16[768,1024]{1,0:T(8,128)(2,1)}, u32[]{:S(2)}) copy-start(bf16[768,1024]{1,0:T(8,128)(2,1)} %param.13) | copy-start | bytes 4718596
  7.2 4.7 %copy-start.5 = (s32[96]{0:T(128)S(1)}, s32[96]{0:T(128)}, u32[]{:S(2)}) copy-start(s32[96]{0:T(128)} %param.11) | copy-start | bytes 1156
  7.2 6.3 %copy-start.6 = (s32[96]{0:T(128)S(1)}, s32[96]{0:T(128)}, u32[]{:S(2)}) copy-start(s32[96]{0:T(128)} %param.12) | copy-start | bytes 1156
  7.2 6.3 %copy-start.3 = (bf16[8192,48]{0,1:T(8,128)(2,1)S(1)}, bf16[8192,48]{0,1:T(8,128)(2,1)}, u32[]{:S(2)}) copy-start(bf16[8192,48]{0,1:T(8,128)(2,1)} %param.9) | copy-start | bytes 2359300
  7.2 80.7 %all-reduce.3.cloned.1.call-start = ((), (), s32[]{:S(2)}) async-start(), calls=%async_computation.7 | async-start | bytes 262144
  13.4 149.2 %reduce-scatter.4.cloned.1.call-start = ((), (), s32[]{:S(2)}) async-start(), calls=%async_computation.3 | async-start | bytes 7077888 | tf_op jit(solution)/shard_map/reduce_scatter | solution.py:22
  44.0 0.7 copy-start.7
  44.0 1.9 copy-start.2
  44.0 250.0 %reduce-scatter.6.cloned.1.call-start = ((), (), s32[]{:S(2)}) async-start(), calls=%async_computation.4 | async-start | bytes 17825792 | tf_op jit(solution)/shard_map/reduce_scatter | solution.py:32
  177.8 116.2 %copy-start.4 = (bf16[4096,64]{0,1:T(8,128)(2,1)S(1)}, bf16[4096,64]{0,1:T(8,128)(2,1)}, u32[]{:S(2)}) copy-start(bf16[4096,64]{0,1:T(8,128)(2,1)} %param.15) | copy-start | bytes 1572868
  177.8 238.7 %copy-start.1 = (bf16[768,1024]{1,0:T(8,128)(2,1)S(1)}, bf16[768,1024]{1,0:T(8,128)(2,1)}, u32[]{:S(2)}) copy-start(bf16[768,1024]{1,0:T(8,128)(2,1)} %param.13) | copy-start | bytes 4718596
  177.8 194.2 %all-gather.2.cloned.1.call-start = ((), (), s32[]{:S(2)}) async-start(), calls=%async_computation.5 | async-start | bytes 8912896 | tf_op jit(solution)/shard_map/all_gather | solution.py:38
  296.4 118.7 %reduce-scatter.8.cloned.1.call-start = ((), (), s32[]{:S(2)}) async-start(), calls=%async_computation.6 | async-start | bytes 442368 | tf_op jit(solution)/shard_map/reduce_scatter | solution.py:42
Sparse Core Ops, SparseCore 0:
  13.6 74.3 all-reduce.2
  90.7 71.9 reduce-scatter.3
  177.9 116.0 reduce-scatter.5
  296.6 75.3 all-gather.1
  379.0 36.0 reduce-scatter.7
where the time goes:
time: 425 us; the launch traced here: 423 us
  waiting for transfers between devices  336 us (79%)
  matrix products  35.4 us (8%)
  other arithmetic  24.5 us (6%)
  between operations  14.6 us (3%)
  local copies, waits for them, and re-layouts  12.4 us (3%)
    reduce_scatter x1, waiting for transfers between devices, shards(): lax.psum_scatter(first + second, 'feat', scatter_dimension=0, tiled=True)  116 us
    all_gather x1, waiting for transfers between devices, shards(): lax.all_gather(dpre, 'feat', axis=1, tiled=True)  75.6 us
    reduce_scatter x1, waiting for transfers between devices, shards(): lax.psum_scatter(partial_sum, 'group', scatter_dimension=0, tiled=True)  74 us
    reduce_scatter x1, waiting for transfers between devices, shards(): lax.psum_scatter(partial_grad, 'group', scatter_dimension=1, tiled=True)  36.2 us
    unnamed x6, waiting for transfers between devices  34 us
    scatter-add x1, other arithmetic, shards(): jax.ops.segment_sum(tile_out, dst_block, nblk).reshape(-1, cols)  14.1 us
    dot_general x1, matrix products, shards(): lax.dot_general(neigh_rows, neigh_mean, dims, preferred_element_type=jnp....  13.9 us
  transfers between devices with their start and end apart: 5, of which 5 were waited for; matrix products, arithmetic and copies ran while one was open for 9% of the time, Pallas kernels for 0%

commit v1 on v0

v1 whole, which is shorter than its diff:
```python
import jax
import jax.numpy as jnp
from jax import lax
from jax.experimental import pallas as pl
from jax.experimental.pallas import tpu as pltpu
from jax.sharding import PartitionSpec as P

F32, BF16 = jnp.float32, jnp.bfloat16
UNROLL = 16
SIDE = 4
HBM = pl.BlockSpec(memory_space=pltpu.HBM)


def far(*arrays):
    return [pltpu.with_memory_space_constraint(a, pltpu.HBM) for a in arrays]


def tile_kernel(dst_ref, src_ref, feats_h, counts_ref, acc, deg_ref, held, feats, sem):
    step = pl.program_id(0)
    cols = feats.shape[0]
    nsrc, rows, tile = held.shape
    per_owner = acc.shape[2] // tile

    @pl.when(step == 0)
    def _():
        load = pltpu.make_async_copy(feats_h, feats, sem)
        load.start()
        acc[...] = jnp.zeros_like(acc)
        deg_ref[...] = jnp.zeros_like(deg_ref)
        load.wait()
        for b in range(nsrc):
            held[b, :cols, :] = feats[:, b * tile : (b + 1) * tile]
            held[b, cols:, :] = jnp.ones((rows - cols, tile), BF16)

    for u in range(UNROLL):
        t = step * UNROLL + u
        d = dst_ref[t]
        got = lax.dot_general(
            held[src_ref[t]],
            counts_ref[u].astype(F32).astype(BF16),
            (((1,), (1,)), ((), ())),
            preferred_element_type=F32,
        )
        owner = d // per_owner
        lanes = pl.ds(pl.multiple_of((d % per_owner) * tile, tile), tile)
        acc[owner, :, lanes] += got[:cols]
        deg_ref[owner, :, lanes] += got[cols : cols + 8]


def tile_sums(dst_block, src_block, feats_t, counts, owners, seeds_here):
    ntile, tile, _ = counts.shape
    cols, sources = feats_t.shape
    outs = [(owners, cols, seeds_here), (owners, 8, seeds_here)]
    return pl.pallas_call(
        tile_kernel,
        grid_spec=pltpu.PrefetchScalarGridSpec(
            num_scalar_prefetch=2,
            grid=(ntile // UNROLL,),
            in_specs=[HBM, pl.BlockSpec((UNROLL, tile, tile), lambda i, *_: (i, 0, 0))],
            out_specs=[pl.BlockSpec(o, lambda i, *_: (0, 0, 0)) for o in outs],
            scratch_shapes=[
                pltpu.VMEM((sources // tile, cols + 16, tile), BF16),
                pltpu.VMEM((cols, sources), BF16),
                pltpu.SemaphoreType.DMA,
            ],
        ),
        out_shape=[pltpu.HBM(o, F32) for o in outs],
        compiler_params=pltpu.CompilerParams(
            dimension_semantics=("arbitrary",), vmem_limit_bytes=48 * 1024 * 1024
        ),
    )(*far(dst_block, src_block, feats_t), counts)


def mean_kernel(total_h, degree_h, send_h, total, degree, send, sems):
    loads = [
        pltpu.make_async_copy(total_h, total, sems.at[0]),
        pltpu.make_async_copy(degree_h, degree, sems.at[1]),
    ]
    for load in loads:
        load.start()
    for load in loads:
        load.wait()
    width = send.shape[2]
    stores = []
    for y in range(SIDE):
        lanes = slice(y * width, (y + 1) * width)
        send[y] = (total[:, lanes] / (degree[:, lanes] + 1.0)).astype(BF16)
    for x in range(SIDE):
        store = pltpu.make_async_copy(send, send_h.at[pl.ds(x * SIDE, SIDE)], sems.at[2 + x])
        store.start()
        stores.append(store)
    for store in stores:
        store.wait()


def mean_rows(total, degree):
    cols, n = total.shape
    send = (SIDE, cols, n // SIDE)
    return pl.pallas_call(
        mean_kernel,
        in_specs=[HBM, HBM],
        out_specs=HBM,
        out_shape=pltpu.HBM((SIDE * SIDE, *send[1:]), BF16),
        scratch_shapes=[
            pltpu.VMEM(total.shape, F32),
            pltpu.VMEM(degree.shape, F32),
            pltpu.VMEM(send, BF16),
            pltpu.SemaphoreType.DMA((2 + SIDE,)),
        ],
        compiler_params=pltpu.CompilerParams(vmem_limit_bytes=16 * 1024 * 1024),
    )(*far(total), degree)


def layer_kernel(wn_h, means_h, pre_h, cot_h, seeds_h, hid_h, grad_h, *refs):
    wn, means, pre, cot, seeds, hid, grad, sems = refs
    given = (wn_h, means_h, pre_h, cot_h, seeds_h)
    near = (wn, means, pre, cot, seeds)
    loads = [pltpu.make_async_copy(given[i], near[i], sems.at[i]) for i in range(5)]
    for load in loads:
        load.start()
    nf, rows, _ = grad.shape
    cols = rows // 2
    for load in loads[:3]:
        load.wait()
    total = pre[...] + jnp.dot(wn[...], means[...], preferred_element_type=F32)
    h = jnp.maximum(total, 0.0).astype(BF16)
    hid[...] = h
    stores = [pltpu.make_async_copy(hid, hid_h, sems.at[5])]
    stores[0].start()
    loads[3].wait()
    dpre = jnp.where(h > 0, cot[...], jnp.zeros_like(h))
    dims = (((1,), (1,)), ((), ()))
    loads[4].wait()
    for j, x in enumerate((means, seeds)):
        at = (1 - j) * cols
        g = lax.dot_general(x[...], dpre, dims, preferred_element_type=F32).astype(BF16)
        for i in range(nf):
            grad[i, at : at + cols, :] = g[i * cols : (i + 1) * cols]
        where = (slice(None), pl.ds(at, cols), slice(None))
        store = pltpu.make_async_copy(grad.at[where], grad_h.at[where], sems.at[6 + j])
        store.start()
        stores.append(store)
    for store in stores:
        store.wait()


def layer(wn_t, means, pre_self, cot, seeds, nf):
    hcols, rows = pre_self.shape
    args = (wn_t, means, pre_self, cot, seeds)
    shapes = [(hcols, rows), (nf, 2 * means.shape[0] // nf, hcols)]
    return pl.pallas_call(
        layer_kernel,
        in_specs=[HBM] * 5,
        out_specs=[HBM] * 2,
        out_shape=[pltpu.HBM(o, BF16) for o in shapes],
        scratch_shapes=[pltpu.VMEM(a.shape, a.dtype) for a in args]
        + [pltpu.VMEM(o, BF16) for o in shapes]
        + [pltpu.SemaphoreType.DMA((8,))],
        compiler_params=pltpu.CompilerParams(vmem_limit_bytes=40 * 1024 * 1024),
    )(*far(*args))


def shards(seed_feats, src_feats, counts, dst_block, src_block, w_self, w_neigh, cotangent):
    seeds_here, cols = seed_feats.shape
    ng = lax.axis_size("group")
    nf = lax.axis_size("feat")
    part = seeds_here // SIDE
    ccols = cotangent.shape[1]
    hcols = SIDE * ccols
    f = lax.axis_index("feat")
    fx, fy = f // SIDE, f % SIDE
    along_y = [[x * SIDE + y for y in range(SIDE)] for x in range(SIDE)]

    def shift_y(a, k):
        return lax.ppermute(
            a, "feat", [(i, i // SIDE * SIDE + (i % SIDE + k) % SIDE) for i in range(nf)]
        )

    with jax.named_scope("tile_sums"):
        sums, deg = tile_sums(dst_block, src_block, src_feats.T, counts, ng, seeds_here)

    with jax.named_scope("neighbour_sum"):
        total = lax.psum_scatter(
            sums.reshape(ng * cols, seeds_here), "group", scatter_dimension=0, tiled=True
        )

    seed_t, cot_t, deg, _ = lax.optimization_barrier((seed_feats.T, cotangent.T, deg, sums))

    with jax.named_scope("degree"):
        degree = jnp.sum(lax.all_to_all(deg[:, 0], "group", 0, 0, tiled=True), axis=0)[None]

    with jax.named_scope("cotangent_rows"):
        send = cot_t.reshape(ccols, SIDE, part).transpose(1, 0, 2)
        cot = lax.all_to_all(send, "feat", 0, 0, axis_index_groups=along_y)
        cot = cot.reshape(hcols, part)

    with jax.named_scope("seed_rows"):
        send = seed_t.reshape(cols, SIDE, part).transpose(1, 0, 2)
        send = jnp.broadcast_to(send[None], (SIDE, SIDE, cols, part)).reshape(nf, cols, part)
        seeds = lax.all_to_all(send, "feat", 0, 0).reshape(nf * cols, part)

    with jax.named_scope("self_part"):
        ws_t = lax.dynamic_slice_in_dim(w_self, fx * hcols, hcols, 1).T
        wn_t = lax.dynamic_slice_in_dim(w_neigh, fx * hcols, hcols, 1).T
        pre_self = jnp.dot(ws_t, seeds, preferred_element_type=F32)

    with jax.named_scope("mean_rows"):
        total, degree, pre_self, cot = lax.optimization_barrier((total, degree, pre_self, cot))
        send = mean_rows(total, degree)
        means = lax.all_to_all(send, "feat", 0, 0).reshape(nf * cols, part)

    with jax.named_scope("layer"):
        hid, both = layer(wn_t, means, pre_self, cot, seeds, nf)

    with jax.named_scope("grads"):
        got = lax.all_to_all(both, "feat", 0, 0).astype(F32)
        got = jnp.sum(got.reshape(SIDE, SIDE, 2 * cols, hcols), axis=1)
        got = got.reshape(SIDE, 2 * cols, 2, hcols // 2).transpose(0, 2, 1, 3)
        got = got.reshape(ng, 2 * cols, hcols // 2).astype(BF16)
        got, hid = lax.optimization_barrier((got, hid))
        got = jnp.sum(lax.all_to_all(got, "group", 0, 0).astype(F32), axis=0)

    with jax.named_scope("hidden_columns"):
        hid4 = hid.reshape(SIDE, ccols, part)
        out = jnp.zeros((ccols, seeds_here), BF16)
        for k in range(SIDE):
            piece = lax.dynamic_index_in_dim(hid4, (fy + k) % SIDE, 0, keepdims=False)
            piece = shift_y(piece, k) if k else piece
            out = lax.dynamic_update_slice(out, piece, (0, (fy - k) % SIDE * part))
    return (out.T, got[:cols], got[cols:])


def solution(mesh):
    in_specs = (
        P(("rep", "group"), "feat"),
        P(("rep", "group"), "feat"),
        P(("rep", "group"), None, None),
        P(("rep", "group")),
        P(("rep", "group")),
        P(),
        P(),
        P(("rep", "group"), "feat"),
    )
    out_specs = (
        P(("rep", "group"), "feat"),
        P(("rep", "feat"), "group"),
        P(("rep", "feat"), "group"),
    )
    return jax.shard_map(shards, mesh=mesh, in_specs=in_specs, out_specs=out_specs, check_vma=False)
```

time: 425 us -> 176 us (0.41)
  waiting for transfers between devices: 336 us -> 90.5 us
  starting transfers between devices: 0.21 us -> 39.8 us
  matrix products: 35.4 us -> 1.66 us
  other arithmetic: 24.5 us -> 0.92 us
  Pallas kernels: 0 us -> 17.8 us
    reduce_scatter x3 -> x1, waiting for transfers between devices: 226 us -> 15.7 us  [shards(): lax.psum_scatter(sums.reshape(ng * cols, seeds_here), 'group', scatter_di...]
    all_gather x1 -> x0, waiting for transfers between devices: 75.6 us -> none  [shards(): lax.all_gather(dpre, 'feat', axis=1, tiled=True)]
    all_to_all x0 -> x6, waiting for transfers between devices: none -> 68.3 us  [the longest x1 21.9 us: shards(): means = lax.all_to_all(send, 'feat', 0, 0).reshape(nf * cols, part)]
    all_to_all x0 -> x6, starting transfers between devices: none -> 36.4 us  [the longest x1 8.56 us: shards(): lax.all_to_all(deg[:, 0], 'group', 0, 0, tiled=True)]
    unnamed x6 -> x1, waiting for transfers between devices: 34 us -> 0.02 us
    dot_general x4 -> x1, matrix products: 35.4 us -> 1.66 us  [shards(): pre_self = jnp.dot(ws_t, seeds, preferred_element_type=F32)]
    pallas_call x0 -> x3, Pallas kernels: none -> 17.8 us  [the longest x1 10.9 us: tile_sums(): pl.pallas_call(tile_kernel, grid_spec=pltpu.PrefetchScalarGridSpec(num_sc...]
    scatter-add x2 -> x0, other arithmetic: 15.6 us -> none  [the longest x1 14.1 us: shards(): jax.ops.segment_sum(tile_out, dst_block, nblk).reshape(-1, cols)]
  transfers between devices with their start and end apart: 5 -> 10, of which waited for: 5 -> 7; matrix products, arithmetic and copies ran while one was open for 9% -> 5% of each run, Pallas kernels for 0% -> 0%
where the time goes in v1:
time: 176 us; the launch traced here: 175 us
  waiting for transfers between devices  90.5 us (51%)
  starting transfers between devices  39.8 us (23%)
  Pallas kernels  17.8 us (10%)
  between operations  14.3 us (8%)
  local copies, waits for them, and re-layouts  9.72 us (6%)
    all_to_all x1, waiting for transfers between devices, shards(): means = lax.all_to_all(send, 'feat', 0, 0).reshape(nf * cols, part)  21.9 us
    all_to_all x1, waiting for transfers between devices, shards(): seeds = lax.all_to_all(send, 'feat', 0, 0).reshape(nf * cols, part)  20.5 us
    reduce_scatter x1, waiting for transfers between devices, shards(): lax.psum_scatter(sums.reshape(ng * cols, seeds_here), 'group', scatter_di...  15.7 us
    all_to_all x1, waiting for transfers between devices, shards(): got = lax.all_to_all(both, 'feat', 0, 0).astype(F32)  12.6 us
    pallas_call x1, Pallas kernels, tile_sums(): pl.pallas_call(tile_kernel, grid_spec=pltpu.PrefetchScalarGridSpec(num_sc...  10.9 us
    all_to_all x1, starting transfers between devices, shards(): lax.all_to_all(deg[:, 0], 'group', 0, 0, tiled=True)  8.56 us
    all_to_all x1, waiting for transfers between devices, shards(): lax.all_to_all(deg[:, 0], 'group', 0, 0, tiled=True)  7.04 us
    all_to_all x1, starting transfers between devices, shards(): seeds = lax.all_to_all(send, 'feat', 0, 0).reshape(nf * cols, part)  7.03 us
  transfers between devices with their start and end apart: 10, of which 7 were waited for; matrix products, arithmetic and copies ran while one was open for 5% of the time, Pallas kernels for 0%

profile of v1, /device:TPU:32, one launch (start us, length us, event | category | flops | bytes accessed | tf_op | source)
XLA Modules:
  0.0 174.7 jit_solution(6050496365276435863)
XLA Ops:
  7.2 0.0 copy-start
  7.2 0.0 reduce-scatter.2.cloned.1.call-start
  7.2 10.9 %tile_sums.1 = (f32[8,48,4096]{2,1,0:T(8,128)}, f32[8,8,4096]{2,1,0:T(8,128)}) custom-call(s32[96]{0:T(128)} %dst_ref.1, s32[96]{0:T(128)} %src_ref.1, bf16[48,8192]{1,0:T(8,128)(2,1)} %bitcast.41, s32[96,128,128]{2,1,0:T(8,128)} %counts_ref.1), custom_call_target="tpu_custom_call" | custom-call | tf_op jit(solution)/shard_map/tile_sums/pallas_call | solution.py:54
  18.2 0.0 copy-start.5
  18.2 0.0 reduce-scatter.2.cloned.1.call-update
  18.2 2.0 %slice.17 = f32[8,1,4096]{2,1,0:T(1,128)} slice(f32[8,8,4096]{2,1,0:T(8,128)} %get-tuple-element.18), slice={[0:8], [0:1], [0:4096]} | slice | bytes 262144 | tf_op jit(solution)/shard_map/degree/slice | solution.py:190
  20.2 8.6 %all-to-all-start = ((f32[8,1,4096]{2,1,0:T(1,128)}), f32[8,1,4096]{2,1,0:T(1,128)S(1)}, u32[]{:S(2)}, u32[]{:S(2)}) async-start(f32[8,1,4096]{2,1,0:T(1,128)} %slice.17), calls=%async_computation.1 | async-start | bytes 262144 | tf_op jit(solution)/shard_map/degree/all_to_all | solution.py:190
  28.8 0.0 copy-done.5
  28.8 0.3 reshape.44
  29.0 0.1 copy.15
  29.2 7.0 %all-to-all-done = f32[8,1,4096]{2,1,0:T(1,128)S(1)} async-done(((f32[8,1,4096]{2,1,0:T(1,128)}), f32[8,1,4096]{2,1,0:T(1,128)S(1)}, u32[]{:S(2)}, u32[]{:S(2)}) %all-to-all-start) | async-done | bytes 131104 | tf_op jit(solution)/shard_map/degree/all_to_all | solution.py:190
  36.2 1.3 broadcast_in_dim.14
  37.6 7.0 %all-to-all-start.1 = ((bf16[16,48,1024]{2,1,0:T(8,128)(2,1)}), bf16[16,48,1024]{2,1,0:T(8,128)(2,1)S(1)}, u32[]{:S(2)}, u32[]{:S(2)}) async-start(bf16[16,48,1024]{2,1,0:T(8,128)(2,1)} %bitcast.37), calls=%async_computation.2 | async-start | bytes 3145728 | tf_op jit(solution)/shard_map/seed_rows/all_to_all | solution.py:200
  44.6 1.9 %copy.20 = bf16[8,4,8,1024]{3,2,0,1:T(8,128)(2,1)} copy(bf16[8,4,8,1024]{3,2,1,0:T(8,128)(2,1)} %bitcast.43) | data formatting | bytes 1048576 | tf_op jit(solution)/shard_map/cotangent_rows/reshape | solution.py:193
  46.5 20.5 %all-to-all-done.1 = bf16[16,48,1024]{2,1,0:T(8,128)(2,1)S(1)} async-done(((bf16[16,48,1024]{2,1,0:T(8,128)(2,1)}), bf16[16,48,1024]{2,1,0:T(8,128)(2,1)S(1)}, u32[]{:S(2)}, u32[]{:S(2)}) %all-to-all-start.1) | async-done | bytes 1572896 | tf_op jit(solution)/shard_map/seed_rows/all_to_all | solution.py:200
  67.0 0.0 copy-start.1
  67.0 4.1 %all-to-all-start.2 = ((bf16[4,64,1024]{2,1,0:T(8,128)(2,1)}), bf16[4,64,1024]{2,1,0:T(8,128)(2,1)}, u32[]{:S(2)}, u32[]{:S(2)}) async-start(bf16[4,64,1024]{2,1,0:T(8,128)(2,1)} %bitcast.38), calls=%async_computation.3 | async-start | bytes 1048576 | tf_op jit(solution)/shard_map/cotangent_rows/all_to_all | solution.py:194
  71.1 0.1 reduce_sum.27
  71.2 0.0 copy-done
  71.2 1.7 fusion.pre_h
  72.9 0.0 copy-done.1
  72.9 6.3 %all-to-all-done.2 = bf16[4,64,1024]{2,1,0:T(8,128)(2,1)} async-done(((bf16[4,64,1024]{2,1,0:T(8,128)(2,1)}), bf16[4,64,1024]{2,1,0:T(8,128)(2,1)}, u32[]{:S(2)}, u32[]{:S(2)}) %all-to-all-start.2) | async-done | bytes 524320 | tf_op jit(solution)/shard_map/cotangent_rows/all_to_all | solution.py:194
  79.2 15.7 %reduce-scatter.2.cloned.1.call-done.total_h = f32[48,4096]{1,0:T(8,128)} async-done(((f32[384,4096]{1,0:T(8,128)}), f32[48,4096]{1,0:T(8,128)}) %reduce-scatter.2.cloned.1.call-update) | async-done | bytes 786448 | tf_op jit(solution)/shard_map/neighbour_sum/reduce_scatter | solution.py:183
  95.0 2.4 %mean_rows.1 = bf16[16,48,1024]{2,1,0:T(8,128)(2,1)} custom-call(f32[48,4096]{1,0:T(8,128)} %reduce-scatter.2.cloned.1.call-done.total_h, f32[1,4096]{1,0:T(1,128)S(1)} %bitcast.32), custom_call_target="tpu_custom_call" | custom-call | tf_op jit(solution)/shard_map/mean_rows/pallas_call | solution.py:99
  97.4 6.8 %all-to-all-start.3 = ((bf16[16,48,1024]{2,1,0:T(8,128)(2,1)}), bf16[16,48,1024]{2,1,0:T(8,128)(2,1)S(1)}, u32[]{:S(2)}, u32[]{:S(2)}) async-start(bf16[16,48,1024]{2,1,0:T(8,128)(2,1)} %mean_rows.1), calls=%async_computation.4 | async-start | bytes 3145728 | tf_op jit(solution)/shard_map/mean_rows/all_to_all | solution.py:210
  104.2 1.0 constant_dynamic-slice_fusion
  105.3 0.9 copy.17
  106.2 21.9 %all-to-all-done.3 = bf16[16,48,1024]{2,1,0:T(8,128)(2,1)S(1)} async-done(((bf16[16,48,1024]{2,1,0:T(8,128)(2,1)}), bf16[16,48,1024]{2,1,0:T(8,128)(2,1)S(1)}, u32[]{:S(2)}, u32[]{:S(2)}) %all-to-all-start.3) | async-done | bytes 1572896 | tf_op jit(solution)/shard_map/mean_rows/all_to_all | solution.py:210
  128.1 0.0 copy-start.2
  128.1 1.2 copy-done.2
  129.3 4.5 %layer.1 = (bf16[256,1024]{1,0:T(8,128)(2,1)}, bf16[16,96,256]{2,1,0:T(8,128)(2,1)}) custom-call(bf16[256,768]{1,0:T(8,128)(2,1)} %bitcast.39, bf16[768,1024]{1,0:T(8,128)(2,1)} %bitcast.36, f32[256,1024]{1,0:T(8,128)} %fusion.pre_h, bf16[256,1024]{1,0:T(8,128)(2,1)} %bitcast.10.cot_h, bf16[768,1024]{1,0:T(8,128)(2,1)} %bitcast.34), custom_call_target="tpu_custom_call" | custom-call | tf_op jit(solution)/shard_map/layer/pallas_call | solution.py:151
  133.7 0.0 copy-start.4
  133.7 4.0 %all-to-all-start.4 = ((bf16[16,96,256]{2,1,0:T(8,128)(2,1)}), bf16[16,96,256]{2,1,0:T(8,128)(2,1)S(1)}, u32[]{:S(2)}, u32[]{:S(2)}) async-start(bf16[16,96,256]{2,1,0:T(8,128)(2,1)} %get-tuple-element.25), calls=%async_computation.5 | async-start | bytes 1572864 | tf_op jit(solution)/shard_map/grads/all_to_all | solution.py:216
  137.8 12.6 %all-to-all-done.4 = bf16[16,96,256]{2,1,0:T(8,128)(2,1)S(1)} async-done(((bf16[16,96,256]{2,1,0:T(8,128)(2,1)}), bf16[16,96,256]{2,1,0:T(8,128)(2,1)S(1)}, u32[]{:S(2)}, u32[]{:S(2)}) %all-to-all-start.4) | async-done | bytes 786464 | tf_op jit(solution)/shard_map/grads/all_to_all | solution.py:216
  150.5 0.1 bitcast_reduce_fusion
  150.6 0.7 pad_maximum_fusion
  151.3 0.0 copy-done.4
  151.3 0.6 collective-permute-start
  152.0 5.8 %all-to-all-start.5 = ((bf16[8,96,128]{2,1,0:T(8,128)(2,1)}), bf16[8,96,128]{2,1,0:T(8,128)(2,1)S(1)}, u32[]{:S(2)}, u32[]{:S(2)}) async-start(bf16[8,96,128]{2,1,0:T(8,128)(2,1)} %bitcast.13), calls=%async_computation.6 | async-start | bytes 393216 | tf_op jit(solution)/shard_map/grads/all_to_all | solution.py:221
  157.8 2.7 %collective-permute-start.2 = (bf16[64,1024]{1,0:T(8,128)(2,1)S(1)}, bf16[64,1024]{1,0:T(8,128)(2,1)S(1)}, u32[]{:S(2)}, u32[]{:S(2)}) collective-permute-start(bf16[64,1024]{1,0:T(8,128)(2,1)S(1)} %get-tuple-element.29), channel_id=1, source_target_pairs={{0,48},{16,0},{32,16},{48,32},{64,112},{80,64},{96,80},{112,96},{1... | collective-permute-start | bytes 393224 | tf_op jit(solution)/shard_map/hidden_columns/ppermute | solution.py:175
  160.5 0.0 collective-permute-start.1
  160.6 0.0 collective-permute-done
  160.6 6.4 %collective-permute-done.1 = bf16[64,1024]{1,0:T(8,128)(2,1)S(1)} collective-permute-done((bf16[64,1024]{1,0:T(8,128)(2,1)S(1)}, bf16[64,1024]{1,0:T(8,128)(2,1)S(1)}, u32[]{:S(2)}, u32[]{:S(2)}) %collective-permute-start.1) | collective-permute-done | bytes 131104 | tf_op jit(solution)/shard_map/hidden_columns/ppermute | solution.py:175
  167.0 0.0 collective-permute-done.2
  167.0 0.0 copy-start.3
  167.0 0.0 all-to-all-done.5
  167.1 0.7 fusion.4
  167.8 0.0 copy-done.3
  (8 shorter events, 0.2 us)
Async XLA Ops:
  7.2 64.1 %copy-start = (bf16[768,1024]{1,0:T(8,128)(2,1)S(1)}, bf16[768,1024]{1,0:T(8,128)(2,1)}, u32[]{:S(2)}) copy-start(bf16[768,1024]{1,0:T(8,128)(2,1)} %param.13) | copy-start | bytes 4718596
  7.2 87.8 %reduce-scatter.2.cloned.1.call-start = ((), (), s32[]{:S(2)}) async-start(), calls=%async_computation.7 | async-start | bytes 7077888 | tf_op jit(solution)/shard_map/neighbour_sum/reduce_scatter | solution.py:183
  18.2 10.6 %copy-start.5 = (bf16[4096,48]{0,1:T(8,128)(2,1)S(1)}, bf16[4096,48]{0,1:T(8,128)(2,1)}, u32[]{:S(2)}) copy-start(bf16[4096,48]{0,1:T(8,128)(2,1)} %param.8) | copy-start | bytes 1179652
  20.2 16.0 %all-to-all-start = ((f32[8,1,4096]{2,1,0:T(1,128)}), f32[8,1,4096]{2,1,0:T(1,128)S(1)}, u32[]{:S(2)}, u32[]{:S(2)}) async-start(f32[8,1,4096]{2,1,0:T(1,128)} %slice.17), calls=%async_computation.1 | async-start | bytes 262144 | tf_op jit(solution)/shard_map/degree/all_to_all | solution.py:190
  37.6 29.4 %all-to-all-start.1 = ((bf16[16,48,1024]{2,1,0:T(8,128)(2,1)}), bf16[16,48,1024]{2,1,0:T(8,128)(2,1)S(1)}, u32[]{:S(2)}, u32[]{:S(2)}) async-start(bf16[16,48,1024]{2,1,0:T(8,128)(2,1)} %bitcast.37), calls=%async_computation.2 | async-start | bytes 3145728 | tf_op jit(solution)/shard_map/seed_rows/all_to_all | solution.py:200
  67.0 6.0 %copy-start.1 = (bf16[16,48,1024]{2,1,0:T(8,128)(2,1)}, bf16[16,48,1024]{2,1,0:T(8,128)(2,1)S(1)}, u32[]{:S(2)}) copy-start(bf16[16,48,1024]{2,1,0:T(8,128)(2,1)S(1)} %all-to-all-done.1) | copy-start | bytes 4718596
  67.0 12.3 %all-to-all-start.2 = ((bf16[4,64,1024]{2,1,0:T(8,128)(2,1)}), bf16[4,64,1024]{2,1,0:T(8,128)(2,1)}, u32[]{:S(2)}, u32[]{:S(2)}) async-start(bf16[4,64,1024]{2,1,0:T(8,128)(2,1)} %bitcast.38), calls=%async_computation.3 | async-start | bytes 1048576 | tf_op jit(solution)/shard_map/cotangent_rows/all_to_all | solution.py:194
  97.4 30.7 %all-to-all-start.3 = ((bf16[16,48,1024]{2,1,0:T(8,128)(2,1)}), bf16[16,48,1024]{2,1,0:T(8,128)(2,1)S(1)}, u32[]{:S(2)}, u32[]{:S(2)}) async-start(bf16[16,48,1024]{2,1,0:T(8,128)(2,1)} %mean_rows.1), calls=%async_computation.4 | async-start | bytes 3145728 | tf_op jit(solution)/shard_map/mean_rows/all_to_all | solution.py:210
  128.1 1.2 copy-start.2
  133.7 17.6 %copy-start.4 = (bf16[256,1024]{1,0:T(8,128)(2,1)S(1)}, bf16[256,1024]{1,0:T(8,128)(2,1)}, u32[]{:S(2)}) copy-start(bf16[256,1024]{1,0:T(8,128)(2,1)} %get-tuple-element.27) | copy-start | bytes 1572868
  133.7 16.7 %all-to-all-start.4 = ((bf16[16,96,256]{2,1,0:T(8,128)(2,1)}), bf16[16,96,256]{2,1,0:T(8,128)(2,1)S(1)}, u32[]{:S(2)}, u32[]{:S(2)}) async-start(bf16[16,96,256]{2,1,0:T(8,128)(2,1)} %get-tuple-element.25), calls=%async_computation.5 | async-start | bytes 1572864 | tf_op jit(solution)/shard_map/grads/all_to_all | solution.py:216
  151.3 9.2 %collective-permute-start = (bf16[64,1024]{1,0:T(8,128)(2,1)S(1)}, bf16[64,1024]{1,0:T(8,128)(2,1)S(1)}, u32[]{:S(2)}, u32[]{:S(2)}) collective-permute-start(bf16[64,1024]{1,0:T(8,128)(2,1)S(1)} %get-tuple-element.31), channel_id=1, source_target_pairs={{0,16},{16,32},{32,48},{48,0},{64,80},{80,96},{96,112},{112,64},{1... | collective-permute-start | bytes 393224 | tf_op jit(solution)/shard_map/hidden_columns/ppermute | solution.py:175
  152.0 15.1 %all-to-all-start.5 = ((bf16[8,96,128]{2,1,0:T(8,128)(2,1)}), bf16[8,96,128]{2,1,0:T(8,128)(2,1)S(1)}, u32[]{:S(2)}, u32[]{:S(2)}) async-start(bf16[8,96,128]{2,1,0:T(8,128)(2,1)} %bitcast.13), calls=%async_computation.6 | async-start | bytes 393216 | tf_op jit(solution)/shard_map/grads/all_to_all | solution.py:221
  157.8 9.2 %collective-permute-start.2 = (bf16[64,1024]{1,0:T(8,128)(2,1)S(1)}, bf16[64,1024]{1,0:T(8,128)(2,1)S(1)}, u32[]{:S(2)}, u32[]{:S(2)}) collective-permute-start(bf16[64,1024]{1,0:T(8,128)(2,1)S(1)} %get-tuple-element.29), channel_id=1, source_target_pairs={{0,48},{16,0},{32,16},{48,32},{64,112},{80,64},{96,80},{112,96},{1... | collective-permute-start | bytes 393224 | tf_op jit(solution)/shard_map/hidden_columns/ppermute | solution.py:175
  160.5 6.5 %collective-permute-start.1 = (bf16[64,1024]{1,0:T(8,128)(2,1)S(1)}, bf16[64,1024]{1,0:T(8,128)(2,1)S(1)}, u32[]{:S(2)}, u32[]{:S(2)}) collective-permute-start(bf16[64,1024]{1,0:T(8,128)(2,1)S(1)} %get-tuple-element.30), channel_id=1, source_target_pairs={{0,32},{16,48},{32,0},{48,16},{64,96},{80,112},{96,64},{112,80},{1... | collective-permute-start | bytes 393224 | tf_op jit(solution)/shard_map/hidden_columns/ppermute | solution.py:175
  167.0 0.8 copy-start.3
Sparse Core Ops, SparseCore 0:
  18.3 76.6 reduce-scatter.1

commit v2 on v1

v2 whole, which is shorter than its diff:
```python
import jax
import jax.numpy as jnp
from jax import lax
from jax.experimental import pallas as pl
from jax.experimental.pallas import tpu as pltpu
from jax.sharding import PartitionSpec as P

F32, BF16 = jnp.float32, jnp.bfloat16
UNROLL = 16
SIDE = 4
HBM = pl.BlockSpec(memory_space=pltpu.HBM)


def far(*arrays):
    return [pltpu.with_memory_space_constraint(a, pltpu.HBM) for a in arrays]


def tile_kernel(dst_h, src_h, feats_h, counts_h, sums_h, deg_h, *refs):
    dst, src, feats, counts, acc, deg, held, sems = refs
    cols = feats.shape[0]
    nsrc, rows, tile = held.shape
    owners, _, seeds_here = acc.shape
    per_owner = seeds_here // tile
    ntile = counts.shape[0]
    nload = ntile // UNROLL

    def load_counts(c):
        where = pl.ds(c * UNROLL, UNROLL)
        return pltpu.make_async_copy(counts_h.at[where], counts.at[where], sems.at[c])

    loads = [
        pltpu.make_async_copy(dst_h, dst, sems.at[nload]),
        pltpu.make_async_copy(src_h, src, sems.at[nload + 1]),
        pltpu.make_async_copy(feats_h, feats, sems.at[nload + 2]),
    ]
    for load in loads:
        load.start()
    for c in range(nload):
        load_counts(c).start()
    acc[...] = jnp.zeros_like(acc)
    deg[...] = jnp.zeros_like(deg)
    held[:, cols:, :] = jnp.ones((nsrc, rows - cols, tile), BF16)
    for load in loads:
        load.wait()
    for b in range(nsrc):
        held[b, :cols, :] = feats[:, b * tile : (b + 1) * tile]

    def chunk(c, _):
        load_counts(c).wait()
        for u in range(UNROLL):
            t = c * UNROLL + u
            d = dst[t]
            got = lax.dot_general(
                held[src[t]],
                counts[t].astype(F32).astype(BF16),
                (((1,), (1,)), ((), ())),
                preferred_element_type=F32,
            )
            owner = d // per_owner
            lanes = pl.ds(pl.multiple_of((d % per_owner) * tile, tile), tile)
            acc[owner, :, lanes] += got[:cols]
            deg[owner, :, lanes] += got[cols : cols + 8]
        return _

    lax.fori_loop(0, nload, chunk, 0)
    stores = [
        pltpu.make_async_copy(acc, sums_h, sems.at[0]),
        pltpu.make_async_copy(deg, deg_h, sems.at[1]),
    ]
    for store in stores:
        store.start()
    for store in stores:
        store.wait()


def tile_sums(dst_block, src_block, feats_t, counts, owners, seeds_here):
    ntile, tile, _ = counts.shape
    cols, sources = feats_t.shape
    outs = [(owners, cols, seeds_here), (owners, 8, seeds_here)]
    return pl.pallas_call(
        tile_kernel,
        in_specs=[HBM] * 4,
        out_specs=[HBM] * 2,
        out_shape=[pltpu.HBM(o, F32) for o in outs],
        scratch_shapes=[
            pltpu.SMEM((ntile,), jnp.int32),
            pltpu.SMEM((ntile,), jnp.int32),
            pltpu.VMEM((cols, sources), BF16),
            pltpu.VMEM(counts.shape, jnp.int32),
            *[pltpu.VMEM(o, F32) for o in outs],
            pltpu.VMEM((sources // tile, cols + 16, tile), BF16),
            pltpu.SemaphoreType.DMA((ntile // UNROLL + 3,)),
        ],
        compiler_params=pltpu.CompilerParams(vmem_limit_bytes=40 * 1024 * 1024),
    )(*far(dst_block, src_block, feats_t, counts))


def mean_kernel(total_h, degree_h, send_h, total, degree, send, sems):
    width = send.shape[2]
    lanes = [pl.ds(y * width, width) for y in range(SIDE)]
    first = pltpu.make_async_copy(degree_h, degree, sems.at[0])
    first.start()
    loads = [
        pltpu.make_async_copy(total_h.at[:, lanes[y]], total.at[:, lanes[y]], sems.at[1 + y])
        for y in range(SIDE)
    ]
    for load in loads:
        load.start()
    first.wait()
    stores = []
    for y in range(SIDE):
        loads[y].wait()
        send[y] = (total[:, lanes[y]] / (degree[:, lanes[y]] + 1.0)).astype(BF16)
        for x in range(SIDE):
            i = x * SIDE + y
            store = pltpu.make_async_copy(send.at[y], send_h.at[i], sems.at[1 + SIDE + i])
            store.start()
            stores.append(store)
    for store in stores:
        store.wait()


def mean_rows(total, degree):
    cols, n = total.shape
    send = (SIDE, cols, n // SIDE)
    return pl.pallas_call(
        mean_kernel,
        in_specs=[HBM, HBM],
        out_specs=HBM,
        out_shape=pltpu.HBM((SIDE * SIDE, *send[1:]), BF16),
        scratch_shapes=[
            pltpu.VMEM(total.shape, F32),
            pltpu.VMEM(degree.shape, F32),
            pltpu.VMEM(send, BF16),
            pltpu.SemaphoreType.DMA((1 + SIDE + SIDE * SIDE,)),
        ],
        compiler_params=pltpu.CompilerParams(vmem_limit_bytes=16 * 1024 * 1024),
    )(*far(total), degree)


def layer_kernel(ws_h, seeds_h, wn_h, means_h, cot_h, hid_h, grad_h, *refs):
    ws, seeds, wn, means, cot, hid, grad, sems = refs
    given = (ws_h, seeds_h, wn_h, means_h, cot_h)
    near = (ws, seeds, wn, means, cot)
    loads = [pltpu.make_async_copy(given[i], near[i], sems.at[i]) for i in range(5)]
    for load in loads:
        load.start()
    nf, rows, _ = grad.shape
    cols = rows // 2
    for load in loads[:2]:
        load.wait()
    total = jnp.dot(ws[...], seeds[...], preferred_element_type=F32)
    for load in loads[2:4]:
        load.wait()
    total += jnp.dot(wn[...], means[...], preferred_element_type=F32)
    h = jnp.maximum(total, 0.0).astype(BF16)
    hid[...] = h
    stores = [pltpu.make_async_copy(hid, hid_h, sems.at[5])]
    stores[0].start()
    loads[4].wait()
    dpre = jnp.where(h > 0, cot[...], jnp.zeros_like(h))
    dims = (((1,), (1,)), ((), ()))
    for j, x in enumerate((seeds, means)):
        at = j * cols
        g = lax.dot_general(x[...], dpre, dims, preferred_element_type=F32).astype(BF16)
        for i in range(nf):
            grad[i, at : at + cols, :] = g[i * cols : (i + 1) * cols]
        where = (slice(None), pl.ds(at, cols), slice(None))
        store = pltpu.make_async_copy(grad.at[where], grad_h.at[where], sems.at[6 + j])
        store.start()
        stores.append(store)
    for store in stores:
        store.wait()


def layer(ws_t, seeds, wn_t, means, cot, nf):
    hcols, rows = cot.shape
    args = (ws_t, seeds, wn_t, means, cot)
    shapes = [(hcols, rows), (nf, 2 * means.shape[0] // nf, hcols)]
    return pl.pallas_call(
        layer_kernel,
        in_specs=[HBM] * 5,
        out_specs=[HBM] * 2,
        out_shape=[pltpu.HBM(o, BF16) for o in shapes],
        scratch_shapes=[pltpu.VMEM(a.shape, a.dtype) for a in args]
        + [pltpu.VMEM(o, BF16) for o in shapes]
        + [pltpu.SemaphoreType.DMA((8,))],
        compiler_params=pltpu.CompilerParams(vmem_limit_bytes=40 * 1024 * 1024),
    )(*far(*args))


def shards(seed_feats, src_feats, counts, dst_block, src_block, w_self, w_neigh, cotangent):
    seeds_here, cols = seed_feats.shape
    ng = lax.axis_size("group")
    nf = lax.axis_size("feat")
    part = seeds_here // SIDE
    ccols = cotangent.shape[1]
    hcols = SIDE * ccols
    f = lax.axis_index("feat")
    fx, fy = f // SIDE, f % SIDE
    along_y = [[x * SIDE + y for y in range(SIDE)] for x in range(SIDE)]

    def shift_y(a, k):
        return lax.ppermute(
            a, "feat", [(i, i // SIDE * SIDE + (i % SIDE + k) % SIDE) for i in range(nf)]
        )

    with jax.named_scope("tile_sums"):
        sums, deg = tile_sums(dst_block, src_block, src_feats.T, counts, ng, seeds_here)

    with jax.named_scope("neighbour_sum"):
        total = lax.psum_scatter(
            sums.reshape(ng * cols, seeds_here), "group", scatter_dimension=0, tiled=True
        )

    seed_t, cot_t, deg, _ = lax.optimization_barrier((seed_feats.T, cotangent.T, deg, sums))

    with jax.named_scope("degree"):
        degree = jnp.sum(lax.all_to_all(deg[:, 0], "group", 0, 0, tiled=True), axis=0)[None]

    with jax.named_scope("cotangent_rows"):
        send = cot_t.reshape(ccols, SIDE, part).transpose(1, 0, 2)
        cot = lax.all_to_all(send, "feat", 0, 0, axis_index_groups=along_y)
        cot = cot.reshape(hcols, part)

    with jax.named_scope("seed_rows"):
        send = seed_t.reshape(cols, SIDE, part).transpose(1, 0, 2)
        send = jnp.broadcast_to(send[None], (SIDE, SIDE, cols, part)).reshape(nf, cols, part)
        seeds = lax.all_to_all(send, "feat", 0, 0).reshape(nf * cols, part)

    with jax.named_scope("weights"):
        ws_t = lax.dynamic_slice_in_dim(w_self, fx * hcols, hcols, 1).T
        wn_t = lax.dynamic_slice_in_dim(w_neigh, fx * hcols, hcols, 1).T

    with jax.named_scope("mean_rows"):
        total, degree, seeds, cot, ws_t, wn_t = lax.optimization_barrier(
            (total, degree, seeds, cot, ws_t, wn_t)
        )
        send = mean_rows(total, degree)
        means = lax.all_to_all(send, "feat", 0, 0).reshape(nf * cols, part)

    with jax.named_scope("layer"):
        hid, both = layer(ws_t, seeds, wn_t, means, cot, nf)

    with jax.named_scope("grads"):
        got = lax.all_to_all(both, "feat", 0, 0).astype(F32)
        got = jnp.sum(got.reshape(SIDE, SIDE, 2 * cols, hcols), axis=1)
        got = got.reshape(SIDE, 2 * cols, 2, hcols // 2).transpose(0, 2, 1, 3)
        got = got.reshape(ng, 2 * cols, hcols // 2).astype(BF16)
        got, hid = lax.optimization_barrier((got, hid))
        got = jnp.sum(lax.all_to_all(got, "group", 0, 0).astype(F32), axis=0)

    with jax.named_scope("hidden_columns"):
        hid4 = hid.reshape(SIDE, ccols, part)
        pieces = []
        for k in range(SIDE):
            piece = lax.dynamic_index_in_dim(hid4, (fy + k) % SIDE, 0, keepdims=False)
            pieces.append(shift_y(piece, k) if k else piece)
        got, *pieces = lax.optimization_barrier((got, *pieces))
        out = jnp.zeros((ccols, seeds_here), BF16)
        for k in range(SIDE):
            out = lax.dynamic_update_slice(out, pieces[k], (0, (fy - k) % SIDE * part))
    return (out.T, got[:cols], got[cols:])


def solution(mesh):
    in_specs = (
        P(("rep", "group"), "feat"),
        P(("rep", "group"), "feat"),
        P(("rep", "group"), None, None),
        P(("rep", "group")),
        P(("rep", "group")),
        P(),
        P(),
        P(("rep", "group"), "feat"),
    )
    out_specs = (
        P(("rep", "group"), "feat"),
        P(("rep", "feat"), "group"),
        P(("rep", "feat"), "group"),
    )
    return jax.shard_map(shards, mesh=mesh, in_specs=in_specs, out_specs=out_specs, check_vma=False)
```

time: 176 us -> 170 us (0.966)
  blocking collectives: 0 us -> 46.5 us
  waiting for transfers between devices: 90.5 us -> 55.1 us
  starting transfers between devices: 39.8 us -> 28.1 us
  Pallas kernels: 17.8 us -> 14.7 us
    all_to_all x0 -> x2, blocking collectives: none -> 46.5 us  [the longest x1 29.5 us: shards(): means = lax.all_to_all(send, 'feat', 0, 0).reshape(nf * cols, part)]
    all_to_all x2 -> x0, waiting for transfers between devices: 34.5 us -> none  [the longest x1 21.9 us: shards(): means = lax.all_to_all(send, 'feat', 0, 0).reshape(nf * cols, part)]
    all_to_all x2 -> x0, starting transfers between devices: 10.8 us -> none  [the longest x1 6.82 us: shards(): means = lax.all_to_all(send, 'feat', 0, 0).reshape(nf * cols, part)]
    ppermute x3, waiting for transfers between devices: 6.37 us -> 0.27 us  [shift_y(): lax.ppermute(a, 'feat', [(i, i // SIDE * SIDE + (i % SIDE + k) % SIDE) fo...]
    all_to_all x1, waiting for transfers between devices: 0.01 us -> 4.03 us  [shards(): got = jnp.sum(lax.all_to_all(got, 'group', 0, 0).astype(F32), axis=0)]
    pallas_call x1, Pallas kernels: 10.9 us -> 7.34 us  [tile_sums(): pl.pallas_call(tile_kernel, in_specs=[HBM] * 4, out_specs=[HBM] * 2, out_...]
    reduce_scatter x1, waiting for transfers between devices: 15.7 us -> 19.1 us  [shards(): lax.psum_scatter(sums.reshape(ng * cols, seeds_here), 'group', scatter_di...]
    all_to_all x1, waiting for transfers between devices: 20.5 us -> 17.3 us  [shards(): seeds = lax.all_to_all(send, 'feat', 0, 0).reshape(nf * cols, part)]
  transfers between devices with their start and end apart: 10 -> 8, of which waited for: 7 -> 6; matrix products, arithmetic and copies ran while one was open for 5% -> 5% of each run, Pallas kernels for 0% -> 0%
where the time goes in v2:
time: 170 us; the launch traced here: 169 us
  waiting for transfers between devices  55.1 us (32%)
  blocking collectives  46.5 us (27%)
  starting transfers between devices  28.1 us (17%)
  Pallas kernels  14.7 us (9%)
  between operations  14.2 us (8%)
  local copies, waits for them, and re-layouts  9.31 us (5%)
    all_to_all x1, blocking collectives, shards(): means = lax.all_to_all(send, 'feat', 0, 0).reshape(nf * cols, part)  29.5 us
    reduce_scatter x1, waiting for transfers between devices, shards(): lax.psum_scatter(sums.reshape(ng * cols, seeds_here), 'group', scatter_di...  19.1 us
    all_to_all x1, waiting for transfers between devices, shards(): seeds = lax.all_to_all(send, 'feat', 0, 0).reshape(nf * cols, part)  17.3 us
    all_to_all x1, blocking collectives, shards(): got = lax.all_to_all(both, 'feat', 0, 0).astype(F32)  17 us
    all_to_all x1, starting transfers between devices, shards(): lax.all_to_all(deg[:, 0], 'group', 0, 0, tiled=True)  8.56 us
    all_to_all x1, waiting for transfers between devices, shards(): cot = lax.all_to_all(send, 'feat', 0, 0, axis_index_groups=along_y)  7.82 us
    pallas_call x1, Pallas kernels, tile_sums(): pl.pallas_call(tile_kernel, in_specs=[HBM] * 4, out_specs=[HBM] * 2, out_...  7.34 us
    all_to_all x1, waiting for transfers between devices, shards(): lax.all_to_all(deg[:, 0], 'group', 0, 0, tiled=True)  6.61 us
  transfers between devices with their start and end apart: 8, of which 6 were waited for; matrix products, arithmetic and copies ran while one was open for 5% of the time, Pallas kernels for 0%

profile of v2, /device:TPU:32, one launch (start us, length us, event | category | flops | bytes accessed | tf_op | source)
XLA Modules:
  0.0 169.0 jit_solution(3368035535353024168)
XLA Ops:
  7.2 0.0 reduce-scatter.2.cloned.1.call-start
  7.2 7.3 %tile_sums.1 = (f32[8,48,4096]{2,1,0:T(8,128)}, f32[8,8,4096]{2,1,0:T(8,128)}) custom-call(s32[96]{0:T(128)} %dst_h.1, s32[96]{0:T(128)} %src_h.1, bf16[48,8192]{1,0:T(8,128)(2,1)} %bitcast.40, s32[96,128,128]{2,1,0:T(8,128)} %counts_h.1), custom_call_target="tpu_custom_call" | custom-call | tf_op jit(solution)/shard_map/tile_sums/pallas_call | solution.py:80
  14.6 0.0 copy-start.3
  14.6 0.0 reduce-scatter.2.cloned.1.call-update
  14.6 0.0 copy-start.5
  14.6 2.0 %slice.17 = f32[8,1,4096]{2,1,0:T(1,128)} slice(f32[8,8,4096]{2,1,0:T(8,128)} %get-tuple-element.25), slice={[0:8], [0:1], [0:4096]} | slice | bytes 262144 | tf_op jit(solution)/shard_map/degree/slice | solution.py:219
  16.6 8.6 %all-to-all-start = ((f32[8,1,4096]{2,1,0:T(1,128)}), f32[8,1,4096]{2,1,0:T(1,128)S(1)}, u32[]{:S(2)}, u32[]{:S(2)}) async-start(f32[8,1,4096]{2,1,0:T(1,128)} %slice.17), calls=%async_computation.1 | async-start | bytes 262144 | tf_op jit(solution)/shard_map/degree/all_to_all | solution.py:219
  25.2 0.0 copy-done.3
  25.2 0.8 copy.23
  26.0 6.6 %all-to-all-done = f32[8,1,4096]{2,1,0:T(1,128)S(1)} async-done(((f32[8,1,4096]{2,1,0:T(1,128)}), f32[8,1,4096]{2,1,0:T(1,128)S(1)}, u32[]{:S(2)}, u32[]{:S(2)}) %all-to-all-start) | async-done | bytes 131104 | tf_op jit(solution)/shard_map/degree/all_to_all | solution.py:219
  32.6 4.5 %all-to-all-start.2 = ((bf16[4,64,1024]{2,1,0:T(8,128)(2,1)}), bf16[4,64,1024]{2,1,0:T(8,128)(2,1)S(1)}, u32[]{:S(2)}, u32[]{:S(2)}) async-start(bf16[4,64,1024]{2,1,0:T(8,128)(2,1)} %bitcast.31), calls=%async_computation.3 | async-start | bytes 1048576 | tf_op jit(solution)/shard_map/cotangent_rows/all_to_all | solution.py:223
  37.1 0.0 copy-done.5
  37.1 0.3 reshape.44
  37.4 0.1 copy.15
  37.5 7.8 %all-to-all-done.2 = bf16[4,64,1024]{2,1,0:T(8,128)(2,1)S(1)} async-done(((bf16[4,64,1024]{2,1,0:T(8,128)(2,1)}), bf16[4,64,1024]{2,1,0:T(8,128)(2,1)S(1)}, u32[]{:S(2)}, u32[]{:S(2)}) %all-to-all-start.2) | async-done | bytes 524320 | tf_op jit(solution)/shard_map/cotangent_rows/all_to_all | solution.py:223
  45.3 0.0 copy-start.1
  45.3 1.4 broadcast_in_dim.14
  46.7 0.0 copy-done.1
  46.7 5.1 %all-to-all-start.1 = ((bf16[16,48,1024]{2,1,0:T(8,128)(2,1)}), bf16[16,48,1024]{2,1,0:T(8,128)(2,1)S(1)}, u32[]{:S(2)}, u32[]{:S(2)}) async-start(bf16[16,48,1024]{2,1,0:T(8,128)(2,1)} %bitcast.6), calls=%async_computation.2 | async-start | bytes 3145728 | tf_op jit(solution)/shard_map/seed_rows/all_to_all | solution.py:229
  51.8 1.2 constant_dynamic-slice_fusion
  53.0 1.0 copy.19
  54.0 0.9 copy.20
  54.9 0.1 reduce_sum.27
  55.0 17.3 %all-to-all-done.1 = bf16[16,48,1024]{2,1,0:T(8,128)(2,1)S(1)} async-done(((bf16[16,48,1024]{2,1,0:T(8,128)(2,1)}), bf16[16,48,1024]{2,1,0:T(8,128)(2,1)S(1)}, u32[]{:S(2)}, u32[]{:S(2)}) %all-to-all-start.1) | async-done | bytes 1572896 | tf_op jit(solution)/shard_map/seed_rows/all_to_all | solution.py:229
  72.3 0.0 copy-start
  72.3 19.1 %reduce-scatter.2.cloned.1.call-done.total_h = f32[48,4096]{1,0:T(8,128)} async-done(((f32[384,4096]{1,0:T(8,128)}), f32[48,4096]{1,0:T(8,128)}) %reduce-scatter.2.cloned.1.call-update) | async-done | bytes 786448 | tf_op jit(solution)/shard_map/neighbour_sum/reduce_scatter | solution.py:212
  91.4 2.3 %mean_rows.1 = bf16[16,48,1024]{2,1,0:T(8,128)(2,1)} custom-call(f32[48,4096]{1,0:T(8,128)} %reduce-scatter.2.cloned.1.call-done.total_h, f32[1,4096]{1,0:T(1,128)S(1)} %bitcast.32), custom_call_target="tpu_custom_call" | custom-call | tf_op jit(solution)/shard_map/mean_rows/pallas_call | solution.py:126
  93.7 29.5 %all_to_all.31 = bf16[16,48,1024]{2,1,0:T(8,128)(2,1)} all-to-all(bf16[16,48,1024]{2,1,0:T(8,128)(2,1)} %mean_rows.1), channel_id=1, replica_groups=mesh['feat'=16,'group'=8,'rep'=2] {'feat'}, dimensions={0} | all-to-all | bytes 3145728 | tf_op jit(solution)/shard_map/mean_rows/all_to_all | solution.py:240
  123.2 0.0 copy-done
  123.2 5.1 %layer.1 = (bf16[256,1024]{1,0:T(8,128)(2,1)}, bf16[16,96,256]{2,1,0:T(8,128)(2,1)}) custom-call(bf16[256,768]{1,0:T(8,128)(2,1)} %bitcast.37, bf16[768,1024]{1,0:T(8,128)(2,1)} %bitcast.34, bf16[256,768]{1,0:T(8,128)(2,1)} %bitcast.38, bf16[768,1024]{1,0:T(8,128)(2,1)} %bitcast.35, bf16[256,1024]{1,0:T(8,128)(2,1)} %bitcast.36), custom_call_target="tpu_custom_call" | custom-call | tf_op jit(solution)/shard_map/layer/pallas_call | solution.py:180
  128.3 0.0 copy-start.4
  128.4 17.0 %all_to_all.32 = bf16[16,96,256]{2,1,0:T(8,128)(2,1)S(1)} all-to-all(bf16[16,96,256]{2,1,0:T(8,128)(2,1)} %get-tuple-element.34), channel_id=1, replica_groups=mesh['feat'=16,'group'=8,'rep'=2] {'feat'}, dimensions={0} | all-to-all | bytes 1572864 | tf_op jit(solution)/shard_map/grads/all_to_all | solution.py:246
  145.4 0.1 bitcast_reduce_fusion
  145.5 0.7 pad_maximum_fusion
  146.2 5.8 %all-to-all-start.5 = ((bf16[8,96,128]{2,1,0:T(8,128)(2,1)}), bf16[8,96,128]{2,1,0:T(8,128)(2,1)S(1)}, u32[]{:S(2)}, u32[]{:S(2)}) async-start(bf16[8,96,128]{2,1,0:T(8,128)(2,1)} %bitcast.14), calls=%async_computation.6 | async-start | bytes 393216 | tf_op jit(solution)/shard_map/grads/all_to_all | solution.py:251
  152.0 0.0 copy-done.4
  152.1 0.5 collective-permute-start
  152.5 2.0 %collective-permute-start.1 = (bf16[64,1024]{1,0:T(8,128)(2,1)S(1)}, bf16[64,1024]{1,0:T(8,128)(2,1)S(1)}, u32[]{:S(2)}, u32[]{:S(2)}) collective-permute-start(bf16[64,1024]{1,0:T(8,128)(2,1)S(1)} %get-tuple-element.44), channel_id=1, source_target_pairs={{0,32},{16,48},{32,0},{48,16},{64,96},{80,112},{96,64},{112,80},{1... | collective-permute-start | bytes 393224 | tf_op jit(solution)/shard_map/hidden_columns/ppermute | solution.py:204
  154.6 1.7 %collective-permute-start.2 = (bf16[64,1024]{1,0:T(8,128)(2,1)S(1)}, bf16[64,1024]{1,0:T(8,128)(2,1)S(1)}, u32[]{:S(2)}, u32[]{:S(2)}) collective-permute-start(bf16[64,1024]{1,0:T(8,128)(2,1)S(1)} %get-tuple-element.43), channel_id=1, source_target_pairs={{0,48},{16,0},{32,16},{48,32},{64,112},{80,64},{96,80},{112,96},{1... | collective-permute-start | bytes 393224 | tf_op jit(solution)/shard_map/hidden_columns/ppermute | solution.py:204
  156.2 4.0 %all-to-all-done.5 = bf16[8,96,128]{2,1,0:T(8,128)(2,1)S(1)} async-done(((bf16[8,96,128]{2,1,0:T(8,128)(2,1)}), bf16[8,96,128]{2,1,0:T(8,128)(2,1)S(1)}, u32[]{:S(2)}, u32[]{:S(2)}) %all-to-all-start.5) | async-done | bytes 196640 | tf_op jit(solution)/shard_map/grads/all_to_all | solution.py:251
  160.3 0.0 collective-permute-done
  160.3 0.0 collective-permute-done.1
  160.3 0.3 collective-permute-done.2
  160.6 0.6 fusion.1
  161.3 0.0 copy-start.2
  161.4 0.8 copy-done.2
  (8 shorter events, 0.2 us)
Async XLA Ops:
  7.2 84.2 %reduce-scatter.2.cloned.1.call-start = ((), (), s32[]{:S(2)}) async-start(), calls=%async_computation.7 | async-start | bytes 7077888 | tf_op jit(solution)/shard_map/neighbour_sum/reduce_scatter | solution.py:212
  14.6 10.6 %copy-start.3 = (bf16[4096,64]{0,1:T(8,128)(2,1)S(1)}, bf16[4096,64]{0,1:T(8,128)(2,1)}, u32[]{:S(2)}) copy-start(bf16[4096,64]{0,1:T(8,128)(2,1)} %param.15) | copy-start | bytes 1572868
  14.6 22.5 %copy-start.5 = (bf16[4096,48]{0,1:T(8,128)(2,1)S(1)}, bf16[4096,48]{0,1:T(8,128)(2,1)}, u32[]{:S(2)}) copy-start(bf16[4096,48]{0,1:T(8,128)(2,1)} %param.8) | copy-start | bytes 1179652
  16.6 16.0 %all-to-all-start = ((f32[8,1,4096]{2,1,0:T(1,128)}), f32[8,1,4096]{2,1,0:T(1,128)S(1)}, u32[]{:S(2)}, u32[]{:S(2)}) async-start(f32[8,1,4096]{2,1,0:T(1,128)} %slice.17), calls=%async_computation.1 | async-start | bytes 262144 | tf_op jit(solution)/shard_map/degree/all_to_all | solution.py:219
  32.6 12.7 %all-to-all-start.2 = ((bf16[4,64,1024]{2,1,0:T(8,128)(2,1)}), bf16[4,64,1024]{2,1,0:T(8,128)(2,1)S(1)}, u32[]{:S(2)}, u32[]{:S(2)}) async-start(bf16[4,64,1024]{2,1,0:T(8,128)(2,1)} %bitcast.31), calls=%async_computation.3 | async-start | bytes 1048576 | tf_op jit(solution)/shard_map/cotangent_rows/all_to_all | solution.py:223
  45.3 1.4 copy-start.1
  46.7 25.6 %all-to-all-start.1 = ((bf16[16,48,1024]{2,1,0:T(8,128)(2,1)}), bf16[16,48,1024]{2,1,0:T(8,128)(2,1)S(1)}, u32[]{:S(2)}, u32[]{:S(2)}) async-start(bf16[16,48,1024]{2,1,0:T(8,128)(2,1)} %bitcast.6), calls=%async_computation.2 | async-start | bytes 3145728 | tf_op jit(solution)/shard_map/seed_rows/all_to_all | solution.py:229
  72.3 50.9 %copy-start = (bf16[16,48,1024]{2,1,0:T(8,128)(2,1)}, bf16[16,48,1024]{2,1,0:T(8,128)(2,1)S(1)}, u32[]{:S(2)}) copy-start(bf16[16,48,1024]{2,1,0:T(8,128)(2,1)S(1)} %all-to-all-done.1) | copy-start | bytes 4718596
  128.3 23.7 %copy-start.4 = (bf16[256,1024]{1,0:T(8,128)(2,1)S(1)}, bf16[256,1024]{1,0:T(8,128)(2,1)}, u32[]{:S(2)}) copy-start(bf16[256,1024]{1,0:T(8,128)(2,1)} %get-tuple-element.37) | copy-start | bytes 1572868
  146.2 14.1 %all-to-all-start.5 = ((bf16[8,96,128]{2,1,0:T(8,128)(2,1)}), bf16[8,96,128]{2,1,0:T(8,128)(2,1)S(1)}, u32[]{:S(2)}, u32[]{:S(2)}) async-start(bf16[8,96,128]{2,1,0:T(8,128)(2,1)} %bitcast.14), calls=%async_computation.6 | async-start | bytes 393216 | tf_op jit(solution)/shard_map/grads/all_to_all | solution.py:251
  152.1 8.2 %collective-permute-start = (bf16[64,1024]{1,0:T(8,128)(2,1)S(1)}, bf16[64,1024]{1,0:T(8,128)(2,1)S(1)}, u32[]{:S(2)}, u32[]{:S(2)}) collective-permute-start(bf16[64,1024]{1,0:T(8,128)(2,1)S(1)} %get-tuple-element.45), channel_id=1, source_target_pairs={{0,16},{16,32},{32,48},{48,0},{64,80},{80,96},{96,112},{112,64},{1... | collective-permute-start | bytes 393224 | tf_op jit(solution)/shard_map/hidden_columns/ppermute | solution.py:204
  152.5 7.8 %collective-permute-start.1 = (bf16[64,1024]{1,0:T(8,128)(2,1)S(1)}, bf16[64,1024]{1,0:T(8,128)(2,1)S(1)}, u32[]{:S(2)}, u32[]{:S(2)}) collective-permute-start(bf16[64,1024]{1,0:T(8,128)(2,1)S(1)} %get-tuple-element.44), channel_id=1, source_target_pairs={{0,32},{16,48},{32,0},{48,16},{64,96},{80,112},{96,64},{112,80},{1... | collective-permute-start | bytes 393224 | tf_op jit(solution)/shard_map/hidden_columns/ppermute | solution.py:204
  154.6 6.0 %collective-permute-start.2 = (bf16[64,1024]{1,0:T(8,128)(2,1)S(1)}, bf16[64,1024]{1,0:T(8,128)(2,1)S(1)}, u32[]{:S(2)}, u32[]{:S(2)}) collective-permute-start(bf16[64,1024]{1,0:T(8,128)(2,1)S(1)} %get-tuple-element.43), channel_id=1, source_target_pairs={{0,48},{16,0},{32,16},{48,32},{64,112},{80,64},{96,80},{112,96},{1... | collective-permute-start | bytes 393224 | tf_op jit(solution)/shard_map/hidden_columns/ppermute | solution.py:204
  161.3 0.8 copy-start.2
Sparse Core Ops, SparseCore 0:
  14.7 76.6 reduce-scatter.1

commit v3 on v2

--- a/solution.py
+++ b/solution.py
@@ -8,6 +8,7 @@
 F32, BF16 = jnp.float32, jnp.bfloat16
 UNROLL = 16
 SIDE = 4
+EARLY = 7
 HBM = pl.BlockSpec(memory_space=pltpu.HBM)
 
 
@@ -15,8 +16,10 @@
     return [pltpu.with_memory_space_constraint(a, pltpu.HBM) for a in arrays]
 
 
-def tile_kernel(dst_h, src_h, feats_h, counts_h, sums_h, deg_h, *refs):
-    dst, src, feats, counts, acc, deg, held, sems = refs
+def tile_kernel(me, dst_h, src_h, feats_h, counts_h, sums_h, *refs):
+    *late_h, deg_h, dst, src, feats, counts, acc, deg, held, short, sems = refs
+    per_part = acc.shape[2] // held.shape[2] // SIDE
+    early = sums_h.shape[2]
     cols = feats.shape[0]
     nsrc, rows, tile = held.shape
     owners, _, seeds_here = acc.shape
@@ -56,43 +59,59 @@
                 (((1,), (1,)), ((), ())),
                 preferred_element_type=F32,
             )
-            owner = d // per_owner
-            lanes = pl.ds(pl.multiple_of((d % per_owner) * tile, tile), tile)
+            owner, blk = d // per_owner, d % per_owner
+            y, r = blk // per_part, blk % per_part
+            late_at = SIDE * EARLY + y * (per_part - EARLY) + r - EARLY
+            at = jnp.where(r < EARLY, y * EARLY + r, late_at)
+            lanes = pl.ds(pl.multiple_of(at * tile, tile), tile)
             acc[owner, :, lanes] += got[:cols]
             deg[owner, :, lanes] += got[cols : cols + 8]
         return _
 
     lax.fori_loop(0, nload, chunk, 0)
-    stores = [
-        pltpu.make_async_copy(acc, sums_h, sems.at[0]),
-        pltpu.make_async_copy(deg, deg_h, sems.at[1]),
-    ]
+    stores = []
+    for k in (4, 5):
+        stores.append((acc.at[lax.rem(me[0] + k, owners), :, pl.ds(early, seeds_here - early)], late_h[k]))
+    width = short.shape[2]
+    for o in range(owners):
+        for r in range(short.shape[1]):
+            short[o, r : r + 1, :] = deg[o, :1, r * width : (r + 1) * width]
+    stores.append((short, deg_h))
+    stores.append((acc.at[:, :, pl.ds(0, early)], sums_h))
+    for k in (3, 6, 2, 7, 1, 0):
+        stores.append((acc.at[lax.rem(me[0] + k, owners), :, pl.ds(early, seeds_here - early)], late_h[k]))
+    stores = [pltpu.make_async_copy(p, q, sems.at[i]) for i, (p, q) in enumerate(stores)]
     for store in stores:
         store.start()
     for store in stores:
         store.wait()
 
 
-def tile_sums(dst_block, src_block, feats_t, counts, owners, seeds_here):
+def tile_sums(me, dst_block, src_block, feats_t, counts, owners, seeds_here):
     ntile, tile, _ = counts.shape
     cols, sources = feats_t.shape
-    outs = [(owners, cols, seeds_here), (owners, 8, seeds_here)]
-    return pl.pallas_call(
+    early = seeds_here // 8 * EARLY
+    outs = [(owners, cols, early)] + [(cols, seeds_here - early)] * owners
+    outs.append((owners, 8, seeds_here // 8))
+    sums, *late, deg = pl.pallas_call(
         tile_kernel,
-        in_specs=[HBM] * 4,
-        out_specs=[HBM] * 2,
+        in_specs=[pl.BlockSpec(memory_space=pltpu.SMEM)] + [HBM] * 4,
+        out_specs=[HBM] * len(outs),
         out_shape=[pltpu.HBM(o, F32) for o in outs],
         scratch_shapes=[
             pltpu.SMEM((ntile,), jnp.int32),
             pltpu.SMEM((ntile,), jnp.int32),
             pltpu.VMEM((cols, sources), BF16),
             pltpu.VMEM(counts.shape, jnp.int32),
-            *[pltpu.VMEM(o, F32) for o in outs],
+            pltpu.VMEM((owners, cols, seeds_here), F32),
+            pltpu.VMEM((owners, 8, seeds_here), F32),
             pltpu.VMEM((sources // tile, cols + 16, tile), BF16),
-            pltpu.SemaphoreType.DMA((ntile // UNROLL + 3,)),
+            pltpu.VMEM((owners, 8, seeds_here // 8), F32),
+            pltpu.SemaphoreType.DMA((max(ntile // UNROLL + 3, len(outs)),)),
         ],
         compiler_params=pltpu.CompilerParams(vmem_limit_bytes=40 * 1024 * 1024),
-    )(*far(dst_block, src_block, feats_t, counts))
+    )(me, *far(dst_block, src_block, feats_t, counts))
+    return sums, late, deg
 
 
 def mean_kernel(total_h, degree_h, send_h, total, degree, send, sems):
@@ -138,15 +157,25 @@
     )(*far(total), degree)
 
 
-def layer_kernel(ws_h, seeds_h, wn_h, means_h, cot_h, hid_h, grad_h, *refs):
-    ws, seeds, wn, means, cot, hid, grad, sems = refs
-    given = (ws_h, seeds_h, wn_h, means_h, cot_h)
-    near = (ws, seeds, wn, means, cot)
-    loads = [pltpu.make_async_copy(given[i], near[i], sems.at[i]) for i in range(5)]
+def layer_kernel(lo, last, *refs):
+    nin = 7 if last else 5
+    given, (hid_h, grad_h) = refs[:nin], refs[nin : nin + 2]
+    ws, seeds, wn, means, cot, hid, grad, *rest = refs[nin + 2 :]
+    sems = rest[-1]
+    width = means.shape[1]
+    lanes = (slice(None), pl.ds(lo, width))
+    pairs = [
+        (given[0], ws),
+        (given[1].at[lanes], seeds),
+        (given[2], wn),
+        (given[3], means),
+        (given[4].at[lanes], cot),
+    ]
+    if last:
+        pairs.append((given[6], rest[0]))
+    loads = [pltpu.make_async_copy(p, q, sems.at[i]) for i, (p, q) in enumerate(pairs)]
     for load in loads:
         load.start()
-    nf, rows, _ = grad.shape
-    cols = rows // 2
     for load in loads[:2]:
         load.wait()
     total = jnp.dot(ws[...], seeds[...], preferred_element_type=F32)
@@ -155,36 +184,55 @@
     total += jnp.dot(wn[...], means[...], preferred_element_type=F32)
     h = jnp.maximum(total, 0.0).astype(BF16)
     hid[...] = h
-    stores = [pltpu.make_async_copy(hid, hid_h, sems.at[5])]
+    stores = [pltpu.make_async_copy(hid, hid_h.at[lanes], sems.at[6])]
     stores[0].start()
-    loads[4].wait()
+    for load in loads[4:]:
+        load.wait()
     dpre = jnp.where(h > 0, cot[...], jnp.zeros_like(h))
     dims = (((1,), (1,)), ((), ()))
     for j, x in enumerate((seeds, means)):
-        at = j * cols
-        g = lax.dot_general(x[...], dpre, dims, preferred_element_type=F32).astype(BF16)
-        for i in range(nf):
-            grad[i, at : at + cols, :] = g[i * cols : (i + 1) * cols]
-        where = (slice(None), pl.ds(at, cols), slice(None))
-        store = pltpu.make_async_copy(grad.at[where], grad_h.at[where], sems.at[6 + j])
+        g = lax.dot_general(x[...], dpre, dims, preferred_element_type=F32)
+        if last:
+            g = (g + rest[0][j]).astype(BF16)
+            cols = grad.shape[1] // 2
+            at = j * cols
+            for i in range(grad.shape[0]):
+                grad[i, at : at + cols, :] = g[i * cols : (i + 1) * cols]
+            where = (slice(None), pl.ds(at, cols), slice(None))
+        else:
+            grad[j] = g
+            where = j
+        store = pltpu.make_async_copy(grad.at[where], grad_h.at[where], sems.at[7 + j])
         store.start()
         stores.append(store)
     for store in stores:
         store.wait()
 
 
-def layer(ws_t, seeds, wn_t, means, cot, nf):
+def layer(ws_t, seeds, wn_t, means, cot, lo, before, nf):
     hcols, rows = cot.shape
-    args = (ws_t, seeds, wn_t, means, cot)
-    shapes = [(hcols, rows), (nf, 2 * means.shape[0] // nf, hcols)]
+    depth, width = means.shape
+    last = before is not None
+    args = (ws_t, seeds, wn_t, means, cot) + (before if last else ())
+    grad = ((nf, 2 * depth // nf, hcols), BF16) if last else ((2, depth, hcols), F32)
+    near = [
+        ((hcols, depth), BF16),
+        ((depth, width), BF16),
+        ((hcols, depth), BF16),
+        ((depth, width), BF16),
+        ((hcols, width), BF16),
+        ((hcols, width), BF16),
+        grad,
+    ]
+    if last:
+        near.append(((2, depth, hcols), F32))
     return pl.pallas_call(
-        layer_kernel,
-        in_specs=[HBM] * 5,
+        lambda *refs: layer_kernel(lo, last, *refs),
+        in_specs=[HBM] * len(args),
         out_specs=[HBM] * 2,
-        out_shape=[pltpu.HBM(o, BF16) for o in shapes],
-        scratch_shapes=[pltpu.VMEM(a.shape, a.dtype) for a in args]
-        + [pltpu.VMEM(o, BF16) for o in shapes]
-        + [pltpu.SemaphoreType.DMA((8,))],
+        out_shape=[pltpu.HBM((hcols, rows), BF16), pltpu.HBM(*grad)],
+        scratch_shapes=[pltpu.VMEM(*n) for n in near] + [pltpu.SemaphoreType.DMA((9,))],
+        input_output_aliases={5: 0} if last else {},
         compiler_params=pltpu.CompilerParams(vmem_limit_bytes=40 * 1024 * 1024),
     )(*far(*args))
 
@@ -205,42 +253,68 @@
             a, "feat", [(i, i // SIDE * SIDE + (i % SIDE + k) % SIDE) for i in range(nf)]
         )
 
+    def shift_z(a, k):
+        return lax.ppermute(a, "group", [(i, (i + k) % ng) for i in range(ng)])
+
+    def meet(*arrays):
+        return lax.optimization_barrier(arrays)
+
     with jax.named_scope("tile_sums"):
-        sums, deg = tile_sums(dst_block, src_block, src_feats.T, counts, ng, seeds_here)
+        me = lax.axis_index("group")[None].astype(jnp.int32)
+        sums, late, deg = tile_sums(
+            me, dst_block, src_block, src_feats.T, counts, ng, seeds_here
+        )
 
     with jax.named_scope("neighbour_sum"):
         total = lax.psum_scatter(
-            sums.reshape(ng * cols, seeds_here), "group", scatter_dimension=0, tiled=True
+            sums.reshape(ng * cols, -1), "group", scatter_dimension=0, tiled=True
         )
 
-    seed_t, cot_t, deg, _ = lax.optimization_barrier((seed_feats.T, cotangent.T, deg, sums))
+    with jax.named_scope("weights"):
+        ws_t = lax.dynamic_slice_in_dim(w_self, fx * hcols, hcols, 1).T
+        wn_t = lax.dynamic_slice_in_dim(w_neigh, fx * hcols, hcols, 1).T
+
+    with jax.named_scope("hop_1"):
+        up = shift_z(late[4], 1)
+        down = shift_z(late[5], -1)
+        up, down, seed_t = meet(up, down, seed_feats.T)
 
     with jax.named_scope("degree"):
-        degree = jnp.sum(lax.all_to_all(deg[:, 0], "group", 0, 0, tiled=True), axis=0)[None]
+        degree = jnp.sum(lax.all_to_all(deg, "group", 0, 0), axis=0).reshape(1, seeds_here)
+
+    with jax.named_scope("seed_rows"):
+        send = seed_t.reshape(cols, SIDE, part).transpose(1, 0, 2)
+        send = jnp.broadcast_to(send[None], (SIDE, SIDE, cols, part)).reshape(nf, cols, part)
+        seeds = lax.all_to_all(send, "feat", 0, 0).reshape(nf * cols, part)
+
+    with jax.named_scope("hop_2"):
+        up = shift_z(up + late[3], 1)
+        down = shift_z(down + late[6], -1)
+        up, down, degree, cot_t = meet(up, down, degree, cotangent.T)
 
     with jax.named_scope("cotangent_rows"):
         send = cot_t.reshape(ccols, SIDE, part).transpose(1, 0, 2)
         cot = lax.all_to_all(send, "feat", 0, 0, axis_index_groups=along_y)
         cot = cot.reshape(hcols, part)
 
-    with jax.named_scope("seed_rows"):
-        send = seed_t.reshape(cols, SIDE, part).transpose(1, 0, 2)
-        send = jnp.broadcast_to(send[None], (SIDE, SIDE, cols, part)).reshape(nf, cols, part)
-        seeds = lax.all_to_all(send, "feat", 0, 0).reshape(nf * cols, part)
-
-    with jax.named_scope("weights"):
-        ws_t = lax.dynamic_slice_in_dim(w_self, fx * hcols, hcols, 1).T
-        wn_t = lax.dynamic_slice_in_dim(w_neigh, fx * hcols, hcols, 1).T
-
-    with jax.named_scope("mean_rows"):
-        total, degree, seeds, cot, ws_t, wn_t = lax.optimization_barrier(
-            (total, degree, seeds, cot, ws_t, wn_t)
-        )
-        send = mean_rows(total, degree)
-        means = lax.all_to_all(send, "feat", 0, 0).reshape(nf * cols, part)
-
-    with jax.named_scope("layer"):
-        hid, both = layer(ws_t, seeds, wn_t, means, cot, nf)
+    with jax.named_scope("hop_3"):
+        up = shift_z(up + late[2], 1)
+        down = shift_z(down + late[7], -1)
+        up, down, seeds = meet(up, down, seeds)
+
+    with jax.named_scope("hop_4"):
+        up = shift_z(up + late[1], 1)
+        total2, cot = meet(late[0] + up + down, cot)
+
+    early = total.shape[1]
+    before = None
+    for x, lo, hi in ((total2, early, seeds_here), (total, 0, early)):
+        with jax.named_scope("mean_rows_%d" % lo):
+            send = mean_rows(x, degree[:, lo:hi])
+            means = lax.all_to_all(send, "feat", 0, 0).reshape(nf * cols, -1)
+        with jax.named_scope("layer_%d" % lo):
+            before = layer(ws_t, seeds, wn_t, means, cot, lo // SIDE, before, nf)
+    hid, both = before
 
     with jax.named_scope("grads"):
         got = lax.all_to_all(both, "feat", 0, 0).astype(F32)

time: 170 us -> 168 us (0.988)
  blocking collectives: 46.5 us -> 16.3 us
  starting transfers between devices: 28.1 us -> 50.1 us
  Pallas kernels: 14.7 us -> 19.3 us
  waiting for transfers between devices: 55.1 us -> 57.1 us
    all_to_all x1 -> x0, blocking collectives: 29.5 us -> none  [shards(): means = lax.all_to_all(send, 'feat', 0, 0).reshape(nf * cols, part)]
    ppermute x0 -> x7, waiting for transfers between devices: none -> 16.7 us  [shift_z(): return lax.ppermute(a, 'group', [(i, (i + k) % ng) for i in range(ng)])]
    all_to_all x1 -> x3, starting transfers between devices: 8.56 us -> 20.6 us  [the longest x2 11.9 us: shards(): means = lax.all_to_all(send, 'feat', 0, 0).reshape(nf * cols, -1)]
    reduce_scatter x1, waiting for transfers between devices: 19.1 us -> 7.95 us  [shards(): lax.psum_scatter(sums.reshape(ng * cols, -1), 'group', scatter_dimension=...]
    all_to_all x1 -> x3, waiting for transfers between devices: 6.61 us -> 16.1 us  [the longest x2 15.3 us: shards(): means = lax.all_to_all(send, 'feat', 0, 0).reshape(nf * cols, -1)]
    ppermute x0 -> x7, starting transfers between devices: none -> 8.38 us  [shift_z(): return lax.ppermute(a, 'group', [(i, (i + k) % ng) for i in range(ng)])]
    all_to_all x1, waiting for transfers between devices: 7.82 us -> 0.34 us  [shards(): cot = lax.all_to_all(send, 'feat', 0, 0, axis_index_groups=along_y)]
    all_to_all x1, waiting for transfers between devices: 17.3 us -> 10 us  [shards(): seeds = lax.all_to_all(send, 'feat', 0, 0).reshape(nf * cols, part)]
  transfers between devices with their start and end apart: 8 -> 17, of which waited for: 6 -> 12; matrix products, arithmetic and copies ran while one was open for 5% -> 4% of each run, Pallas kernels for 0% -> 4%
where the time goes in v3:
time: 168 us; the launch traced here: 167 us
  waiting for transfers between devices  57.1 us (34%)
  starting transfers between devices  50.1 us (30%)
  Pallas kernels  19.3 us (11%)
  blocking collectives  16.3 us (10%)
  between operations  14.4 us (9%)
  local copies, waits for them, and re-layouts  8.43 us (5%)
    ppermute x7, waiting for transfers between devices, shift_z(): return lax.ppermute(a, 'group', [(i, (i + k) % ng) for i in range(ng)])  16.7 us
    all_to_all x1, blocking collectives, shards(): got = lax.all_to_all(both, 'feat', 0, 0).astype(F32)  16.3 us
    all_to_all x2, waiting for transfers between devices, shards(): means = lax.all_to_all(send, 'feat', 0, 0).reshape(nf * cols, -1)  15.3 us
    all_to_all x2, starting transfers between devices, shards(): means = lax.all_to_all(send, 'feat', 0, 0).reshape(nf * cols, -1)  11.9 us
    all_to_all x1, waiting for transfers between devices, shards(): seeds = lax.all_to_all(send, 'feat', 0, 0).reshape(nf * cols, part)  10 us
    all_to_all x1, starting transfers between devices, shards(): lax.all_to_all(deg, 'group', 0, 0)  8.71 us
    ppermute x7, starting transfers between devices, shift_z(): return lax.ppermute(a, 'group', [(i, (i + k) % ng) for i in range(ng)])  8.38 us
    pallas_call x2, Pallas kernels, layer(): pl.pallas_call(lambda *refs: layer_kernel(lo, last, *refs), in_specs=[HBM...  8.21 us
  transfers between devices with their start and end apart: 17, of which 12 were waited for; matrix products, arithmetic and copies ran while one was open for 4% of the time, Pallas kernels for 4%

profile of v3, /device:TPU:32, one launch (start us, length us, event | category | flops | bytes accessed | tf_op | source)
XLA Modules:
  0.0 167.3 jit_solution(14218168021780617675)
XLA Ops:
  7.2 0.0 reduce-scatter.2.cloned.1.call-start
  7.2 7.1 %tile_sums.1 = (f32[8,48,3584]{2,1,0:T(8,128)}, f32[48,512]{1,0:T(8,128)}, f32[48,512]{1,0:T(8,128)}, f32[48,512]{1,0:T(8,128)}, f32[48,512]{1,0:T(8,128)}, /*in...) custom-call(s32[1]{0:T(128)} %bitcast.1.me, s32[96]{0:T(128)} %dst_h.1, ...), custom_call_target="tpu_custom_call" | custom-call | tf_op jit(solution)/shard_map/tile_sums/pallas_call | solution.py:96
  14.4 0.0 copy-start.15
  14.4 0.0 copy-start.7
  14.4 0.0 reduce-scatter.2.cloned.1.call-update
  14.4 8.7 %all-to-all-start = ((f32[8,8,512]{2,1,0:T(8,128)}), f32[8,8,512]{2,1,0:T(8,128)S(1)}, u32[]{:S(2)}, u32[]{:S(2)}) async-start(f32[8,8,512]{2,1,0:T(8,128)} %get-tuple-element.42), calls=%async_computation | async-start | bytes 262144 | tf_op jit(solution)/shard_map/degree/all_to_all | solution.py:283
  23.1 1.5 collective-permute-start
  24.6 0.6 collective-permute-start.1
  25.2 3.8 %collective-permute-done = f32[48,512]{1,0:T(8,128)S(1)} collective-permute-done((f32[48,512]{1,0:T(8,128)S(1)}, f32[48,512]{1,0:T(8,128)S(1)}, u32[]{:S(2)}, u32[]{:S(2)}) %collective-permute-start) | collective-permute-done | bytes 98336 | tf_op jit(solution)/shard_map/hop_1/ppermute | solution.py:257
  28.9 1.3 collective-permute-done.1
  30.2 0.0 copy-done.7
  30.2 0.3 reshape.47
  30.5 0.1 copy.17
  30.6 0.9 all-to-all-done
  31.5 1.4 broadcast_in_dim.14
  32.9 0.0 copy-start.6
  32.9 7.2 %all-to-all-start.1 = ((bf16[16,48,1024]{2,1,0:T(8,128)(2,1)}), bf16[16,48,1024]{2,1,0:T(8,128)(2,1)S(1)}, u32[]{:S(2)}, u32[]{:S(2)}) async-start(bf16[16,48,1024]{2,1,0:T(8,128)(2,1)} %bitcast.6), calls=%async_computation.1 | async-start | bytes 3145728 | tf_op jit(solution)/shard_map/seed_rows/all_to_all | solution.py:288
  40.1 1.5 collective-permute-start.3
  41.7 0.0 copy-start.8
  41.7 0.6 collective-permute-start.2
  42.4 4.8 %collective-permute-done.3 = f32[48,512]{1,0:T(8,128)S(1)} collective-permute-done((f32[48,512]{1,0:T(8,128)S(1)}, f32[48,512]{1,0:T(8,128)S(1)}, u32[]{:S(2)}, u32[]{:S(2)}) %collective-permute-start.3) | collective-permute-done | bytes 98336 | tf_op jit(solution)/shard_map/hop_2/ppermute | solution.py:257
  47.2 1.5 collective-permute-done.2
  48.7 2.5 %collective-permute-start.5 = (f32[48,512]{1,0:T(8,128)S(1)}, f32[48,512]{1,0:T(8,128)S(1)}, u32[]{:S(2)}, u32[]{:S(2)}) collective-permute-start(f32[48,512]{1,0:T(8,128)S(1)} %add.95), channel_id=1, source_target_pairs={{0,14},{2,0},{4,2},{6,4},{8,6},{10,8},{12,10},{14,12},{1,15},{3,1}... | collective-permute-start | bytes 294920 | tf_op jit(solution)/shard_map/hop_3/ppermute | solution.py:257
  51.2 0.1 collective-permute-start.4
  51.3 0.0 copy-done.6
  51.3 0.8 copy.25
  52.2 10.0 %all-to-all-done.1 = bf16[16,48,1024]{2,1,0:T(8,128)(2,1)S(1)} async-done(((bf16[16,48,1024]{2,1,0:T(8,128)(2,1)}), bf16[16,48,1024]{2,1,0:T(8,128)(2,1)S(1)}, u32[]{:S(2)}, u32[]{:S(2)}) %all-to-all-start.1) | async-done | bytes 1572896 | tf_op jit(solution)/shard_map/seed_rows/all_to_all | solution.py:288
  62.2 3.5 %all-to-all-start.3 = ((bf16[4,64,1024]{2,1,0:T(8,128)(2,1)}), bf16[4,64,1024]{2,1,0:T(8,128)(2,1)S(1)}, u32[]{:S(2)}, u32[]{:S(2)}) async-start(bf16[4,64,1024]{2,1,0:T(8,128)(2,1)} %bitcast.35), calls=%async_computation.4 | async-start | bytes 1048576 | tf_op jit(solution)/shard_map/cotangent_rows/all_to_all | solution.py:297
  65.7 0.0 collective-permute-done.5
  65.7 0.0 collective-permute-done.4
  65.7 1.6 collective-permute-start.6
  67.3 5.4 %collective-permute-done.6 = f32[48,512]{1,0:T(8,128)S(1)} collective-permute-done((f32[48,512]{1,0:T(8,128)S(1)}, f32[48,512]{1,0:T(8,128)S(1)}, u32[]{:S(2)}, u32[]{:S(2)}) %collective-permute-start.6) | collective-permute-done | bytes 98336 | tf_op jit(solution)/shard_map/hop_4/ppermute | solution.py:257
  72.7 0.7 add_add_fusion.total_h
  73.4 0.3 all-to-all-done.3
  73.7 1.7 %mean_rows_3584.1 = bf16[16,48,128]{2,1,0:T(8,128)(2,1)} custom-call(f32[48,512]{1,0:T(8,128)} %add_add_fusion.total_h, f32[1,512]{1,0:T(1,128)S(1)} %slice.21.degree_h), custom_call_target="tpu_custom_call" | custom-call | tf_op jit(solution)/shard_map/mean_rows_3584/pallas_call | solution.py:145
  75.4 4.8 %all-to-all-start.4 = ((bf16[16,48,128]{2,1,0:T(8,128)(2,1)}), bf16[16,48,128]{2,1,0:T(8,128)(2,1)S(1)}, u32[]{:S(2)}, u32[]{:S(2)}) async-start(bf16[16,48,128]{2,1,0:T(8,128)(2,1)} %mean_rows_3584.1), calls=%async_computation.5 | async-start | bytes 393216 | tf_op jit(solution)/shard_map/mean_rows_3584/all_to_all | solution.py:314
  80.3 8.0 %reduce-scatter.2.cloned.1.call-done.total_h = f32[48,3584]{1,0:T(8,128)} async-done(((f32[384,3584]{1,0:T(8,128)}), f32[48,3584]{1,0:T(8,128)}) %reduce-scatter.2.cloned.1.call-update) | async-done | bytes 688144 | tf_op jit(solution)/shard_map/neighbour_sum/reduce_scatter | solution.py:269
  88.3 2.2 %mean_rows_0.1 = bf16[16,48,896]{2,1,0:T(8,128)(2,1)} custom-call(f32[48,3584]{1,0:T(8,128)} %reduce-scatter.2.cloned.1.call-done.total_h, f32[1,3584]{1,0:T(1,128)S(1)} %slice.20.degree_h), custom_call_target="tpu_custom_call" | custom-call | tf_op jit(solution)/shard_map/mean_rows_0/pallas_call | solution.py:145
  90.5 0.0 all-to-all-done.4
  90.5 0.0 copy-start.4
  90.5 0.0 copy-done.2
  90.5 7.1 %all-to-all-start.2 = ((bf16[16,48,896]{2,1,0:T(8,128)(2,1)}), bf16[16,48,896]{2,1,0:T(8,128)(2,1)S(1)}, u32[]{:S(2)}, u32[]{:S(2)}) async-start(bf16[16,48,896]{2,1,0:T(8,128)(2,1)} %mean_rows_0.1), calls=%async_computation.3 | async-start | bytes 2752512 | tf_op jit(solution)/shard_map/mean_rows_0/all_to_all | solution.py:314
  97.7 1.2 constant_dynamic-slice_fusion
  98.8 0.9 copy.21
  99.8 0.9 copy.20
  100.7 3.2 %layer_3584.1 = (bf16[256,1024]{1,0:T(8,128)(2,1)}, f32[2,768,256]{2,1,0:T(8,128)}) custom-call(bf16[256,768]{1,0:T(8,128)(2,1)} %bitcast.44, bf16[768,1024]{1,0:T(8,128)(2,1)} %bitcast.36, bf16[256,768]{1,0:T(8,128)(2,1)} %bitcast.42, bf16[768,128]{1,0:T(8,128)(2,1)} %bitcast.48, bf16[256,1024]{1,0:T(8,128)(2,1)} %bitcast.40), custom_call_target="tpu_custom_call" | custom-call | tf_op jit(solution)/shard_map/layer_3584/pallas_call | solution.py:229
  104.0 15.3 %all-to-all-done.2 = bf16[16,48,896]{2,1,0:T(8,128)(2,1)S(1)} async-done(((bf16[16,48,896]{2,1,0:T(8,128)(2,1)}), bf16[16,48,896]{2,1,0:T(8,128)(2,1)S(1)}, u32[]{:S(2)}, u32[]{:S(2)}) %all-to-all-start.2) | async-done | bytes 1376288 | tf_op jit(solution)/shard_map/mean_rows_0/all_to_all | solution.py:314
  119.2 1.1 copy-done.1
  120.3 5.0 %layer_0.1 = (bf16[256,1024]{1,0:T(8,128)(2,1)}, bf16[16,96,256]{2,1,0:T(8,128)(2,1)}) custom-call(bf16[256,768]{1,0:T(8,128)(2,1)} %bitcast.45, bf16[768,1024]{1,0:T(8,128)(2,1)} %bitcast.37, bf16[256,768]{1,0:T(8,128)(2,1)} %bitcast.43, bf16[768,896]{1,0:T(8,128)(2,1)} %bitcast.38, bf16[256,1024]{1,0:T(8,128)(2,1)} %bitcast.41, ...), custom_call_target="tpu_custom_call", output_to_operand_aliasing={{0}: (5, {})} | custom-call | tf_op jit(solution)/shard_map/layer_0/pallas_call | solution.py:229
  125.3 0.0 copy-start.3
  125.3 16.3 %all_to_all.35 = bf16[16,96,256]{2,1,0:T(8,128)(2,1)S(1)} all-to-all(bf16[16,96,256]{2,1,0:T(8,128)(2,1)} %get-tuple-element.60), channel_id=1, replica_groups=mesh['feat'=16,'group'=8,'rep'=2] {'feat'}, dimensions={0} | all-to-all | bytes 1572864 | tf_op jit(solution)/shard_map/grads/all_to_all | solution.py:320
  141.6 0.1 bitcast_reduce_fusion
  141.8 0.7 pad_maximum_fusion
  142.5 7.4 %all-to-all-start.6 = ((bf16[8,96,128]{2,1,0:T(8,128)(2,1)}), bf16[8,96,128]{2,1,0:T(8,128)(2,1)S(1)}, u32[]{:S(2)}, u32[]{:S(2)}) async-start(bf16[8,96,128]{2,1,0:T(8,128)(2,1)} %bitcast.15), calls=%async_computation.7 | async-start | bytes 393216 | tf_op jit(solution)/shard_map/grads/all_to_all | solution.py:325
  150.0 1.0 collective-permute-start.9
  151.0 1.5 collective-permute-start.8
  152.5 0.4 collective-permute-start.7
  152.9 5.2 %all-to-all-done.6 = bf16[8,96,128]{2,1,0:T(8,128)(2,1)S(1)} async-done(((bf16[8,96,128]{2,1,0:T(8,128)(2,1)}), bf16[8,96,128]{2,1,0:T(8,128)(2,1)S(1)}, u32[]{:S(2)}, u32[]{:S(2)}) %all-to-all-start.6) | async-done | bytes 196640 | tf_op jit(solution)/shard_map/grads/all_to_all | solution.py:325
  158.1 0.0 collective-permute-done.9
  158.1 0.0 collective-permute-done.8
  158.1 0.7 collective-permute-done.7
  158.9 0.6 fusion.1
  159.6 0.0 copy-start.5
  159.6 0.8 copy-done.5
  (37 shorter events, 0.4 us)
Async XLA Ops:
  7.2 81.1 %reduce-scatter.2.cloned.1.call-start = ((), (), s32[]{:S(2)}) async-start(), calls=%async_computation.8 | async-start | bytes 6193152 | tf_op jit(solution)/shard_map/neighbour_sum/reduce_scatter | solution.py:269
  14.4 8.8 %copy-start.15 = (f32[48,512]{1,0:T(8,128)S(1)}, f32[48,512]{1,0:T(8,128)}, u32[]{:S(2)}) copy-start(f32[48,512]{1,0:T(8,128)} %get-tuple-element.36) | copy-start | bytes 294916
  14.4 10.2 %copy-start.14 = (f32[48,512]{1,0:T(8,128)S(1)}, f32[48,512]{1,0:T(8,128)}, u32[]{:S(2)}) copy-start(f32[48,512]{1,0:T(8,128)} %get-tuple-element.37) | copy-start | bytes 294916
  14.4 15.8 %copy-start.7 = (bf16[4096,48]{0,1:T(8,128)(2,1)S(1)}, bf16[4096,48]{0,1:T(8,128)(2,1)}, u32[]{:S(2)}) copy-start(bf16[4096,48]{0,1:T(8,128)(2,1)} %param.8) | copy-start | bytes 1179652
  14.4 17.1 %all-to-all-start = ((f32[8,8,512]{2,1,0:T(8,128)}), f32[8,8,512]{2,1,0:T(8,128)S(1)}, u32[]{:S(2)}, u32[]{:S(2)}) async-start(f32[8,8,512]{2,1,0:T(8,128)} %get-tuple-element.42), calls=%async_computation | async-start | bytes 262144 | tf_op jit(solution)/shard_map/degree/all_to_all | solution.py:283
  23.1 5.8 %collective-permute-start = (f32[48,512]{1,0:T(8,128)S(1)}, f32[48,512]{1,0:T(8,128)S(1)}, u32[]{:S(2)}, u32[]{:S(2)}) collective-permute-start(f32[48,512]{1,0:T(8,128)S(1)} %copy-done.15), channel_id=1, source_target_pairs={{0,2},{2,4},{4,6},{6,8},{8,10},{10,12},{12,14},{14,0},{1,3},{3,5},... | collective-permute-start | bytes 294920 | tf_op jit(solution)/shard_map/hop_1/ppermute | solution.py:257
  24.6 5.6 %collective-permute-start.1 = (f32[48,512]{1,0:T(8,128)S(1)}, f32[48,512]{1,0:T(8,128)S(1)}, u32[]{:S(2)}, u32[]{:S(2)}) collective-permute-start(f32[48,512]{1,0:T(8,128)S(1)} %copy-done.14), channel_id=1, source_target_pairs={{0,14},{2,0},{4,2},{6,4},{8,6},{10,8},{12,10},{14,12},{1,15},{3,1}... | collective-permute-start | bytes 294920 | tf_op jit(solution)/shard_map/hop_1/ppermute | solution.py:257
  32.9 7.2 %copy-start.13 = (f32[48,512]{1,0:T(8,128)S(1)}, f32[48,512]{1,0:T(8,128)}, u32[]{:S(2)}) copy-start(f32[48,512]{1,0:T(8,128)} %get-tuple-element.41) | copy-start | bytes 294916
  32.9 8.8 %copy-start.12 = (f32[48,512]{1,0:T(8,128)S(1)}, f32[48,512]{1,0:T(8,128)}, u32[]{:S(2)}) copy-start(f32[48,512]{1,0:T(8,128)} %get-tuple-element.39) | copy-start | bytes 294916
  32.9 15.8 %copy-start.11 = (f32[48,512]{1,0:T(8,128)S(1)}, f32[48,512]{1,0:T(8,128)}, u32[]{:S(2)}) copy-start(f32[48,512]{1,0:T(8,128)} %get-tuple-element.46) | copy-start | bytes 294916
  32.9 18.3 %copy-start.10 = (f32[48,512]{1,0:T(8,128)S(1)}, f32[48,512]{1,0:T(8,128)}, u32[]{:S(2)}) copy-start(f32[48,512]{1,0:T(8,128)} %get-tuple-element.44) | copy-start | bytes 294916
  32.9 18.4 %copy-start.6 = (bf16[4096,64]{0,1:T(8,128)(2,1)S(1)}, bf16[4096,64]{0,1:T(8,128)(2,1)}, u32[]{:S(2)}) copy-start(bf16[4096,64]{0,1:T(8,128)(2,1)} %param.15) | copy-start | bytes 1572868
  32.9 29.3 %all-to-all-start.1 = ((bf16[16,48,1024]{2,1,0:T(8,128)(2,1)}), bf16[16,48,1024]{2,1,0:T(8,128)(2,1)S(1)}, u32[]{:S(2)}, u32[]{:S(2)}) async-start(bf16[16,48,1024]{2,1,0:T(8,128)(2,1)} %bitcast.6), calls=%async_computation.1 | async-start | bytes 3145728 | tf_op jit(solution)/shard_map/seed_rows/all_to_all | solution.py:288
  40.1 7.1 %collective-permute-start.3 = (f32[48,512]{1,0:T(8,128)S(1)}, f32[48,512]{1,0:T(8,128)S(1)}, u32[]{:S(2)}, u32[]{:S(2)}) collective-permute-start(f32[48,512]{1,0:T(8,128)S(1)} %add.93), channel_id=1, source_target_pairs={{0,14},{2,0},{4,2},{6,4},{8,6},{10,8},{12,10},{14,12},{1,15},{3,1}... | collective-permute-start | bytes 294920 | tf_op jit(solution)/shard_map/hop_2/ppermute | solution.py:257
  41.7 24.0 %copy-start.9 = (f32[48,512]{1,0:T(8,128)S(1)}, f32[48,512]{1,0:T(8,128)}, u32[]{:S(2)}) copy-start(f32[48,512]{1,0:T(8,128)} %get-tuple-element.53) | copy-start | bytes 294916
  41.7 31.0 %copy-start.8 = (f32[48,512]{1,0:T(8,128)S(1)}, f32[48,512]{1,0:T(8,128)}, u32[]{:S(2)}) copy-start(f32[48,512]{1,0:T(8,128)} %get-tuple-element.51) | copy-start | bytes 294916
  41.7 7.0 %collective-permute-start.2 = (f32[48,512]{1,0:T(8,128)S(1)}, f32[48,512]{1,0:T(8,128)S(1)}, u32[]{:S(2)}, u32[]{:S(2)}) collective-permute-start(f32[48,512]{1,0:T(8,128)S(1)} %add.92), channel_id=1, source_target_pairs={{0,2},{2,4},{4,6},{6,8},{8,10},{10,12},{12,14},{14,0},{1,3},{3,5},... | collective-permute-start | bytes 294920 | tf_op jit(solution)/shard_map/hop_2/ppermute | solution.py:257
  48.7 17.0 %collective-permute-start.5 = (f32[48,512]{1,0:T(8,128)S(1)}, f32[48,512]{1,0:T(8,128)S(1)}, u32[]{:S(2)}, u32[]{:S(2)}) collective-permute-start(f32[48,512]{1,0:T(8,128)S(1)} %add.95), channel_id=1, source_target_pairs={{0,14},{2,0},{4,2},{6,4},{8,6},{10,8},{12,10},{14,12},{1,15},{3,1}... | collective-permute-start | bytes 294920 | tf_op jit(solution)/shard_map/hop_3/ppermute | solution.py:257
  51.2 14.5 %collective-permute-start.4 = (f32[48,512]{1,0:T(8,128)S(1)}, f32[48,512]{1,0:T(8,128)S(1)}, u32[]{:S(2)}, u32[]{:S(2)}) collective-permute-start(f32[48,512]{1,0:T(8,128)S(1)} %add.94), channel_id=1, source_target_pairs={{0,2},{2,4},{4,6},{6,8},{8,10},{10,12},{12,14},{14,0},{1,3},{3,5},... | collective-permute-start | bytes 294920 | tf_op jit(solution)/shard_map/hop_3/ppermute | solution.py:257
  62.2 28.3 %copy-start = (bf16[16,48,1024]{2,1,0:T(8,128)(2,1)}, bf16[16,48,1024]{2,1,0:T(8,128)(2,1)S(1)}, u32[]{:S(2)}) copy-start(bf16[16,48,1024]{2,1,0:T(8,128)(2,1)S(1)} %all-to-all-done.1) | copy-start | bytes 4718596
  62.2 11.5 %all-to-all-start.3 = ((bf16[4,64,1024]{2,1,0:T(8,128)(2,1)}), bf16[4,64,1024]{2,1,0:T(8,128)(2,1)S(1)}, u32[]{:S(2)}, u32[]{:S(2)}) async-start(bf16[4,64,1024]{2,1,0:T(8,128)(2,1)} %bitcast.35), calls=%async_computation.4 | async-start | bytes 1048576 | tf_op jit(solution)/shard_map/cotangent_rows/all_to_all | solution.py:297
  65.7 7.0 %collective-permute-start.6 = (f32[48,512]{1,0:T(8,128)S(1)}, f32[48,512]{1,0:T(8,128)S(1)}, u32[]{:S(2)}, u32[]{:S(2)}) collective-permute-start(f32[48,512]{1,0:T(8,128)S(1)} %add.96), channel_id=1, source_target_pairs={{0,2},{2,4},{4,6},{6,8},{8,10},{10,12},{12,14},{14,0},{1,3},{3,5},... | collective-permute-start | bytes 294920 | tf_op jit(solution)/shard_map/hop_4/ppermute | solution.py:257
  73.7 16.8 %copy-start.2 = (bf16[4,64,1024]{2,1,0:T(8,128)(2,1)}, bf16[4,64,1024]{2,1,0:T(8,128)(2,1)S(1)}, u32[]{:S(2)}) copy-start(bf16[4,64,1024]{2,1,0:T(8,128)(2,1)S(1)} %all-to-all-done.3) | copy-start | bytes 1572868
  75.4 15.1 %all-to-all-start.4 = ((bf16[16,48,128]{2,1,0:T(8,128)(2,1)}), bf16[16,48,128]{2,1,0:T(8,128)(2,1)S(1)}, u32[]{:S(2)}, u32[]{:S(2)}) async-start(bf16[16,48,128]{2,1,0:T(8,128)(2,1)} %mean_rows_3584.1), calls=%async_computation.5 | async-start | bytes 393216 | tf_op jit(solution)/shard_map/mean_rows_3584/all_to_all | solution.py:314
  90.5 8.3 %copy-start.4 = (bf16[16,48,128]{2,1,0:T(8,128)(2,1)}, bf16[16,48,128]{2,1,0:T(8,128)(2,1)S(1)}, u32[]{:S(2)}) copy-start(bf16[16,48,128]{2,1,0:T(8,128)(2,1)S(1)} %all-to-all-done.4) | copy-start | bytes 589828
  90.5 28.7 %all-to-all-start.2 = ((bf16[16,48,896]{2,1,0:T(8,128)(2,1)}), bf16[16,48,896]{2,1,0:T(8,128)(2,1)S(1)}, u32[]{:S(2)}, u32[]{:S(2)}) async-start(bf16[16,48,896]{2,1,0:T(8,128)(2,1)} %mean_rows_0.1), calls=%async_computation.3 | async-start | bytes 2752512 | tf_op jit(solution)/shard_map/mean_rows_0/all_to_all | solution.py:314
  119.2 1.1 copy-start.1
  125.3 24.6 %copy-start.3 = (bf16[256,1024]{1,0:T(8,128)(2,1)S(1)}, bf16[256,1024]{1,0:T(8,128)(2,1)}, u32[]{:S(2)}) copy-start(bf16[256,1024]{1,0:T(8,128)(2,1)} %get-tuple-element.63) | copy-start | bytes 1572868
  142.5 15.6 %all-to-all-start.6 = ((bf16[8,96,128]{2,1,0:T(8,128)(2,1)}), bf16[8,96,128]{2,1,0:T(8,128)(2,1)S(1)}, u32[]{:S(2)}, u32[]{:S(2)}) async-start(bf16[8,96,128]{2,1,0:T(8,128)(2,1)} %bitcast.15), calls=%async_computation.7 | async-start | bytes 393216 | tf_op jit(solution)/shard_map/grads/all_to_all | solution.py:325
  150.0 8.2 %collective-permute-start.9 = (bf16[64,1024]{1,0:T(8,128)(2,1)S(1)}, bf16[64,1024]{1,0:T(8,128)(2,1)S(1)}, u32[]{:S(2)}, u32[]{:S(2)}) collective-permute-start(bf16[64,1024]{1,0:T(8,128)(2,1)S(1)} %get-tuple-element.69), channel_id=1, source_target_pairs={{0,48},{16,0},{32,16},{48,32},{64,112},{80,64},{96,80},{112,96},{1... | collective-permute-start | bytes 393224 | tf_op jit(solution)/shard_map/hidden_columns/ppermute | solution.py:252
  151.0 7.2 %collective-permute-start.8 = (bf16[64,1024]{1,0:T(8,128)(2,1)S(1)}, bf16[64,1024]{1,0:T(8,128)(2,1)S(1)}, u32[]{:S(2)}, u32[]{:S(2)}) collective-permute-start(bf16[64,1024]{1,0:T(8,128)(2,1)S(1)} %get-tuple-element.70), channel_id=1, source_target_pairs={{0,32},{16,48},{32,0},{48,16},{64,96},{80,112},{96,64},{112,80},{1... | collective-permute-start | bytes 393224 | tf_op jit(solution)/shard_map/hidden_columns/ppermute | solution.py:252
  152.5 6.4 %collective-permute-start.7 = (bf16[64,1024]{1,0:T(8,128)(2,1)S(1)}, bf16[64,1024]{1,0:T(8,128)(2,1)S(1)}, u32[]{:S(2)}, u32[]{:S(2)}) collective-permute-start(bf16[64,1024]{1,0:T(8,128)(2,1)S(1)} %get-tuple-element.71), channel_id=1, source_target_pairs={{0,16},{16,32},{32,48},{48,0},{64,80},{80,96},{96,112},{112,64},{1... | collective-permute-start | bytes 393224 | tf_op jit(solution)/shard_map/hidden_columns/ppermute | solution.py:252
  159.6 0.8 copy-start.5
Sparse Core Ops, SparseCore 0:
  14.5 73.6 reduce-scatter.1

commit v4 on v3

--- a/solution.py
+++ b/solution.py
@@ -157,84 +157,111 @@
     )(*far(total), degree)
 
 
-def layer_kernel(lo, last, *refs):
-    nin = 7 if last else 5
-    given, (hid_h, grad_h) = refs[:nin], refs[nin : nin + 2]
-    ws, seeds, wn, means, cot, hid, grad, *rest = refs[nin + 2 :]
-    sems = rest[-1]
-    width = means.shape[1]
-    lanes = (slice(None), pl.ds(lo, width))
-    pairs = [
-        (given[0], ws),
-        (given[1].at[lanes], seeds),
-        (given[2], wn),
-        (given[3], means),
-        (given[4].at[lanes], cot),
-    ]
-    if last:
-        pairs.append((given[6], rest[0]))
+def late_kernel(ws_h, seeds_h, wn_h, means_h, hid_h, pre_h, ws, seeds, wn, means, hid, pre, sems):
+    early = pre.shape[1]
+    pairs = ((ws_h, ws), (seeds_h, seeds), (wn_h, wn), (means_h, means))
     loads = [pltpu.make_async_copy(p, q, sems.at[i]) for i, (p, q) in enumerate(pairs)]
     for load in loads:
         load.start()
-    for load in loads[:2]:
+    for load in loads:
         load.wait()
     total = jnp.dot(ws[...], seeds[...], preferred_element_type=F32)
-    for load in loads[2:4]:
+    pre[...] = total[:, :early]
+    total = total[:, early:] + jnp.dot(wn[...], means[...], preferred_element_type=F32)
+    hid[...] = jnp.maximum(total, 0.0).astype(BF16)
+    lanes = (slice(None), pl.ds(early, hid.shape[1]))
+    stores = [
+        pltpu.make_async_copy(hid, hid_h.at[lanes], sems.at[4]),
+        pltpu.make_async_copy(pre, pre_h, sems.at[5]),
+    ]
+    for store in stores:
+        store.start()
+    for store in stores:
+        store.wait()
+
+
+def late_rows(ws_t, seeds, wn_t, means):
+    hcols, _ = ws_t.shape
+    rows, late = seeds.shape[1], means.shape[1]
+    return pl.pallas_call(
+        late_kernel,
+        in_specs=[HBM] * 3 + [pl.BlockSpec(memory_space=pl.ANY)],
+        out_specs=[HBM] * 2,
+        out_shape=[pltpu.HBM((hcols, rows), BF16), pltpu.HBM((hcols, rows - late), F32)],
+        scratch_shapes=[pltpu.VMEM(a.shape, BF16) for a in (ws_t, seeds, wn_t, means)]
+        + [
+            pltpu.VMEM((hcols, late), BF16),
+            pltpu.VMEM((hcols, rows - late), F32),
+            pltpu.SemaphoreType.DMA((6,)),
+        ],
+        compiler_params=pltpu.CompilerParams(vmem_limit_bytes=32 * 1024 * 1024),
+    )(*far(ws_t, seeds, wn_t), means)
+
+
+def layer_kernel(wn_h, means_h, pre_h, cot_h, late_h, before_h, seeds_h, hid_h, grad_h, *refs):
+    wn, means, pre, cot, seeds, hid, grad, sems = refs
+    early, rows = pre.shape[1], cot.shape[1]
+    first = (slice(None), pl.ds(0, early))
+    rest = (slice(None), pl.ds(early, rows - early))
+    pairs = (
+        (wn_h, wn),
+        (means_h, means.at[first]),
+        (pre_h, pre),
+        (cot_h, cot),
+        (before_h.at[rest], hid.at[rest]),
+        (seeds_h, seeds),
+        (late_h, means.at[rest]),
+    )
+    loads = [pltpu.make_async_copy(p, q, sems.at[i]) for i, (p, q) in enumerate(pairs)]
+    for load in loads:
+        load.start()
+    for load in loads[:3]:
         load.wait()
-    total += jnp.dot(wn[...], means[...], preferred_element_type=F32)
-    h = jnp.maximum(total, 0.0).astype(BF16)
-    hid[...] = h
-    stores = [pltpu.make_async_copy(hid, hid_h.at[lanes], sems.at[6])]
+    total = pre[...] + jnp.dot(wn[...], means[first], preferred_element_type=F32)
+    hid[first] = jnp.maximum(total, 0.0).astype(BF16)
+    stores = [pltpu.make_async_copy(hid.at[first], hid_h.at[first], sems.at[7])]
     stores[0].start()
-    for load in loads[4:]:
+    for load in loads[3:]:
         load.wait()
-    dpre = jnp.where(h > 0, cot[...], jnp.zeros_like(h))
+    dpre = jnp.where(hid[...] > 0, cot[...], jnp.zeros_like(cot))
     dims = (((1,), (1,)), ((), ()))
+    nf, cols = grad.shape[0], grad.shape[1] // 2
     for j, x in enumerate((seeds, means)):
-        g = lax.dot_general(x[...], dpre, dims, preferred_element_type=F32)
-        if last:
-            g = (g + rest[0][j]).astype(BF16)
-            cols = grad.shape[1] // 2
-            at = j * cols
-            for i in range(grad.shape[0]):
-                grad[i, at : at + cols, :] = g[i * cols : (i + 1) * cols]
-            where = (slice(None), pl.ds(at, cols), slice(None))
-        else:
-            grad[j] = g
-            where = j
-        store = pltpu.make_async_copy(grad.at[where], grad_h.at[where], sems.at[7 + j])
+        at = j * cols
+        g = lax.dot_general(x[...], dpre, dims, preferred_element_type=F32).astype(BF16)
+        for i in range(nf):
+            grad[i, at : at + cols, :] = g[i * cols : (i + 1) * cols]
+        where = (slice(None), pl.ds(at, cols), slice(None))
+        store = pltpu.make_async_copy(grad.at[where], grad_h.at[where], sems.at[8 + j])
         store.start()
         stores.append(store)
     for store in stores:
         store.wait()
 
 
-def layer(ws_t, seeds, wn_t, means, cot, lo, before, nf):
+def layer(wn_t, means, pre, cot, late, before, seeds, nf):
     hcols, rows = cot.shape
-    depth, width = means.shape
-    last = before is not None
-    args = (ws_t, seeds, wn_t, means, cot) + (before if last else ())
-    grad = ((nf, 2 * depth // nf, hcols), BF16) if last else ((2, depth, hcols), F32)
-    near = [
-        ((hcols, depth), BF16),
-        ((depth, width), BF16),
-        ((hcols, depth), BF16),
-        ((depth, width), BF16),
-        ((hcols, width), BF16),
-        ((hcols, width), BF16),
-        grad,
-    ]
-    if last:
-        near.append(((2, depth, hcols), F32))
+    depth, early = means.shape
+    grad = (nf, 2 * depth // nf, hcols)
+    anywhere = pl.BlockSpec(memory_space=pl.ANY)
     return pl.pallas_call(
-        lambda *refs: layer_kernel(lo, last, *refs),
-        in_specs=[HBM] * len(args),
+        layer_kernel,
+        in_specs=[HBM, anywhere] + [HBM] * 2 + [anywhere] + [HBM] * 2,
         out_specs=[HBM] * 2,
-        out_shape=[pltpu.HBM((hcols, rows), BF16), pltpu.HBM(*grad)],
-        scratch_shapes=[pltpu.VMEM(*n) for n in near] + [pltpu.SemaphoreType.DMA((9,))],
-        input_output_aliases={5: 0} if last else {},
+        out_shape=[pltpu.HBM((hcols, rows), BF16), pltpu.HBM(grad, BF16)],
+        scratch_shapes=[
+            pltpu.VMEM((hcols, depth), BF16),
+            pltpu.VMEM((depth, rows), BF16),
+            pltpu.VMEM((hcols, early), F32),
+            pltpu.VMEM((hcols, rows), BF16),
+            pltpu.VMEM((depth, rows), BF16),
+            pltpu.VMEM((hcols, rows), BF16),
+            pltpu.VMEM(grad, BF16),
+            pltpu.SemaphoreType.DMA((10,)),
+        ],
+        input_output_aliases={5: 0},
         compiler_params=pltpu.CompilerParams(vmem_limit_bytes=40 * 1024 * 1024),
-    )(*far(*args))
+    )(*far(wn_t), means, *far(pre, cot), late, *far(before, seeds))
 
 
 def shards(seed_feats, src_feats, counts, dst_block, src_block, w_self, w_neigh, cotangent):
@@ -307,14 +334,15 @@
         total2, cot = meet(late[0] + up + down, cot)
 
     early = total.shape[1]
-    before = None
+    means = []
     for x, lo, hi in ((total2, early, seeds_here), (total, 0, early)):
         with jax.named_scope("mean_rows_%d" % lo):
             send = mean_rows(x, degree[:, lo:hi])
-            means = lax.all_to_all(send, "feat", 0, 0).reshape(nf * cols, -1)
-        with jax.named_scope("layer_%d" % lo):
-            before = layer(ws_t, seeds, wn_t, means, cot, lo // SIDE, before, nf)
-    hid, both = before
+            means.append(lax.all_to_all(send, "feat", 0, 0).reshape(nf * cols, -1))
+
+    with jax.named_scope("layer"):
+        hid, pre = late_rows(ws_t, seeds, wn_t, means[0])
+        hid, both = layer(wn_t, means[1], pre, cot, means[0], hid, seeds, nf)
 
     with jax.named_scope("grads"):
         got = lax.all_to_all(both, "feat", 0, 0).astype(F32)

time: 168 us -> 166 us (0.988)
    unnamed x35 -> x31, local copies, waits for them, and re-layouts: 3.84 us -> 2.74 us
where the time goes in v4:
time: 166 us; the launch traced here: 165 us
  waiting for transfers between devices  55.9 us (34%)
  starting transfers between devices  50.7 us (31%)
  Pallas kernels  18.5 us (11%)
  blocking collectives  16.4 us (10%)
  between operations  14.4 us (9%)
  local copies, waits for them, and re-layouts  7.32 us (4%)
    ppermute x7, waiting for transfers between devices, shift_z(): return lax.ppermute(a, 'group', [(i, (i + k) % ng) for i in range(ng)])  17.1 us
    all_to_all x1, blocking collectives, shards(): got = lax.all_to_all(both, 'feat', 0, 0).astype(F32)  16.4 us
    all_to_all x2, waiting for transfers between devices, shards(): means.append(lax.all_to_all(send, 'feat', 0, 0).reshape(nf * cols, -1))  15.2 us
    all_to_all x2, starting transfers between devices, shards(): means.append(lax.all_to_all(send, 'feat', 0, 0).reshape(nf * cols, -1))  11.9 us
    all_to_all x1, waiting for transfers between devices, shards(): seeds = lax.all_to_all(send, 'feat', 0, 0).reshape(nf * cols, part)  10.1 us
    all_to_all x1, starting transfers between devices, shards(): lax.all_to_all(deg, 'group', 0, 0)  8.71 us
    ppermute x7, starting transfers between devices, shift_z(): return lax.ppermute(a, 'group', [(i, (i + k) % ng) for i in range(ng)])  7.99 us
    reduce_scatter x1, waiting for transfers between devices, shards(): lax.psum_scatter(sums.reshape(ng * cols, -1), 'group', scatter_dimension=...  7.98 us
  transfers between devices with their start and end apart: 17, of which 12 were waited for; matrix products, arithmetic and copies ran while one was open for 4% of the time, Pallas kernels for 4%

profile of v4, /device:TPU:32, one launch (start us, length us, event | category | flops | bytes accessed | tf_op | source)
XLA Modules:
  0.0 164.8 jit_solution(5353603291118319755)
XLA Ops:
  7.2 0.0 reduce-scatter.2.cloned.1.call-start
  7.2 7.1 %tile_sums.1 = (f32[8,48,3584]{2,1,0:T(8,128)}, f32[48,512]{1,0:T(8,128)}, f32[48,512]{1,0:T(8,128)}, f32[48,512]{1,0:T(8,128)}, f32[48,512]{1,0:T(8,128)}, /*in...) custom-call(s32[1]{0:T(128)} %bitcast.1.me, s32[96]{0:T(128)} %dst_h.1, ...), custom_call_target="tpu_custom_call" | custom-call | tf_op jit(solution)/shard_map/tile_sums/pallas_call | solution.py:96
  14.4 0.0 copy-start.13
  14.4 0.0 copy-start.12
  14.4 0.0 copy-start.5
  14.4 0.0 reduce-scatter.2.cloned.1.call-update
  14.4 8.7 %all-to-all-start = ((f32[8,8,512]{2,1,0:T(8,128)}), f32[8,8,512]{2,1,0:T(8,128)S(1)}, u32[]{:S(2)}, u32[]{:S(2)}) async-start(f32[8,8,512]{2,1,0:T(8,128)} %get-tuple-element.43), calls=%async_computation.1 | async-start | bytes 262144 | tf_op jit(solution)/shard_map/degree/all_to_all | solution.py:310
  23.1 0.0 copy-done.13
  23.1 1.5 collective-permute-start
  24.6 0.0 copy-done.12
  24.6 0.6 collective-permute-start.1
  25.2 3.8 %collective-permute-done = f32[48,512]{1,0:T(8,128)S(1)} collective-permute-done((f32[48,512]{1,0:T(8,128)S(1)}, f32[48,512]{1,0:T(8,128)S(1)}, u32[]{:S(2)}, u32[]{:S(2)}) %collective-permute-start) | collective-permute-done | bytes 98336 | tf_op jit(solution)/shard_map/hop_1/ppermute | solution.py:284
  28.9 1.3 collective-permute-done.1
  30.2 0.0 copy-done.5
  30.2 0.3 reshape.49
  30.5 0.1 copy.18
  30.6 0.9 all-to-all-done
  31.5 1.4 broadcast_in_dim.14
  32.9 0.0 copy-start.4
  32.9 7.2 %all-to-all-start.2 = ((bf16[16,48,1024]{2,1,0:T(8,128)(2,1)}), bf16[16,48,1024]{2,1,0:T(8,128)(2,1)S(1)}, u32[]{:S(2)}, u32[]{:S(2)}) async-start(bf16[16,48,1024]{2,1,0:T(8,128)(2,1)} %bitcast.9), calls=%async_computation.3 | async-start | bytes 3145728 | tf_op jit(solution)/shard_map/seed_rows/all_to_all | solution.py:315
  40.1 0.0 copy-done.11
  40.1 1.7 %collective-permute-start.2 = (f32[48,512]{1,0:T(8,128)S(1)}, f32[48,512]{1,0:T(8,128)S(1)}, u32[]{:S(2)}, u32[]{:S(2)}) collective-permute-start(f32[48,512]{1,0:T(8,128)S(1)} %add.92), channel_id=1, source_target_pairs={{0,2},{2,4},{4,6},{6,8},{8,10},{10,12},{12,14},{14,0},{1,3},{3,5},... | collective-permute-start | bytes 294920 | tf_op jit(solution)/shard_map/hop_2/ppermute | solution.py:284
  41.8 0.5 collective-permute-start.3
  42.4 4.8 %collective-permute-done.2 = f32[48,512]{1,0:T(8,128)S(1)} collective-permute-done((f32[48,512]{1,0:T(8,128)S(1)}, f32[48,512]{1,0:T(8,128)S(1)}, u32[]{:S(2)}, u32[]{:S(2)}) %collective-permute-start.2) | collective-permute-done | bytes 98336 | tf_op jit(solution)/shard_map/hop_2/ppermute | solution.py:284
  47.2 1.8 %collective-permute-done.3 = f32[48,512]{1,0:T(8,128)S(1)} collective-permute-done((f32[48,512]{1,0:T(8,128)S(1)}, f32[48,512]{1,0:T(8,128)S(1)}, u32[]{:S(2)}, u32[]{:S(2)}) %collective-permute-start.3) | collective-permute-done | bytes 98336 | tf_op jit(solution)/shard_map/hop_2/ppermute | solution.py:284
  49.0 2.1 %collective-permute-start.4 = (f32[48,512]{1,0:T(8,128)S(1)}, f32[48,512]{1,0:T(8,128)S(1)}, u32[]{:S(2)}, u32[]{:S(2)}) collective-permute-start(f32[48,512]{1,0:T(8,128)S(1)} %add.94), channel_id=1, source_target_pairs={{0,2},{2,4},{4,6},{6,8},{8,10},{10,12},{12,14},{14,0},{1,3},{3,5},... | collective-permute-start | bytes 294920 | tf_op jit(solution)/shard_map/hop_3/ppermute | solution.py:284
  51.2 0.1 collective-permute-start.5
  51.3 0.8 copy.25
  52.1 10.1 %all-to-all-done.2 = bf16[16,48,1024]{2,1,0:T(8,128)(2,1)S(1)} async-done(((bf16[16,48,1024]{2,1,0:T(8,128)(2,1)}), bf16[16,48,1024]{2,1,0:T(8,128)(2,1)S(1)}, u32[]{:S(2)}, u32[]{:S(2)}) %all-to-all-start.2) | async-done | bytes 1572896 | tf_op jit(solution)/shard_map/seed_rows/all_to_all | solution.py:315
  62.2 3.5 %all-to-all-start.3 = ((bf16[4,64,1024]{2,1,0:T(8,128)(2,1)}), bf16[4,64,1024]{2,1,0:T(8,128)(2,1)S(1)}, u32[]{:S(2)}, u32[]{:S(2)}) async-start(bf16[4,64,1024]{2,1,0:T(8,128)(2,1)} %bitcast.35), calls=%async_computation.4 | async-start | bytes 1048576 | tf_op jit(solution)/shard_map/cotangent_rows/all_to_all | solution.py:324
  65.7 0.0 collective-permute-done.4
  65.7 0.0 collective-permute-done.5
  65.7 1.6 collective-permute-start.6
  67.3 5.4 %collective-permute-done.6 = f32[48,512]{1,0:T(8,128)S(1)} collective-permute-done((f32[48,512]{1,0:T(8,128)S(1)}, f32[48,512]{1,0:T(8,128)S(1)}, u32[]{:S(2)}, u32[]{:S(2)}) %collective-permute-start.6) | collective-permute-done | bytes 98336 | tf_op jit(solution)/shard_map/hop_4/ppermute | solution.py:284
  72.7 0.7 add_add_fusion.total_h
  73.4 0.4 all-to-all-done.3
  73.7 1.7 %mean_rows_3584.1 = bf16[16,48,128]{2,1,0:T(8,128)(2,1)} custom-call(f32[48,512]{1,0:T(8,128)} %add_add_fusion.total_h, f32[1,512]{1,0:T(1,128)S(1)} %slice.21.degree_h), custom_call_target="tpu_custom_call" | custom-call | tf_op jit(solution)/shard_map/mean_rows_3584/pallas_call | solution.py:145
  75.4 4.8 %all-to-all-start.4 = ((bf16[16,48,128]{2,1,0:T(8,128)(2,1)}), bf16[16,48,128]{2,1,0:T(8,128)(2,1)S(1)}, u32[]{:S(2)}, u32[]{:S(2)}) async-start(bf16[16,48,128]{2,1,0:T(8,128)(2,1)} %mean_rows_3584.1), calls=%async_computation.5 | async-start | bytes 393216 | tf_op jit(solution)/shard_map/mean_rows_3584/all_to_all | solution.py:341
  80.3 8.0 %reduce-scatter.2.cloned.1.call-done.total_h = f32[48,3584]{1,0:T(8,128)} async-done(((f32[384,3584]{1,0:T(8,128)}), f32[48,3584]{1,0:T(8,128)}) %reduce-scatter.2.cloned.1.call-update) | async-done | bytes 688144 | tf_op jit(solution)/shard_map/neighbour_sum/reduce_scatter | solution.py:296
  88.3 2.2 %mean_rows_0.1 = bf16[16,48,896]{2,1,0:T(8,128)(2,1)} custom-call(f32[48,3584]{1,0:T(8,128)} %reduce-scatter.2.cloned.1.call-done.total_h, f32[1,3584]{1,0:T(1,128)S(1)} %slice.20.degree_h), custom_call_target="tpu_custom_call" | custom-call | tf_op jit(solution)/shard_map/mean_rows_0/pallas_call | solution.py:145
  90.5 0.0 all-to-all-done.4
  90.5 0.0 copy-done.1
  90.5 7.0 %all-to-all-start.1 = ((bf16[16,48,896]{2,1,0:T(8,128)(2,1)}), bf16[16,48,896]{2,1,0:T(8,128)(2,1)S(1)}, u32[]{:S(2)}, u32[]{:S(2)}) async-start(bf16[16,48,896]{2,1,0:T(8,128)(2,1)} %mean_rows_0.1), calls=%async_computation.2 | async-start | bytes 2752512 | tf_op jit(solution)/shard_map/mean_rows_0/all_to_all | solution.py:341
  97.6 1.2 constant_dynamic-slice_fusion
  98.8 0.9 copy.20
  99.7 0.9 copy.21
  100.7 3.3 %layer.2 = (bf16[256,1024]{1,0:T(8,128)(2,1)}, f32[256,896]{1,0:T(8,128)}) custom-call(bf16[256,768]{1,0:T(8,128)(2,1)} %bitcast.46, bf16[768,1024]{1,0:T(8,128)(2,1)} %bitcast.39, bf16[256,768]{1,0:T(8,128)(2,1)} %bitcast.42, bf16[768,128]{1,0:T(8,128)(2,1)S(1)} %bitcast.37), custom_call_target="tpu_custom_call" | custom-call | tf_op jit(solution)/shard_map/layer/pallas_call | solution.py:186
  103.9 15.2 %all-to-all-done.1 = bf16[16,48,896]{2,1,0:T(8,128)(2,1)S(1)} async-done(((bf16[16,48,896]{2,1,0:T(8,128)(2,1)}), bf16[16,48,896]{2,1,0:T(8,128)(2,1)S(1)}, u32[]{:S(2)}, u32[]{:S(2)}) %all-to-all-start.1) | async-done | bytes 1376288 | tf_op jit(solution)/shard_map/mean_rows_0/all_to_all | solution.py:341
  119.2 4.1 %layer.3 = (bf16[256,1024]{1,0:T(8,128)(2,1)}, bf16[16,96,256]{2,1,0:T(8,128)(2,1)}) custom-call(bf16[256,768]{1,0:T(8,128)(2,1)} %bitcast.43, bf16[768,896]{1,0:T(8,128)(2,1)S(1)} %bitcast.36, f32[256,896]{1,0:T(8,128)} %get-tuple-element.57.pre_h, bf16[256,1024]{1,0:T(8,128)(2,1)} %bitcast.44, ...), custom_call_target="tpu_custom_call", output_to_operand_aliasing={{0}: (5, {})} | custom-call | tf_op jit(solution)/shard_map/layer/pallas_call | solution.py:247
  123.3 0.0 copy-start.2
  123.3 16.4 %all_to_all.35 = bf16[16,96,256]{2,1,0:T(8,128)(2,1)S(1)} all-to-all(bf16[16,96,256]{2,1,0:T(8,128)(2,1)} %get-tuple-element.60), channel_id=1, replica_groups=mesh['feat'=16,'group'=8,'rep'=2] {'feat'}, dimensions={0} | all-to-all | bytes 1572864 | tf_op jit(solution)/shard_map/grads/all_to_all | solution.py:348
  139.7 0.1 bitcast_reduce_fusion
  139.8 0.7 pad_maximum_fusion
  140.5 7.3 %all-to-all-start.6 = ((bf16[8,96,128]{2,1,0:T(8,128)(2,1)}), bf16[8,96,128]{2,1,0:T(8,128)(2,1)S(1)}, u32[]{:S(2)}, u32[]{:S(2)}) async-start(bf16[8,96,128]{2,1,0:T(8,128)(2,1)} %bitcast.15), calls=%async_computation.7 | async-start | bytes 393216 | tf_op jit(solution)/shard_map/grads/all_to_all | solution.py:353
  147.8 0.5 collective-permute-start.7
  148.3 2.0 %collective-permute-start.8 = (bf16[64,1024]{1,0:T(8,128)(2,1)S(1)}, bf16[64,1024]{1,0:T(8,128)(2,1)S(1)}, u32[]{:S(2)}, u32[]{:S(2)}) collective-permute-start(bf16[64,1024]{1,0:T(8,128)(2,1)S(1)} %get-tuple-element.70), channel_id=1, source_target_pairs={{0,32},{16,48},{32,0},{48,16},{64,96},{80,112},{96,64},{112,80},{1... | collective-permute-start | bytes 393224 | tf_op jit(solution)/shard_map/hidden_columns/ppermute | solution.py:279
  150.3 1.7 %collective-permute-start.9 = (bf16[64,1024]{1,0:T(8,128)(2,1)S(1)}, bf16[64,1024]{1,0:T(8,128)(2,1)S(1)}, u32[]{:S(2)}, u32[]{:S(2)}) collective-permute-start(bf16[64,1024]{1,0:T(8,128)(2,1)S(1)} %get-tuple-element.69), channel_id=1, source_target_pairs={{0,48},{16,0},{32,16},{48,32},{64,112},{80,64},{96,80},{112,96},{1... | collective-permute-start | bytes 393224 | tf_op jit(solution)/shard_map/hidden_columns/ppermute | solution.py:279
  152.0 4.1 %all-to-all-done.6 = bf16[8,96,128]{2,1,0:T(8,128)(2,1)S(1)} async-done(((bf16[8,96,128]{2,1,0:T(8,128)(2,1)}), bf16[8,96,128]{2,1,0:T(8,128)(2,1)S(1)}, u32[]{:S(2)}, u32[]{:S(2)}) %all-to-all-start.6) | async-done | bytes 196640 | tf_op jit(solution)/shard_map/grads/all_to_all | solution.py:353
  156.1 0.0 collective-permute-done.7
  156.2 0.0 collective-permute-done.8
  156.2 0.2 collective-permute-done.9
  156.4 0.6 fusion.1
  157.1 0.0 copy-start.3
  157.1 0.8 copy-done.3
  (33 shorter events, 0.3 us)
Async XLA Ops:
  7.2 81.1 %reduce-scatter.2.cloned.1.call-start = ((), (), s32[]{:S(2)}) async-start(), calls=%async_computation.8 | async-start | bytes 6193152 | tf_op jit(solution)/shard_map/neighbour_sum/reduce_scatter | solution.py:296
  14.4 8.8 %copy-start.13 = (f32[48,512]{1,0:T(8,128)S(1)}, f32[48,512]{1,0:T(8,128)}, u32[]{:S(2)}) copy-start(f32[48,512]{1,0:T(8,128)} %get-tuple-element.37) | copy-start | bytes 294916
  14.4 10.2 %copy-start.12 = (f32[48,512]{1,0:T(8,128)S(1)}, f32[48,512]{1,0:T(8,128)}, u32[]{:S(2)}) copy-start(f32[48,512]{1,0:T(8,128)} %get-tuple-element.38) | copy-start | bytes 294916
  14.4 15.8 %copy-start.5 = (bf16[4096,48]{0,1:T(8,128)(2,1)S(1)}, bf16[4096,48]{0,1:T(8,128)(2,1)}, u32[]{:S(2)}) copy-start(bf16[4096,48]{0,1:T(8,128)(2,1)} %param.8) | copy-start | bytes 1179652
  14.4 17.1 %all-to-all-start = ((f32[8,8,512]{2,1,0:T(8,128)}), f32[8,8,512]{2,1,0:T(8,128)S(1)}, u32[]{:S(2)}, u32[]{:S(2)}) async-start(f32[8,8,512]{2,1,0:T(8,128)} %get-tuple-element.43), calls=%async_computation.1 | async-start | bytes 262144 | tf_op jit(solution)/shard_map/degree/all_to_all | solution.py:310
  23.1 5.8 %collective-permute-start = (f32[48,512]{1,0:T(8,128)S(1)}, f32[48,512]{1,0:T(8,128)S(1)}, u32[]{:S(2)}, u32[]{:S(2)}) collective-permute-start(f32[48,512]{1,0:T(8,128)S(1)} %copy-done.13), channel_id=1, source_target_pairs={{0,2},{2,4},{4,6},{6,8},{8,10},{10,12},{12,14},{14,0},{1,3},{3,5},... | collective-permute-start | bytes 294920 | tf_op jit(solution)/shard_map/hop_1/ppermute | solution.py:284
  24.6 5.6 %collective-permute-start.1 = (f32[48,512]{1,0:T(8,128)S(1)}, f32[48,512]{1,0:T(8,128)S(1)}, u32[]{:S(2)}, u32[]{:S(2)}) collective-permute-start(f32[48,512]{1,0:T(8,128)S(1)} %copy-done.12), channel_id=1, source_target_pairs={{0,14},{2,0},{4,2},{6,4},{8,6},{10,8},{12,10},{14,12},{1,15},{3,1}... | collective-permute-start | bytes 294920 | tf_op jit(solution)/shard_map/hop_1/ppermute | solution.py:284
  32.9 7.2 %copy-start.11 = (f32[48,512]{1,0:T(8,128)S(1)}, f32[48,512]{1,0:T(8,128)}, u32[]{:S(2)}) copy-start(f32[48,512]{1,0:T(8,128)} %get-tuple-element.40) | copy-start | bytes 294916
  32.9 8.9 %copy-start.10 = (f32[48,512]{1,0:T(8,128)S(1)}, f32[48,512]{1,0:T(8,128)}, u32[]{:S(2)}) copy-start(f32[48,512]{1,0:T(8,128)} %get-tuple-element.42) | copy-start | bytes 294916
  32.9 16.1 %copy-start.9 = (f32[48,512]{1,0:T(8,128)S(1)}, f32[48,512]{1,0:T(8,128)}, u32[]{:S(2)}) copy-start(f32[48,512]{1,0:T(8,128)} %get-tuple-element.46) | copy-start | bytes 294916
  32.9 18.3 %copy-start.8 = (f32[48,512]{1,0:T(8,128)S(1)}, f32[48,512]{1,0:T(8,128)}, u32[]{:S(2)}) copy-start(f32[48,512]{1,0:T(8,128)} %get-tuple-element.48) | copy-start | bytes 294916
  32.9 18.4 %copy-start.4 = (bf16[4096,64]{0,1:T(8,128)(2,1)S(1)}, bf16[4096,64]{0,1:T(8,128)(2,1)}, u32[]{:S(2)}) copy-start(bf16[4096,64]{0,1:T(8,128)(2,1)} %param.15) | copy-start | bytes 1572868
  32.9 29.3 %all-to-all-start.2 = ((bf16[16,48,1024]{2,1,0:T(8,128)(2,1)}), bf16[16,48,1024]{2,1,0:T(8,128)(2,1)S(1)}, u32[]{:S(2)}, u32[]{:S(2)}) async-start(bf16[16,48,1024]{2,1,0:T(8,128)(2,1)} %bitcast.9), calls=%async_computation.3 | async-start | bytes 3145728 | tf_op jit(solution)/shard_map/seed_rows/all_to_all | solution.py:315
  40.1 7.1 %collective-permute-start.2 = (f32[48,512]{1,0:T(8,128)S(1)}, f32[48,512]{1,0:T(8,128)S(1)}, u32[]{:S(2)}, u32[]{:S(2)}) collective-permute-start(f32[48,512]{1,0:T(8,128)S(1)} %add.92), channel_id=1, source_target_pairs={{0,2},{2,4},{4,6},{6,8},{8,10},{10,12},{12,14},{14,0},{1,3},{3,5},... | collective-permute-start | bytes 294920 | tf_op jit(solution)/shard_map/hop_2/ppermute | solution.py:284
  41.8 23.9 %copy-start.7 = (f32[48,512]{1,0:T(8,128)S(1)}, f32[48,512]{1,0:T(8,128)}, u32[]{:S(2)}) copy-start(f32[48,512]{1,0:T(8,128)} %get-tuple-element.53) | copy-start | bytes 294916
  41.8 30.9 %copy-start.6 = (f32[48,512]{1,0:T(8,128)S(1)}, f32[48,512]{1,0:T(8,128)}, u32[]{:S(2)}) copy-start(f32[48,512]{1,0:T(8,128)} %get-tuple-element.51) | copy-start | bytes 294916
  41.8 7.2 %collective-permute-start.3 = (f32[48,512]{1,0:T(8,128)S(1)}, f32[48,512]{1,0:T(8,128)S(1)}, u32[]{:S(2)}, u32[]{:S(2)}) collective-permute-start(f32[48,512]{1,0:T(8,128)S(1)} %add.93), channel_id=1, source_target_pairs={{0,14},{2,0},{4,2},{6,4},{8,6},{10,8},{12,10},{14,12},{1,15},{3,1}... | collective-permute-start | bytes 294920 | tf_op jit(solution)/shard_map/hop_2/ppermute | solution.py:284
  49.0 16.6 %collective-permute-start.4 = (f32[48,512]{1,0:T(8,128)S(1)}, f32[48,512]{1,0:T(8,128)S(1)}, u32[]{:S(2)}, u32[]{:S(2)}) collective-permute-start(f32[48,512]{1,0:T(8,128)S(1)} %add.94), channel_id=1, source_target_pairs={{0,2},{2,4},{4,6},{6,8},{8,10},{10,12},{12,14},{14,0},{1,3},{3,5},... | collective-permute-start | bytes 294920 | tf_op jit(solution)/shard_map/hop_3/ppermute | solution.py:284
  51.2 14.5 %collective-permute-start.5 = (f32[48,512]{1,0:T(8,128)S(1)}, f32[48,512]{1,0:T(8,128)S(1)}, u32[]{:S(2)}, u32[]{:S(2)}) collective-permute-start(f32[48,512]{1,0:T(8,128)S(1)} %add.95), channel_id=1, source_target_pairs={{0,14},{2,0},{4,2},{6,4},{8,6},{10,8},{12,10},{14,12},{1,15},{3,1}... | collective-permute-start | bytes 294920 | tf_op jit(solution)/shard_map/hop_3/ppermute | solution.py:284
  62.2 28.3 %copy-start = (bf16[16,48,1024]{2,1,0:T(8,128)(2,1)}, bf16[16,48,1024]{2,1,0:T(8,128)(2,1)S(1)}, u32[]{:S(2)}) copy-start(bf16[16,48,1024]{2,1,0:T(8,128)(2,1)S(1)} %all-to-all-done.2) | copy-start | bytes 4718596
  62.2 11.5 %all-to-all-start.3 = ((bf16[4,64,1024]{2,1,0:T(8,128)(2,1)}), bf16[4,64,1024]{2,1,0:T(8,128)(2,1)S(1)}, u32[]{:S(2)}, u32[]{:S(2)}) async-start(bf16[4,64,1024]{2,1,0:T(8,128)(2,1)} %bitcast.35), calls=%async_computation.4 | async-start | bytes 1048576 | tf_op jit(solution)/shard_map/cotangent_rows/all_to_all | solution.py:324
  65.7 7.0 %collective-permute-start.6 = (f32[48,512]{1,0:T(8,128)S(1)}, f32[48,512]{1,0:T(8,128)S(1)}, u32[]{:S(2)}, u32[]{:S(2)}) collective-permute-start(f32[48,512]{1,0:T(8,128)S(1)} %add.96), channel_id=1, source_target_pairs={{0,2},{2,4},{4,6},{6,8},{8,10},{10,12},{12,14},{14,0},{1,3},{3,5},... | collective-permute-start | bytes 294920 | tf_op jit(solution)/shard_map/hop_4/ppermute | solution.py:284
  73.7 16.8 %copy-start.1 = (bf16[4,64,1024]{2,1,0:T(8,128)(2,1)}, bf16[4,64,1024]{2,1,0:T(8,128)(2,1)S(1)}, u32[]{:S(2)}) copy-start(bf16[4,64,1024]{2,1,0:T(8,128)(2,1)S(1)} %all-to-all-done.3) | copy-start | bytes 1572868
  75.4 15.1 %all-to-all-start.4 = ((bf16[16,48,128]{2,1,0:T(8,128)(2,1)}), bf16[16,48,128]{2,1,0:T(8,128)(2,1)S(1)}, u32[]{:S(2)}, u32[]{:S(2)}) async-start(bf16[16,48,128]{2,1,0:T(8,128)(2,1)} %mean_rows_3584.1), calls=%async_computation.5 | async-start | bytes 393216 | tf_op jit(solution)/shard_map/mean_rows_3584/all_to_all | solution.py:341
  90.5 28.7 %all-to-all-start.1 = ((bf16[16,48,896]{2,1,0:T(8,128)(2,1)}), bf16[16,48,896]{2,1,0:T(8,128)(2,1)S(1)}, u32[]{:S(2)}, u32[]{:S(2)}) async-start(bf16[16,48,896]{2,1,0:T(8,128)(2,1)} %mean_rows_0.1), calls=%async_computation.2 | async-start | bytes 2752512 | tf_op jit(solution)/shard_map/mean_rows_0/all_to_all | solution.py:341
  123.3 24.5 %copy-start.2 = (bf16[256,1024]{1,0:T(8,128)(2,1)S(1)}, bf16[256,1024]{1,0:T(8,128)(2,1)}, u32[]{:S(2)}) copy-start(bf16[256,1024]{1,0:T(8,128)(2,1)} %get-tuple-element.63) | copy-start | bytes 1572868
  140.5 15.6 %all-to-all-start.6 = ((bf16[8,96,128]{2,1,0:T(8,128)(2,1)}), bf16[8,96,128]{2,1,0:T(8,128)(2,1)S(1)}, u32[]{:S(2)}, u32[]{:S(2)}) async-start(bf16[8,96,128]{2,1,0:T(8,128)(2,1)} %bitcast.15), calls=%async_computation.7 | async-start | bytes 393216 | tf_op jit(solution)/shard_map/grads/all_to_all | solution.py:353
  147.8 8.3 %collective-permute-start.7 = (bf16[64,1024]{1,0:T(8,128)(2,1)S(1)}, bf16[64,1024]{1,0:T(8,128)(2,1)S(1)}, u32[]{:S(2)}, u32[]{:S(2)}) collective-permute-start(bf16[64,1024]{1,0:T(8,128)(2,1)S(1)} %get-tuple-element.71), channel_id=1, source_target_pairs={{0,16},{16,32},{32,48},{48,0},{64,80},{80,96},{96,112},{112,64},{1... | collective-permute-start | bytes 393224 | tf_op jit(solution)/shard_map/hidden_columns/ppermute | solution.py:279
  148.3 7.9 %collective-permute-start.8 = (bf16[64,1024]{1,0:T(8,128)(2,1)S(1)}, bf16[64,1024]{1,0:T(8,128)(2,1)S(1)}, u32[]{:S(2)}, u32[]{:S(2)}) collective-permute-start(bf16[64,1024]{1,0:T(8,128)(2,1)S(1)} %get-tuple-element.70), channel_id=1, source_target_pairs={{0,32},{16,48},{32,0},{48,16},{64,96},{80,112},{96,64},{112,80},{1... | collective-permute-start | bytes 393224 | tf_op jit(solution)/shard_map/hidden_columns/ppermute | solution.py:279
  150.3 6.0 %collective-permute-start.9 = (bf16[64,1024]{1,0:T(8,128)(2,1)S(1)}, bf16[64,1024]{1,0:T(8,128)(2,1)S(1)}, u32[]{:S(2)}, u32[]{:S(2)}) collective-permute-start(bf16[64,1024]{1,0:T(8,128)(2,1)S(1)} %get-tuple-element.69), channel_id=1, source_target_pairs={{0,48},{16,0},{32,16},{48,32},{64,112},{80,64},{96,80},{112,96},{1... | collective-permute-start | bytes 393224 | tf_op jit(solution)/shard_map/hidden_columns/ppermute | solution.py:279
  157.1 0.8 copy-start.3
Sparse Core Ops, SparseCore 0:
  14.5 73.6 reduce-scatter.1

commit v5 on v4

--- a/solution.py
+++ b/solution.py
@@ -8,7 +8,7 @@
 F32, BF16 = jnp.float32, jnp.bfloat16
 UNROLL = 16
 SIDE = 4
-EARLY = 7
+EARLY = 6
 HBM = pl.BlockSpec(memory_space=pltpu.HBM)
 
 
@@ -17,7 +17,7 @@
 
 
 def tile_kernel(me, dst_h, src_h, feats_h, counts_h, sums_h, *refs):
-    *late_h, deg_h, dst, src, feats, counts, acc, deg, held, short, sems = refs
+    *late_h, deg_h, dst, src, feats, counts, acc, deg, held, short, far_sums, sems = refs
     per_part = acc.shape[2] // held.shape[2] // SIDE
     early = sums_h.shape[2]
     cols = feats.shape[0]
@@ -70,8 +70,9 @@
 
     lax.fori_loop(0, nload, chunk, 0)
     stores = []
-    for k in (4, 5):
-        stores.append((acc.at[lax.rem(me[0] + k, owners), :, pl.ds(early, seeds_here - early)], late_h[k]))
+    far_sums[...] = acc[lax.rem(me[0] + 4, owners), :, early:].astype(BF16)
+    stores.append((far_sums, late_h[4]))
+    stores.append((acc.at[lax.rem(me[0] + 5, owners), :, pl.ds(early, seeds_here - early)], late_h[5]))
     width = short.shape[2]
     for o in range(owners):
         for r in range(short.shape[1]):
@@ -91,13 +92,15 @@
     ntile, tile, _ = counts.shape
     cols, sources = feats_t.shape
     early = seeds_here // 8 * EARLY
-    outs = [(owners, cols, early)] + [(cols, seeds_here - early)] * owners
-    outs.append((owners, 8, seeds_here // 8))
+    outs = [((owners, cols, early), F32)]
+    for k in range(owners):
+        outs.append(((cols, seeds_here - early), BF16 if k == 4 else F32))
+    outs.append(((owners, 8, seeds_here // 8), F32))
     sums, *late, deg = pl.pallas_call(
         tile_kernel,
         in_specs=[pl.BlockSpec(memory_space=pltpu.SMEM)] + [HBM] * 4,
         out_specs=[HBM] * len(outs),
-        out_shape=[pltpu.HBM(o, F32) for o in outs],
+        out_shape=[pltpu.HBM(*o) for o in outs],
         scratch_shapes=[
             pltpu.SMEM((ntile,), jnp.int32),
             pltpu.SMEM((ntile,), jnp.int32),
@@ -107,6 +110,7 @@
             pltpu.VMEM((owners, 8, seeds_here), F32),
             pltpu.VMEM((sources // tile, cols + 16, tile), BF16),
             pltpu.VMEM((owners, 8, seeds_here // 8), F32),
+            pltpu.VMEM((cols, seeds_here - early), BF16),
             pltpu.SemaphoreType.DMA((max(ntile // UNROLL + 3, len(outs)),)),
         ],
         compiler_params=pltpu.CompilerParams(vmem_limit_bytes=40 * 1024 * 1024),
@@ -273,7 +277,6 @@
     hcols = SIDE * ccols
     f = lax.axis_index("feat")
     fx, fy = f // SIDE, f % SIDE
-    along_y = [[x * SIDE + y for y in range(SIDE)] for x in range(SIDE)]
 
     def shift_y(a, k):
         return lax.ppermute(
@@ -282,6 +285,9 @@
 
     def shift_z(a, k):
         return lax.ppermute(a, "group", [(i, (i + k) % ng) for i in range(ng)])
+
+    def plus(a, k):
+        return (a.astype(F32) + late[k]).astype(BF16)
 
     def meet(*arrays):
         return lax.optimization_barrier(arrays)
@@ -304,7 +310,7 @@
     with jax.named_scope("hop_1"):
         up = shift_z(late[4], 1)
         down = shift_z(late[5], -1)
-        up, down, seed_t = meet(up, down, seed_feats.T)
+        up, down, seed_t, cot_t = meet(up, down, seed_feats.T, cotangent.T)
 
     with jax.named_scope("degree"):
         degree = jnp.sum(lax.all_to_all(deg, "group", 0, 0), axis=0).reshape(1, seeds_here)
@@ -315,23 +321,26 @@
         seeds = lax.all_to_all(send, "feat", 0, 0).reshape(nf * cols, part)
 
     with jax.named_scope("hop_2"):
-        up = shift_z(up + late[3], 1)
+        up = shift_z(plus(up, 3), 1)
         down = shift_z(down + late[6], -1)
-        up, down, degree, cot_t = meet(up, down, degree, cotangent.T)
+        up, down, degree = meet(up, down, degree)
 
     with jax.named_scope("cotangent_rows"):
-        send = cot_t.reshape(ccols, SIDE, part).transpose(1, 0, 2)
-        cot = lax.all_to_all(send, "feat", 0, 0, axis_index_groups=along_y)
+        cot = jnp.zeros((SIDE, ccols, part), BF16)
+        for k in range(SIDE):
+            piece = lax.dynamic_slice_in_dim(cot_t, (fy + k) % SIDE * part, part, 1)
+            piece = shift_y(piece, k) if k else piece
+            cot = lax.dynamic_update_slice(cot, piece[None], ((fy - k) % SIDE, 0, 0))
         cot = cot.reshape(hcols, part)
 
     with jax.named_scope("hop_3"):
-        up = shift_z(up + late[2], 1)
+        up = shift_z(plus(up, 2), 1)
         down = shift_z(down + late[7], -1)
-        up, down, seeds = meet(up, down, seeds)
+        up, down, cot = meet(up, down, cot)
 
     with jax.named_scope("hop_4"):
-        up = shift_z(up + late[1], 1)
-        total2, cot = meet(late[0] + up + down, cot)
+        up = shift_z(plus(up, 1), 1)
+        total2, seeds = meet(late[0] + up.astype(F32) + down, seeds)
 
     early = total.shape[1]
     means = []

time: 166 us -> 159 us (0.958)
  waiting for transfers between devices: 55.9 us -> 41 us
  local copies, waits for them, and re-layouts: 7.32 us -> 10.9 us
  starting transfers between devices: 50.7 us -> 53.3 us
    all_to_all x1, waiting for transfers between devices: 10.1 us -> 0.01 us  [shards(): seeds = lax.all_to_all(send, 'feat', 0, 0).reshape(nf * cols, part)]
    ppermute x3 -> x6, starting transfers between devices: 4.17 us -> 10 us  [shift_y(): lax.ppermute(a, 'feat', [(i, i // SIDE * SIDE + (i % SIDE + k) % SIDE) fo...]
    ppermute x7, waiting for transfers between devices: 17.1 us -> 13.6 us  [shift_z(): return lax.ppermute(a, 'group', [(i, (i + k) % ng) for i in range(ng)])]
    all_to_all x1 -> x0, starting transfers between devices: 3.47 us -> none  [shards(): cot = lax.all_to_all(send, 'feat', 0, 0, axis_index_groups=along_y)]
    all_to_all x1, starting transfers between devices: 7.18 us -> 4.91 us  [shards(): seeds = lax.all_to_all(send, 'feat', 0, 0).reshape(nf * cols, part)]
    all_to_all x2, starting transfers between devices: 11.9 us -> 14.1 us  [shards(): means.append(lax.all_to_all(send, 'feat', 0, 0).reshape(nf * cols, -1))]
    ppermute x7, starting transfers between devices: 7.99 us -> 10.2 us  [shift_z(): return lax.ppermute(a, 'group', [(i, (i + k) % ng) for i in range(ng)])]
    all_to_all x2, waiting for transfers between devices: 15.2 us -> 13.3 us  [shards(): means.append(lax.all_to_all(send, 'feat', 0, 0).reshape(nf * cols, -1))]
  transfers between devices with their start and end apart: 17 -> 19, of which waited for: 12 -> 7; matrix products, arithmetic and copies ran while one was open for 4% -> 7% of each run, Pallas kernels for 4% -> 5%
where the time goes in v5:
time: 159 us; the launch traced here: 158 us
  starting transfers between devices  53.3 us (34%)
  waiting for transfers between devices  41 us (26%)
  Pallas kernels  18.4 us (12%)
  blocking collectives  16.6 us (10%)
  between operations  14.5 us (9%)
  local copies, waits for them, and re-layouts  10.9 us (7%)
  other arithmetic  3.19 us (2%)
    all_to_all x1, blocking collectives, shards(): got = lax.all_to_all(both, 'feat', 0, 0).astype(F32)  16.6 us
    all_to_all x2, starting transfers between devices, shards(): means.append(lax.all_to_all(send, 'feat', 0, 0).reshape(nf * cols, -1))  14.1 us
    ppermute x7, waiting for transfers between devices, shift_z(): return lax.ppermute(a, 'group', [(i, (i + k) % ng) for i in range(ng)])  13.6 us
    all_to_all x2, waiting for transfers between devices, shards(): means.append(lax.all_to_all(send, 'feat', 0, 0).reshape(nf * cols, -1))  13.3 us
    ppermute x7, starting transfers between devices, shift_z(): return lax.ppermute(a, 'group', [(i, (i + k) % ng) for i in range(ng)])  10.2 us
    ppermute x6, starting transfers between devices, shift_y(): lax.ppermute(a, 'feat', [(i, i // SIDE * SIDE + (i % SIDE + k) % SIDE) fo...  10 us
    reduce_scatter x1, waiting for transfers between devices, shards(): lax.psum_scatter(sums.reshape(ng * cols, -1), 'group', scatter_dimension=...  9.79 us
    all_to_all x1, starting transfers between devices, shards(): lax.all_to_all(deg, 'group', 0, 0)  8.57 us
  transfers between devices with their start and end apart: 19, of which 7 were waited for; matrix products, arithmetic and copies ran while one was open for 7% of the time, Pallas kernels for 5%

profile of v5, /device:TPU:32, one launch (start us, length us, event | category | flops | bytes accessed | tf_op | source)
XLA Modules:
  0.0 157.8 jit_solution(10482221812176900467)
XLA Ops:
  7.2 0.0 reduce-scatter.2.cloned.1.call-start
  7.2 7.1 %tile_sums.1 = (f32[8,48,3072]{2,1,0:T(8,128)}, f32[48,1024]{1,0:T(8,128)}, f32[48,1024]{1,0:T(8,128)}, f32[48,1024]{1,0:T(8,128)}, f32[48,1024]{1,0:T(8,128)}, ...) custom-call(s32[1]{0:T(128)} %bitcast.1.me, ...), custom_call_target="tpu_custom_call" | custom-call | tf_op jit(solution)/shard_map/tile_sums/pallas_call | solution.py:99
  14.4 0.0 copy-start.4
  14.4 0.0 reduce-scatter.2.cloned.1.call-update
  14.4 0.0 copy-start.5
  14.4 0.8 copy-done.13
  15.3 1.8 %collective-permute-start.1 = (f32[48,1024]{1,0:T(8,128)S(1)}, f32[48,1024]{1,0:T(8,128)S(1)}, u32[]{:S(2)}, u32[]{:S(2)}) collective-permute-start(f32[48,1024]{1,0:T(8,128)S(1)} %copy-done.13), channel_id=1, source_target_pairs={{0,14},{2,0},{4,2},{6,4},{8,6},{10,8},{12,10},{14,12},{1,15},{3,1}... | collective-permute-start | bytes 589832 | tf_op jit(solution)/shard_map/hop_1/ppermute | solution.py:287
  17.1 0.2 collective-permute-start
  17.3 8.6 %all-to-all-start = ((f32[8,8,512]{2,1,0:T(8,128)}), f32[8,8,512]{2,1,0:T(8,128)S(1)}, u32[]{:S(2)}, u32[]{:S(2)}) async-start(f32[8,8,512]{2,1,0:T(8,128)} %get-tuple-element.43), calls=%async_computation.1 | async-start | bytes 262144 | tf_op jit(solution)/shard_map/degree/all_to_all | solution.py:316
  25.9 0.0 collective-permute-done
  25.9 0.0 collective-permute-done.1
  25.9 0.8 constant_dynamic-slice_fusion
  26.7 1.6 collective-permute-start.6
  28.3 0.7 add_convert_fusion.2
  28.9 1.5 collective-permute-start.2
  30.4 0.6 collective-permute-start.3
  31.1 2.9 %collective-permute-start.7 = (bf16[64,1024]{1,0:T(8,128)(2,1)}, bf16[64,1024]{1,0:T(8,128)(2,1)}, u32[]{:S(2)}, u32[]{:S(2)}) collective-permute-start(bf16[64,1024]{1,0:T(8,128)(2,1)} %get-tuple-element.74), channel_id=1, source_target_pairs={{0,32},{16,48},{32,0},{48,16},{64,96},{80,112},{96,64},{112,80},{1... | collective-permute-start | bytes 393224 | tf_op jit(solution)/shard_map/cotangent_rows/ppermute | solution.py:282
  34.0 1.3 collective-permute-start.8
  35.3 0.3 reshape.47
  35.6 0.1 copy.17
  35.7 0.1 broadcast_in_dim.29
  35.8 1.4 broadcast_in_dim.34
  37.2 4.9 %all-to-all-start.2 = ((bf16[16,48,1024]{2,1,0:T(8,128)(2,1)}), bf16[16,48,1024]{2,1,0:T(8,128)(2,1)S(1)}, u32[]{:S(2)}, u32[]{:S(2)}) async-start(bf16[16,48,1024]{2,1,0:T(8,128)(2,1)} %bitcast.14), calls=%async_computation.3 | async-start | bytes 3145728 | tf_op jit(solution)/shard_map/seed_rows/all_to_all | solution.py:321
  42.1 0.0 copy-start.9
  42.2 0.0 copy-start.12
  42.2 0.0 collective-permute-done.6
  42.2 1.0 bitcast_dynamic-update-slice_fusion.2
  43.3 0.9 bitcast_dynamic-update-slice_fusion.1
  44.2 0.0 collective-permute-done.2
  44.2 0.9 add_convert_fusion.1
  45.1 1.5 collective-permute-start.4
  46.7 1.4 collective-permute-start.5
  48.1 4.7 %collective-permute-done.4 = bf16[48,1024]{1,0:T(8,128)(2,1)S(1)} collective-permute-done((bf16[48,1024]{1,0:T(8,128)(2,1)S(1)}, bf16[48,1024]{1,0:T(8,128)(2,1)S(1)}, u32[]{:S(2)}, u32[]{:S(2)}) %collective-permute-start.4) | collective-permute-done | bytes 98336 | tf_op jit(solution)/shard_map/hop_3/ppermute | solution.py:287
  52.9 4.9 %collective-permute-done.5 = f32[48,1024]{1,0:T(8,128)S(1)} collective-permute-done((f32[48,1024]{1,0:T(8,128)S(1)}, f32[48,1024]{1,0:T(8,128)S(1)}, u32[]{:S(2)}, u32[]{:S(2)}) %collective-permute-start.5) | collective-permute-done | bytes 196640 | tf_op jit(solution)/shard_map/hop_3/ppermute | solution.py:287
  57.7 3.1 %collective-permute-start.9 = (bf16[48,1024]{1,0:T(8,128)(2,1)S(1)}, bf16[48,1024]{1,0:T(8,128)(2,1)S(1)}, u32[]{:S(2)}, u32[]{:S(2)}) collective-permute-start(bf16[48,1024]{1,0:T(8,128)(2,1)S(1)} %add_convert_fusion), channel_id=1, source_target_pairs={{0,2},{2,4},{4,6},{6,8},{8,10},{10,12},{12,14},{14,0},{1,3},{3,5},... | collective-permute-start | bytes 294920 | tf_op jit(solution)/shard_map/hop_4/ppermute | solution.py:287
  60.8 4.0 %collective-permute-done.9 = bf16[48,1024]{1,0:T(8,128)(2,1)S(1)} collective-permute-done((bf16[48,1024]{1,0:T(8,128)(2,1)S(1)}, bf16[48,1024]{1,0:T(8,128)(2,1)S(1)}, u32[]{:S(2)}, u32[]{:S(2)}) %collective-permute-start.9) | collective-permute-done | bytes 98336 | tf_op jit(solution)/shard_map/hop_4/ppermute | solution.py:287
  64.8 0.7 add_add_fusion.total_h
  65.6 1.9 %mean_rows_3072.1 = bf16[16,48,256]{2,1,0:T(8,128)(2,1)} custom-call(f32[48,1024]{1,0:T(8,128)} %add_add_fusion.total_h, f32[1,1024]{1,0:T(1,128)S(1)} %slice.21.degree_h), custom_call_target="tpu_custom_call" | custom-call | tf_op jit(solution)/shard_map/mean_rows_3072/pallas_call | solution.py:149
  67.5 7.2 %all-to-all-start.3 = ((bf16[16,48,256]{2,1,0:T(8,128)(2,1)}), bf16[16,48,256]{2,1,0:T(8,128)(2,1)S(1)}, u32[]{:S(2)}, u32[]{:S(2)}) async-start(bf16[16,48,256]{2,1,0:T(8,128)(2,1)} %mean_rows_3072.1), calls=%async_computation.4 | async-start | bytes 786432 | tf_op jit(solution)/shard_map/mean_rows_3072/all_to_all | solution.py:350
  74.7 0.7 slice.20.degree_h
  75.4 9.8 %reduce-scatter.2.cloned.1.call-done.total_h = f32[48,3072]{1,0:T(8,128)} async-done(((f32[384,3072]{1,0:T(8,128)}), f32[48,3072]{1,0:T(8,128)}) %reduce-scatter.2.cloned.1.call-update) | async-done | bytes 589840 | tf_op jit(solution)/shard_map/neighbour_sum/reduce_scatter | solution.py:302
  85.2 2.1 %mean_rows_0.1 = bf16[16,48,768]{2,1,0:T(8,128)(2,1)} custom-call(f32[48,3072]{1,0:T(8,128)} %reduce-scatter.2.cloned.1.call-done.total_h, f32[1,3072]{1,0:T(1,128)S(1)} %slice.20.degree_h), custom_call_target="tpu_custom_call" | custom-call | tf_op jit(solution)/shard_map/mean_rows_0/pallas_call | solution.py:149
  87.3 0.0 all-to-all-done.3
  87.3 6.9 %all-to-all-start.1 = ((bf16[16,48,768]{2,1,0:T(8,128)(2,1)}), bf16[16,48,768]{2,1,0:T(8,128)(2,1)S(1)}, u32[]{:S(2)}, u32[]{:S(2)}) async-start(bf16[16,48,768]{2,1,0:T(8,128)(2,1)} %mean_rows_0.1), calls=%async_computation.2 | async-start | bytes 2359296 | tf_op jit(solution)/shard_map/mean_rows_0/all_to_all | solution.py:350
  94.3 1.2 constant_dynamic-slice_fusion.3
  95.5 0.9 copy.18
  96.4 0.9 copy.19
  97.4 3.2 %layer.2 = (bf16[256,1024]{1,0:T(8,128)(2,1)}, f32[256,768]{1,0:T(8,128)}) custom-call(bf16[256,768]{1,0:T(8,128)(2,1)} %bitcast.48, bf16[768,1024]{1,0:T(8,128)(2,1)} %bitcast.40, bf16[256,768]{1,0:T(8,128)(2,1)} %bitcast.43, bf16[768,256]{1,0:T(8,128)(2,1)S(1)} %bitcast.38), custom_call_target="tpu_custom_call" | custom-call | tf_op jit(solution)/shard_map/layer/pallas_call | solution.py:190
  100.6 13.3 %all-to-all-done.1 = bf16[16,48,768]{2,1,0:T(8,128)(2,1)S(1)} async-done(((bf16[16,48,768]{2,1,0:T(8,128)(2,1)}), bf16[16,48,768]{2,1,0:T(8,128)(2,1)S(1)}, u32[]{:S(2)}, u32[]{:S(2)}) %all-to-all-start.1) | async-done | bytes 1179680 | tf_op jit(solution)/shard_map/mean_rows_0/all_to_all | solution.py:350
  113.9 4.0 %layer.3 = (bf16[256,1024]{1,0:T(8,128)(2,1)}, bf16[16,96,256]{2,1,0:T(8,128)(2,1)}) custom-call(bf16[256,768]{1,0:T(8,128)(2,1)} %bitcast.44, bf16[768,768]{1,0:T(8,128)(2,1)S(1)} %bitcast.37, f32[256,768]{1,0:T(8,128)} %get-tuple-element.57.pre_h, bf16[256,1024]{1,0:T(8,128)(2,1)} %bitcast.46, ...), custom_call_target="tpu_custom_call", output_to_operand_aliasing={{0}: (5, {})} | custom-call | tf_op jit(solution)/shard_map/layer/pallas_call | solution.py:251
  117.9 0.0 copy-start.1
  117.9 16.6 %all_to_all.30 = bf16[16,96,256]{2,1,0:T(8,128)(2,1)S(1)} all-to-all(bf16[16,96,256]{2,1,0:T(8,128)(2,1)} %get-tuple-element.60), channel_id=1, replica_groups=mesh['feat'=16,'group'=8,'rep'=2] {'feat'}, dimensions={0} | all-to-all | bytes 1572864 | tf_op jit(solution)/shard_map/grads/all_to_all | solution.py:357
  134.5 0.1 bitcast_reduce_fusion
  134.7 0.7 pad_maximum_fusion
  135.4 5.5 %all-to-all-start.5 = ((bf16[8,96,128]{2,1,0:T(8,128)(2,1)}), bf16[8,96,128]{2,1,0:T(8,128)(2,1)S(1)}, u32[]{:S(2)}, u32[]{:S(2)}) async-start(bf16[8,96,128]{2,1,0:T(8,128)(2,1)} %bitcast.18), calls=%async_computation.6 | async-start | bytes 393216 | tf_op jit(solution)/shard_map/grads/all_to_all | solution.py:362
  140.9 0.5 collective-permute-start.10
  141.4 2.0 %collective-permute-start.11 = (bf16[64,1024]{1,0:T(8,128)(2,1)S(1)}, bf16[64,1024]{1,0:T(8,128)(2,1)S(1)}, u32[]{:S(2)}, u32[]{:S(2)}) collective-permute-start(bf16[64,1024]{1,0:T(8,128)(2,1)S(1)} %get-tuple-element.70), channel_id=1, source_target_pairs={{0,32},{16,48},{32,0},{48,16},{64,96},{80,112},{96,64},{112,80},{1... | collective-permute-start | bytes 393224 | tf_op jit(solution)/shard_map/hidden_columns/ppermute | solution.py:282
  143.4 1.7 %collective-permute-start.12 = (bf16[64,1024]{1,0:T(8,128)(2,1)S(1)}, bf16[64,1024]{1,0:T(8,128)(2,1)S(1)}, u32[]{:S(2)}, u32[]{:S(2)}) collective-permute-start(bf16[64,1024]{1,0:T(8,128)(2,1)S(1)} %get-tuple-element.69), channel_id=1, source_target_pairs={{0,48},{16,0},{32,16},{48,32},{64,112},{80,64},{96,80},{112,96},{1... | collective-permute-start | bytes 393224 | tf_op jit(solution)/shard_map/hidden_columns/ppermute | solution.py:282
  145.1 4.1 %all-to-all-done.5 = bf16[8,96,128]{2,1,0:T(8,128)(2,1)S(1)} async-done(((bf16[8,96,128]{2,1,0:T(8,128)(2,1)}), bf16[8,96,128]{2,1,0:T(8,128)(2,1)S(1)}, u32[]{:S(2)}, u32[]{:S(2)}) %all-to-all-start.5) | async-done | bytes 196640 | tf_op jit(solution)/shard_map/grads/all_to_all | solution.py:362
  149.2 0.0 collective-permute-done.10
  149.2 0.2 collective-permute-done.12
  149.4 0.6 fusion.1
  150.2 0.0 copy-start.3
  150.2 0.8 copy-done.3
  (44 shorter events, 0.4 us)
Async XLA Ops:
  7.2 78.0 %reduce-scatter.2.cloned.1.call-start = ((), (), s32[]{:S(2)}) async-start(), calls=%async_computation.7 | async-start | bytes 5308416 | tf_op jit(solution)/shard_map/neighbour_sum/reduce_scatter | solution.py:302
  14.3 0.9 copy-start.13
  14.3 2.8 %copy-start.14 = (bf16[48,1024]{1,0:T(8,128)(2,1)S(1)}, bf16[48,1024]{1,0:T(8,128)(2,1)}, u32[]{:S(2)}) copy-start(bf16[48,1024]{1,0:T(8,128)(2,1)} %get-tuple-element.37) | copy-start | bytes 294916
  14.4 11.5 %copy-start.4 = (bf16[4096,64]{0,1:T(8,128)(2,1)S(1)}, bf16[4096,64]{0,1:T(8,128)(2,1)}, u32[]{:S(2)}) copy-start(bf16[4096,64]{0,1:T(8,128)(2,1)} %param.15) | copy-start | bytes 1572868
  14.4 13.9 %copy-start.8 = (f32[48,1024]{1,0:T(8,128)S(1)}, f32[48,1024]{1,0:T(8,128)}, u32[]{:S(2)}) copy-start(f32[48,1024]{1,0:T(8,128)} %get-tuple-element.40) | copy-start | bytes 589828
  14.4 16.0 %copy-start.11 = (f32[48,1024]{1,0:T(8,128)S(1)}, f32[48,1024]{1,0:T(8,128)}, u32[]{:S(2)}) copy-start(f32[48,1024]{1,0:T(8,128)} %get-tuple-element.42) | copy-start | bytes 589828
  14.4 20.9 %copy-start.5 = (bf16[4096,48]{0,1:T(8,128)(2,1)S(1)}, bf16[4096,48]{0,1:T(8,128)(2,1)}, u32[]{:S(2)}) copy-start(bf16[4096,48]{0,1:T(8,128)(2,1)} %param.8) | copy-start | bytes 1179652
  15.3 10.6 %collective-permute-start.1 = (f32[48,1024]{1,0:T(8,128)S(1)}, f32[48,1024]{1,0:T(8,128)S(1)}, u32[]{:S(2)}, u32[]{:S(2)}) collective-permute-start(f32[48,1024]{1,0:T(8,128)S(1)} %copy-done.13), channel_id=1, source_target_pairs={{0,14},{2,0},{4,2},{6,4},{8,6},{10,8},{12,10},{14,12},{1,15},{3,1}... | collective-permute-start | bytes 589832 | tf_op jit(solution)/shard_map/hop_1/ppermute | solution.py:287
  17.1 8.8 %collective-permute-start = (bf16[48,1024]{1,0:T(8,128)(2,1)S(1)}, bf16[48,1024]{1,0:T(8,128)(2,1)S(1)}, u32[]{:S(2)}, u32[]{:S(2)}) collective-permute-start(bf16[48,1024]{1,0:T(8,128)(2,1)S(1)} %copy-done.14), channel_id=1, source_target_pairs={{0,2},{2,4},{4,6},{6,8},{8,10},{10,12},{12,14},{14,0},{1,3},{3,5},... | collective-permute-start | bytes 294920 | tf_op jit(solution)/shard_map/hop_1/ppermute | solution.py:287
  17.3 18.5 %all-to-all-start = ((f32[8,8,512]{2,1,0:T(8,128)}), f32[8,8,512]{2,1,0:T(8,128)S(1)}, u32[]{:S(2)}, u32[]{:S(2)}) async-start(f32[8,8,512]{2,1,0:T(8,128)} %get-tuple-element.43), calls=%async_computation.1 | async-start | bytes 262144 | tf_op jit(solution)/shard_map/degree/all_to_all | solution.py:316
  26.7 15.5 %collective-permute-start.6 = (bf16[64,1024]{1,0:T(8,128)(2,1)}, bf16[64,1024]{1,0:T(8,128)(2,1)}, u32[]{:S(2)}, u32[]{:S(2)}) collective-permute-start(bf16[64,1024]{1,0:T(8,128)(2,1)} %get-tuple-element.75), channel_id=1, source_target_pairs={{0,16},{16,32},{32,48},{48,0},{64,80},{80,96},{96,112},{112,64},{1... | collective-permute-start | bytes 393224 | tf_op jit(solution)/shard_map/cotangent_rows/ppermute | solution.py:282
  28.9 15.3 %collective-permute-start.2 = (bf16[48,1024]{1,0:T(8,128)(2,1)}, bf16[48,1024]{1,0:T(8,128)(2,1)}, u32[]{:S(2)}, u32[]{:S(2)}) collective-permute-start(bf16[48,1024]{1,0:T(8,128)(2,1)} %add_convert_fusion.2), channel_id=1, source_target_pairs={{0,2},{2,4},{4,6},{6,8},{8,10},{10,12},{12,14},{14,0},{1,3},{3,5},... | collective-permute-start | bytes 294920 | tf_op jit(solution)/shard_map/hop_2/ppermute | solution.py:287
  30.4 13.8 %collective-permute-start.3 = (f32[48,1024]{1,0:T(8,128)S(1)}, f32[48,1024]{1,0:T(8,128)S(1)}, u32[]{:S(2)}, u32[]{:S(2)}) collective-permute-start(f32[48,1024]{1,0:T(8,128)S(1)} %add.124), channel_id=1, source_target_pairs={{0,14},{2,0},{4,2},{6,4},{8,6},{10,8},{12,10},{14,12},{1,15},{3,1}... | collective-permute-start | bytes 589832 | tf_op jit(solution)/shard_map/hop_2/ppermute | solution.py:287
  31.1 12.2 %collective-permute-start.7 = (bf16[64,1024]{1,0:T(8,128)(2,1)}, bf16[64,1024]{1,0:T(8,128)(2,1)}, u32[]{:S(2)}, u32[]{:S(2)}) collective-permute-start(bf16[64,1024]{1,0:T(8,128)(2,1)} %get-tuple-element.74), channel_id=1, source_target_pairs={{0,32},{16,48},{32,0},{48,16},{64,96},{80,112},{96,64},{112,80},{1... | collective-permute-start | bytes 393224 | tf_op jit(solution)/shard_map/cotangent_rows/ppermute | solution.py:282
  34.0 14.2 %collective-permute-start.8 = (bf16[64,1024]{1,0:T(8,128)(2,1)}, bf16[64,1024]{1,0:T(8,128)(2,1)S(1)}, u32[]{:S(2)}, u32[]{:S(2)}) collective-permute-start(bf16[64,1024]{1,0:T(8,128)(2,1)} %get-tuple-element.73), channel_id=1, source_target_pairs={{0,48},{16,0},{32,16},{48,32},{64,112},{80,64},{96,80},{112,96},{1... | collective-permute-start | bytes 393224 | tf_op jit(solution)/shard_map/cotangent_rows/ppermute | solution.py:282
  37.2 7.0 %copy-start.7 = (f32[48,1024]{1,0:T(8,128)S(1)}, f32[48,1024]{1,0:T(8,128)}, u32[]{:S(2)}) copy-start(f32[48,1024]{1,0:T(8,128)} %get-tuple-element.47) | copy-start | bytes 589828
  37.2 9.5 %copy-start.10 = (f32[48,1024]{1,0:T(8,128)S(1)}, f32[48,1024]{1,0:T(8,128)}, u32[]{:S(2)}) copy-start(f32[48,1024]{1,0:T(8,128)} %get-tuple-element.49) | copy-start | bytes 589828
  37.2 28.3 %all-to-all-start.2 = ((bf16[16,48,1024]{2,1,0:T(8,128)(2,1)}), bf16[16,48,1024]{2,1,0:T(8,128)(2,1)S(1)}, u32[]{:S(2)}, u32[]{:S(2)}) async-start(bf16[16,48,1024]{2,1,0:T(8,128)(2,1)} %bitcast.14), calls=%async_computation.3 | async-start | bytes 3145728 | tf_op jit(solution)/shard_map/seed_rows/all_to_all | solution.py:321
  42.1 15.6 %copy-start.6 = (f32[48,1024]{1,0:T(8,128)S(1)}, f32[48,1024]{1,0:T(8,128)}, u32[]{:S(2)}) copy-start(f32[48,1024]{1,0:T(8,128)} %get-tuple-element.52) | copy-start | bytes 589828
  42.1 22.7 %copy-start.9 = (f32[48,1024]{1,0:T(8,128)S(1)}, f32[48,1024]{1,0:T(8,128)}, u32[]{:S(2)}) copy-start(f32[48,1024]{1,0:T(8,128)} %get-tuple-element.45) | copy-start | bytes 589828
  42.2 25.3 %copy-start.12 = (f32[1,1,8,512]{3,1,2,0:T(1,128)}, f32[1,1,8,512]{3,1,2,0:T(1,128)S(1)}, u32[]{:S(2)}) copy-start(f32[1,1,8,512]{3,1,2,0:T(1,128)S(1)} %copy.20) | copy-start | bytes 49156
  45.1 7.7 %collective-permute-start.4 = (bf16[48,1024]{1,0:T(8,128)(2,1)S(1)}, bf16[48,1024]{1,0:T(8,128)(2,1)S(1)}, u32[]{:S(2)}, u32[]{:S(2)}) collective-permute-start(bf16[48,1024]{1,0:T(8,128)(2,1)S(1)} %add_convert_fusion.1), channel_id=1, source_target_pairs={{0,2},{2,4},{4,6},{6,8},{8,10},{10,12},{12,14},{14,0},{1,3},{3,5},... | collective-permute-start | bytes 294920 | tf_op jit(solution)/shard_map/hop_3/ppermute | solution.py:287
  46.7 11.0 %collective-permute-start.5 = (f32[48,1024]{1,0:T(8,128)S(1)}, f32[48,1024]{1,0:T(8,128)S(1)}, u32[]{:S(2)}, u32[]{:S(2)}) collective-permute-start(f32[48,1024]{1,0:T(8,128)S(1)} %add.126), channel_id=1, source_target_pairs={{0,14},{2,0},{4,2},{6,4},{8,6},{10,8},{12,10},{14,12},{1,15},{3,1}... | collective-permute-start | bytes 589832 | tf_op jit(solution)/shard_map/hop_3/ppermute | solution.py:287
  48.1 39.2 %copy-start.2 = (bf16[4,64,1024]{2,1,0:T(8,128)(2,1)}, bf16[4,64,1024]{2,1,0:T(8,128)(2,1)S(1)}, u32[]{:S(2)}) copy-start(bf16[4,64,1024]{2,1,0:T(8,128)(2,1)S(1)} %bitcast_dynamic-update-slice_fusion) | copy-start | bytes 1572868
  57.7 7.1 %collective-permute-start.9 = (bf16[48,1024]{1,0:T(8,128)(2,1)S(1)}, bf16[48,1024]{1,0:T(8,128)(2,1)S(1)}, u32[]{:S(2)}, u32[]{:S(2)}) collective-permute-start(bf16[48,1024]{1,0:T(8,128)(2,1)S(1)} %add_convert_fusion), channel_id=1, source_target_pairs={{0,2},{2,4},{4,6},{6,8},{8,10},{10,12},{12,14},{14,0},{1,3},{3,5},... | collective-permute-start | bytes 294920 | tf_op jit(solution)/shard_map/hop_4/ppermute | solution.py:287
  65.6 21.8 %copy-start = (bf16[16,48,1024]{2,1,0:T(8,128)(2,1)}, bf16[16,48,1024]{2,1,0:T(8,128)(2,1)S(1)}, u32[]{:S(2)}) copy-start(bf16[16,48,1024]{2,1,0:T(8,128)(2,1)S(1)} %all-to-all-done.2) | copy-start | bytes 4718596
  67.5 19.8 %all-to-all-start.3 = ((bf16[16,48,256]{2,1,0:T(8,128)(2,1)}), bf16[16,48,256]{2,1,0:T(8,128)(2,1)S(1)}, u32[]{:S(2)}, u32[]{:S(2)}) async-start(bf16[16,48,256]{2,1,0:T(8,128)(2,1)} %mean_rows_3072.1), calls=%async_computation.4 | async-start | bytes 786432 | tf_op jit(solution)/shard_map/mean_rows_3072/all_to_all | solution.py:350
  87.3 26.5 %all-to-all-start.1 = ((bf16[16,48,768]{2,1,0:T(8,128)(2,1)}), bf16[16,48,768]{2,1,0:T(8,128)(2,1)S(1)}, u32[]{:S(2)}, u32[]{:S(2)}) async-start(bf16[16,48,768]{2,1,0:T(8,128)(2,1)} %mean_rows_0.1), calls=%async_computation.2 | async-start | bytes 2359296 | tf_op jit(solution)/shard_map/mean_rows_0/all_to_all | solution.py:350
  117.9 23.0 %copy-start.1 = (bf16[256,1024]{1,0:T(8,128)(2,1)S(1)}, bf16[256,1024]{1,0:T(8,128)(2,1)}, u32[]{:S(2)}) copy-start(bf16[256,1024]{1,0:T(8,128)(2,1)} %get-tuple-element.63) | copy-start | bytes 1572868
  135.4 13.8 %all-to-all-start.5 = ((bf16[8,96,128]{2,1,0:T(8,128)(2,1)}), bf16[8,96,128]{2,1,0:T(8,128)(2,1)S(1)}, u32[]{:S(2)}, u32[]{:S(2)}) async-start(bf16[8,96,128]{2,1,0:T(8,128)(2,1)} %bitcast.18), calls=%async_computation.6 | async-start | bytes 393216 | tf_op jit(solution)/shard_map/grads/all_to_all | solution.py:362
  140.9 8.3 %collective-permute-start.10 = (bf16[64,1024]{1,0:T(8,128)(2,1)S(1)}, bf16[64,1024]{1,0:T(8,128)(2,1)S(1)}, u32[]{:S(2)}, u32[]{:S(2)}) collective-permute-start(bf16[64,1024]{1,0:T(8,128)(2,1)S(1)} %get-tuple-element.71), channel_id=1, source_target_pairs={{0,16},{16,32},{32,48},{48,0},{64,80},{80,96},{96,112},{112,64},{1... | collective-permute-start | bytes 393224 | tf_op jit(solution)/shard_map/hidden_columns/ppermute | solution.py:282
  141.4 7.8 %collective-permute-start.11 = (bf16[64,1024]{1,0:T(8,128)(2,1)S(1)}, bf16[64,1024]{1,0:T(8,128)(2,1)S(1)}, u32[]{:S(2)}, u32[]{:S(2)}) collective-permute-start(bf16[64,1024]{1,0:T(8,128)(2,1)S(1)} %get-tuple-element.70), channel_id=1, source_target_pairs={{0,32},{16,48},{32,0},{48,16},{64,96},{80,112},{96,64},{112,80},{1... | collective-permute-start | bytes 393224 | tf_op jit(solution)/shard_map/hidden_columns/ppermute | solution.py:282
  143.4 6.0 %collective-permute-start.12 = (bf16[64,1024]{1,0:T(8,128)(2,1)S(1)}, bf16[64,1024]{1,0:T(8,128)(2,1)S(1)}, u32[]{:S(2)}, u32[]{:S(2)}) collective-permute-start(bf16[64,1024]{1,0:T(8,128)(2,1)S(1)} %get-tuple-element.69), channel_id=1, source_target_pairs={{0,48},{16,0},{32,16},{48,32},{64,112},{80,64},{96,80},{112,96},{1... | collective-permute-start | bytes 393224 | tf_op jit(solution)/shard_map/hidden_columns/ppermute | solution.py:282
  150.2 0.8 copy-start.3
Sparse Core Ops, SparseCore 0:
  14.5 70.6 reduce-scatter.1
